TPU v7x, 512 devices: a whole 4x8x8 slice. The times are simulated.
512 devices in a mesh: section: 2 (over x_hi), tp: 8 (over z), cp: 32 (over y, x_lo, core).
Axes of the slice: x: 4 (x_hi: 2, x_lo: 2; x = x_hi * 2 + x_lo), y: 8, z: 8, core: 2. Of those that a mesh axis runs over, the one named last changes fastest.
Arguments:
- query_rows: bfloat16 [2, 4096, 6144], P('section', 'cp', 'tp'), may hold values from -5 to 5
- key_rows: bfloat16 [2, 4096, 1024], P('section', 'cp', 'tp'), may hold values from -5 to 5
- stored_value_rows: bfloat16 [2, 4096, 1024], P('section', 'cp', 'tp'), may hold values from -6 to 6
- output_grad: bfloat16 [2, 4096, 6144], P('section', 'cp', 'tp'), may hold values from -0.75 to 0.75
- span_order: int32 [64], replicated, may hold values from 0 to 63, each once
- episode_ids: int32 [2, 4096], P('section'), may hold values from 0 to 3, never falling along the last dimension, each value on 1 to 2048 neighbouring positions
Outputs:
- query_gradient: bfloat16 [2, 4096, 6144], P('section', 'cp', 'tp')
- key_gradient: bfloat16 [2, 4096, 1024], P('section', 'cp', 'tp')
- value_gradient: bfloat16 [2, 4096, 1024], P('section', 'cp', 'tp')
Inputs may be any that keep to these rules, and one draw needn't show every extreme that they name: `span_order`: each number of 0 to 63 appears once. `episode_ids`: never falls along the positions of a micro-batch; an episode covers at most 2048 positions.
All inputs are finite; a program needn't handle non-finite values.
Results may differ from a plain program's by a relative error of at most 0.018.
Values may be sent and summed in bfloat16 or wider, within the bound.
No kernel may reach another device: no remote copies, remote signals or barrier semaphores. Data moves between devices by JAX's collectives and lax.ppermute only.
A program may use at most 64 MiB of HBM per device.

v0:
```python
import math

import jax
import jax.numpy as jnp
from jax import lax
from jax.sharding import PartitionSpec as P

HEAD_SIZE = 128


NEG_FILL = -1e30
BLOCK_ROWS = 512


def from_behind(block, axis, distance):
    devices = range(lax.axis_size(axis))
    route = [((i - distance) % len(devices), i) for i in devices]
    return lax.ppermute(block, axis, route)


def span_positions(span_order, row_start, row_count, span_len):
    row_ids = row_start + jnp.arange(row_count, dtype=jnp.int32)
    slot_ids = row_ids // span_len
    matches = slot_ids[:, None] == jnp.arange(span_order.shape[0], dtype=jnp.int32)[None, :]
    span_ids = jnp.sum(jnp.where(matches, span_order[None, :], 0), axis=1)
    return span_ids * span_len + row_ids % span_len


def per_device(query_rows, key_rows, stored_value_rows, output_grad, span_order, episode_ids):
    tokens = query_rows.shape[1]
    span_len = tokens // 2
    kv_heads = key_rows.shape[2] // HEAD_SIZE
    heads_per_group = query_rows.shape[2] // key_rows.shape[2]
    scaling = HEAD_SIZE ** (-0.5)
    flat_rows = tokens * heads_per_group
    columns = kv_heads * HEAD_SIZE

    def by_head(array):
        return (
            array[0]
            .reshape(tokens, kv_heads, heads_per_group, HEAD_SIZE)
            .transpose(1, 0, 2, 3)
            .reshape(kv_heads, flat_rows, HEAD_SIZE)
        )

    query_heads = by_head(query_rows)
    grad_heads = by_head(output_grad)
    keys_all, values_all = (
        lax.all_gather(key_rows[0], "cp", axis=0, tiled=True),
        lax.all_gather(stored_value_rows[0], "cp", axis=0, tiled=True),
    )
    total = keys_all.shape[0]
    block = math.gcd(total, BLOCK_ROWS)
    blocks = total // block
    episode = episode_ids[0]
    query_pos = span_positions(span_order, lax.axis_index("cp") * tokens, tokens, span_len)
    row_pos = jnp.repeat(query_pos, heads_per_group)
    row_episode = jnp.repeat(jnp.take(episode, query_pos), heads_per_group)

    def block_data(key_start, count):
        key_pos = span_positions(span_order, key_start, count, span_len)
        key_episode = jnp.take(episode, key_pos)
        allowed = (key_pos[None, :] <= row_pos[:, None]) & (
            key_episode[None, :] == row_episode[:, None]
        )
        key_block = lax.dynamic_slice_in_dim(keys_all, key_start, count, 0).reshape(
            count, kv_heads, HEAD_SIZE
        )
        value_block = lax.dynamic_slice_in_dim(values_all, key_start, count, 0).reshape(
            count, kv_heads, HEAD_SIZE
        )
        return (allowed, key_block, value_block)

    def raw_scores(key_block):
        return (
            jnp.einsum("jrd,cjd->jrc", query_heads, key_block, preferred_element_type=jnp.float32)
            * scaling
        )

    def value_products(value_block):
        return jnp.einsum(
            "jrd,cjd->jrc", grad_heads, value_block, preferred_element_type=jnp.float32
        )

    def stats_step(carried, block_index):
        allowed, key_block, value_block = block_data(block_index * block, block)
        running_max, running_sum, weighted = carried
        scores = jnp.where(allowed, raw_scores(key_block), NEG_FILL)
        new_max = jnp.maximum(running_max, jnp.max(scores, axis=2))
        weights = jnp.where(allowed, jnp.exp(scores - new_max[:, :, None]), 0.0)
        keep = jnp.exp(running_max - new_max)
        products = value_products(value_block)
        return (
            (
                new_max,
                running_sum * keep + jnp.sum(weights, axis=2),
                weighted * keep + jnp.sum(weights * products, axis=2),
            ),
            None,
        )

    start_state = (
        jnp.full((kv_heads, flat_rows), NEG_FILL, jnp.float32),
        jnp.zeros((kv_heads, flat_rows), jnp.float32),
        jnp.zeros((kv_heads, flat_rows), jnp.float32),
    )
    block_ids = jnp.arange(blocks, dtype=jnp.int32)
    (running_max, running_sum, weighted), unused = lax.scan(stats_step, start_state, block_ids)
    log_total = running_max + jnp.log(running_sum)
    deltas = weighted / running_sum

    def gradients(allowed, key_block, value_block):
        probs = jnp.where(allowed, jnp.exp(raw_scores(key_block) - log_total[:, :, None]), 0.0)
        score_grad = (probs * (value_products(value_block) - deltas[:, :, None])).astype(
            jnp.bfloat16
        )
        return (probs.astype(jnp.bfloat16), score_grad)

    def query_part(score_grad, key_block):
        return (
            jnp.einsum("jrc,cjd->jrd", score_grad, key_block, preferred_element_type=jnp.float32)
            * scaling
        )

    def key_value_part(probs_low, score_grad, count):
        key_part = (
            jnp.einsum("jrc,jrd->cjd", score_grad, query_heads, preferred_element_type=jnp.float32)
            * scaling
        )
        value_part = jnp.einsum(
            "jrc,jrd->cjd", probs_low, grad_heads, preferred_element_type=jnp.float32
        )
        return jnp.stack(
            (key_part.reshape(count, columns), value_part.reshape(count, columns)), axis=1
        )

    query_start = jnp.zeros((kv_heads, flat_rows, HEAD_SIZE), jnp.float32)

    def grad_step(query_acc, block_index):
        allowed, key_block, value_block = block_data(block_index * block, block)
        probs_low, score_grad = gradients(allowed, key_block, value_block)
        return (
            query_acc + query_part(score_grad, key_block),
            key_value_part(probs_low, score_grad, block),
        )

    query_acc, partials = lax.scan(grad_step, query_start, block_ids)
    kv_grads = lax.psum_scatter(
        partials.reshape(total, 2, columns), "cp", scatter_dimension=0, tiled=True
    )
    query_gradient = (
        query_acc.astype(jnp.bfloat16)
        .reshape(kv_heads, tokens, heads_per_group, HEAD_SIZE)
        .transpose(1, 0, 2, 3)
        .reshape(1, tokens, kv_heads * heads_per_group * HEAD_SIZE)
    )
    query_back = from_behind(query_gradient, "section", -1)
    key_gradient = kv_grads[:, 0].astype(jnp.bfloat16)[None]
    value_gradient = kv_grads[:, 1].astype(jnp.bfloat16)[None]
    key_back, value_back = from_behind((key_gradient, value_gradient), "section", -1)
    return (query_back, key_back, value_back)


def solution(mesh):
    return jax.shard_map(
        per_device,
        mesh=mesh,
        in_specs=(
            P("section", "cp", "tp"),
            P("section", "cp", "tp"),
            P("section", "cp", "tp"),
            P("section", "cp", "tp"),
            P(),
            P("section", None),
        ),
        out_specs=(P("section", "cp", "tp"), P("section", "cp", "tp"), P("section", "cp", "tp")),
        check_vma=False,
    )
```

profile of v0, /device:TPU:6, one launch (start us, length us, event | category | flops | bytes accessed | tf_op | source)
XLA Modules:
  0.0 459.8 jit_solution(17316281299910073313)
XLA Ops:
  11.8 1.6 gather_fusion.2
  13.4 66.9 %all-gather.5.cloned.1.call-done = bf16[1,4096,128]{2,1,0:T(8,128)(2,1)} async-done(((bf16[1,128,128]{2,1,0:T(8,128)(2,1)}), bf16[1,4096,128]{2,1,0:T(8,128)(2,1)}) %all-gather.5.cloned.1.call-update) | async-done | bytes 1048592 | tf_op jit(solution)/shard_map/all_gather | solution.py:49
  80.3 68.3 %all-gather.7.cloned.1.call-done = bf16[1,4096,128]{2,1,0:T(8,128)(2,1)} async-done(((bf16[1,128,128]{2,1,0:T(8,128)(2,1)}), bf16[1,4096,128]{2,1,0:T(8,128)(2,1)}) %all-gather.7.cloned.1.call-update) | async-done | bytes 1048592 | tf_op jit(solution)/shard_map/all_gather | solution.py:50
  148.6 74.8 %while.32 = (s32[]{:T(128)}, f32[1,768]{1,0:T(1,128)S(1)}, f32[1,768]{1,0:T(1,128)S(1)}, f32[1,768]{1,0:T(1,128)S(1)}, s32[8]{0:T(128)S(1)}, /*index=5*/s32[64]{...) while((s32[]{:T(128)}, f32[1,768]{1,0:T(1,128)S(1)}, ...), condition=%wide.region_6.8_spmd.clone, body=%wide.region_1.0_spmd.clone.sunk | while | flops 208922368 | bytes 5513722 | solution.py:108
  150.7 3.4 gather_fusion
  156.0 1.5 fusion.81
  160.0 3.4 gather_fusion
  165.3 1.5 fusion.81
  169.4 3.4 gather_fusion
  174.7 1.5 fusion.81
  178.7 3.4 gather_fusion
  184.0 1.5 fusion.81
  188.1 3.4 gather_fusion
  193.4 1.5 fusion.81
  197.5 3.4 gather_fusion
  202.8 1.5 fusion.81
  206.8 3.4 gather_fusion
  212.1 1.5 fusion.81
  216.2 3.4 gather_fusion
  221.5 1.5 fusion.81
  223.5 94.2 %while.33 = (s32[]{:T(128)}, f32[1,768,128]{2,1,0:T(8,128)S(1)}, f32[8,512,2,128]{3,1,0,2:T(8,128)}, s32[8]{0:T(128)S(1)}, s32[64]{0:T(128)}, /*index=5*/s32[409...) while((s32[]{:T(128)}, f32[1,768,128]{2,1,0:T(8,128)S(1)}, ...), condition=%wide.region_9.11_spmd.clone, body=%wide.region_7.10_spmd.clone.sunk | while | flops 507859456 | bytes 10696217 | solution.py:147
  225.6 3.4 gather_fusion.1
  229.5 1.5 bitcast_select_fusion.3
  233.0 1.4 fusion.95
  237.3 3.4 gather_fusion.1
  241.2 1.5 bitcast_select_fusion.3
  244.8 1.4 fusion.95
  249.1 3.4 gather_fusion.1
  253.0 1.5 bitcast_select_fusion.3
  260.9 3.4 gather_fusion.1
  264.8 1.5 bitcast_select_fusion.3
  268.3 1.4 fusion.95
  272.6 3.4 gather_fusion.1
  276.5 1.5 bitcast_select_fusion.3
  280.1 1.4 fusion.95
  284.4 3.4 gather_fusion.1
  288.3 1.5 bitcast_select_fusion.3
  296.2 3.4 gather_fusion.1
  300.1 1.5 bitcast_select_fusion.3
  303.6 1.4 fusion.95
  307.9 3.4 gather_fusion.1
  311.8 1.5 bitcast_select_fusion.3
  315.4 1.4 fusion.95
  317.9 3.3 collective-permute-start
  321.3 118.3 %reduce-scatter.2.cloned.1.call-done = f32[128,2,128]{2,0,1:T(8,128)} async-done(((f32[4096,2,128]{2,0,1:T(8,128)}), f32[128,2,128]{2,0,1:T(8,128)}) %reduce-scatter.2.cloned.1.call-update) | async-done | bytes 131088 | tf_op jit(solution)/shard_map/reduce_scatter | solution.py:148
  440.5 3.6 collective-permute-start.2
  444.1 3.7 collective-permute-start.1
  447.9 3.6 collective-permute-done.1
  (280 shorter events, 77.9 us)
Async XLA Ops:
  7.2 73.2 %all-gather.5.cloned.1.call-start = ((), (), s32[]{:S(2)}) async-start(), calls=%async_computation.2 | async-start | bytes 1081344 | tf_op jit(solution)/shard_map/all_gather | solution.py:49
  7.9 140.7 %all-gather.7.cloned.1.call-start = ((), (), s32[]{:S(2)}) async-start(), calls=%async_computation.3 | async-start | bytes 1081344 | tf_op jit(solution)/shard_map/all_gather | solution.py:50
  8.6 430.9 %reduce-scatter.2.cloned.1.call-start = ((), (), s32[]{:S(2)}) async-start(), calls=%async_computation.1 | async-start | bytes 4325376 | tf_op jit(solution)/shard_map/reduce_scatter | solution.py:148
  317.9 129.9 %collective-permute-start = (bf16[1,128,768]{2,1,0:T(8,128)(2,1)S(1)}, bf16[1,128,768]{2,1,0:T(8,128)(2,1)S(1)}, u32[]{:S(2)}, u32[]{:S(2)}) collective-permute-start(bf16[1,128,768]{2,1,0:T(8,128)(2,1)S(1)} %reshape_transpose_reshape.3), channel_id=1, source_target_pairs={{256,0},{0,256},{257,1},{1,257},{258,2},{2,258},{259,3},{3,259},{2... | collective-permute-start | bytes 589832 | tf_op jit(solution)/shard_map/ppermute | solution.py:18
  440.5 7.4 %collective-permute-start.2 = (bf16[1,128,128]{2,1,0:T(8,128)(2,1)S(1)}, bf16[1,128,128]{2,1,0:T(8,128)(2,1)S(1)}, u32[]{:S(2)}, u32[]{:S(2)}) collective-permute-start(bf16[1,128,128]{2,1,0:T(8,128)(2,1)S(1)} %get-tuple-element.517), channel_id=1, source_target_pairs={{256,0},{0,256},{257,1},{1,257},{258,2},{2,258},{259,3},{3,259},{2... | collective-permute-start | bytes 98312 | tf_op jit(solution)/shard_map/ppermute | solution.py:18
  444.1 7.3 %collective-permute-start.1 = (bf16[1,128,128]{2,1,0:T(8,128)(2,1)S(1)}, bf16[1,128,128]{2,1,0:T(8,128)(2,1)S(1)}, u32[]{:S(2)}, u32[]{:S(2)}) collective-permute-start(bf16[1,128,128]{2,1,0:T(8,128)(2,1)S(1)} %get-tuple-element.518), channel_id=1, source_target_pairs={{256,0},{0,256},{257,1},{1,257},{258,2},{2,258},{259,3},{3,259},{2... | collective-permute-start | bytes 98312 | tf_op jit(solution)/shard_map/ppermute | solution.py:18
Sparse Core Ops, SparseCore 0:
  10.1 70.1 all-gather.4
  82.5 66.1 all-gather.6
  317.8 121.6 reduce-scatter.1
where the time goes:
time: 466 us; the launch traced here: 460 us
  waiting for transfers between devices  258 us (55%)
  local copies, waits for them, and re-layouts  76.8 us (16%)
  matrix products  62.8 us (13%)
  other arithmetic  25.4 us (5%)
  between operations  13.9 us (3%)
  loops' own time  11.8 us (3%)
  starting transfers between devices  10.8 us (2%)
    reduce_scatter x1, waiting for transfers between devices, per_device(): lax.psum_scatter(partials.reshape(total, 2, columns), 'cp', scatter_dimen...  118 us
    all_gather x1, waiting for transfers between devices, per_device(): lax.all_gather(stored_value_rows[0], 'cp', axis=0, tiled=True)  68.3 us
    all_gather x1, waiting for transfers between devices, per_device(): lax.all_gather(key_rows[0], 'cp', axis=0, tiled=True)  66.9 us
    gather x16, local copies, waits for them, and re-layouts, block_data(): key_episode = jnp.take(episode, key_pos)  54.5 us
    dot_general x16, matrix products, raw_scores(): jnp.einsum('jrd,cjd->jrc', query_heads, key_block, preferred_element_type...  23.3 us
    dot_general x16, matrix products, value_products(): jnp.einsum('jrd,cjd->jrc', grad_heads, value_block, preferred_element_typ...  22.2 us
    reduce_sum x17, other arithmetic, span_positions(): span_ids = jnp.sum(jnp.where(matches, span_order[None, :], 0), axis=1)  12.8 us
    dot_general x8, matrix products, query_part(): jnp.einsum('jrc,cjd->jrd', score_grad, key_block, preferred_element_type=...  11.4 us
  transfers between devices with their start and end apart: 6, of which 4 were waited for; matrix products, arithmetic and copies ran while one was open for 1% of the time, Pallas kernels for 0%

commit v1 on v0

v1 whole, which is shorter than its diff:
```python
import functools

import jax
import jax.numpy as jnp
from jax import lax
from jax.experimental import pallas as pl
from jax.experimental.pallas import tpu as pltpu
from jax.sharding import Mesh
from jax.sharding import PartitionSpec as P

HEAD = 128
SPAN = 64
HEADS = 6
ROWS = HEADS * SPAN
GROUP = 4
SCALING = HEAD ** (-0.5)
LOG2E = 1.4426950408889634
NEG_FILL = -1e30
FAR = 1 << 20
NT = (((1,), (1,)), ((), ()))
NN = (((1,), (0,)), ((), ()))


def dot(a, b, dims):
    return lax.dot_general(a, b, dims, preferred_element_type=jnp.float32)


def episode_starts(episode_ref):
    ids = episode_ref[...]
    return [jnp.sum((ids < v).astype(jnp.int32)) for v in (1, 2, 3)]


def start_of(starts, pos):
    first = jnp.zeros_like(pos)
    for s in starts:
        first = jnp.maximum(first, jnp.where(s <= pos, s, 0))
    return first


def list_visible(order_ref, place_ref, starts, query_base, list_ref):
    xl, core, key_count = place_ref[1], place_ref[2], 16
    first = jnp.int32(0)
    for s in starts:
        first = jnp.maximum(first, jnp.where(s <= query_base, s, 0))
    count = jnp.int32(0)
    for k in range(key_count):
        base = order_ref[((k // 2) * 4 + xl * 2 + core) * 2 + k % 2] * SPAN
        list_ref[0, count] = k
        list_ref[1, count] = base
        seen = (base <= query_base) & (base + (SPAN - 1) >= first)
        count = count + seen.astype(jnp.int32)
    for extra in range(GROUP):
        list_ref[0, count + extra] = 0
        list_ref[1, count + extra] = FAR
    return count


def load_group(kv_ref, list_ref, step):
    spans = [list_ref[0, step * GROUP + i] for i in range(GROUP)]
    keys = jnp.concatenate([kv_ref[s, :, :HEAD] for s in spans], axis=0)
    values = jnp.concatenate([kv_ref[s, :, HEAD:] for s in spans], axis=0)
    iota = lax.broadcasted_iota(jnp.int32, (SPAN, HEAD), 0)
    pos = jnp.concatenate([list_ref[1, step * GROUP + i] + iota for i in range(GROUP)], axis=0)
    return spans, keys, values, pos


def by_rows(ref, row, column):
    return jnp.concatenate(
        [
            ref[pl.ds(row, SPAN), column + h * HEAD : column + (h + 1) * HEAD]
            for h in range(HEADS)
        ],
        axis=0,
    )


def masked_scores(scores, visible):
    return jnp.concatenate(
        [
            jnp.where(visible, scores[:, g * HEAD : (g + 1) * HEAD] * (SCALING * LOG2E), NEG_FILL)
            for g in range(ROWS // HEAD)
        ],
        axis=1,
    )


def query_spans(order_ref, place_ref, body):
    y, xl = place_ref[0], place_ref[1]
    for rel in range(2):
        chip = xl if rel == 0 else 1 - xl

        def one(i, unused, rel=rel, chip=chip):
            base = order_ref[y * 8 + chip * 4 + i] * SPAN
            body(rel, i, chip * 4 + i, base)
            return unused

        lax.fori_loop(0, 4, one, 0)


def stats_kernel(order_ref, place_ref, episode_ref, kv_ref, own_ref, other_ref, out_ref, list_ref):
    starts = episode_starts(episode_ref)
    lane = lax.broadcasted_iota(jnp.int32, (1, HEAD), 1) % SPAN

    def body(rel, i, slot, base):
        ref = (own_ref, other_ref)[rel]
        row = pl.multiple_of(i * SPAN, SPAN)
        query = by_rows(ref, row, 0)
        grad = by_rows(ref, row, HEADS * HEAD)
        query_pos = base + lane
        first = start_of(starts, query_pos)
        count = list_visible(order_ref, place_ref, starts, base, list_ref)

        def step(j, carried):
            top, total, weighted = carried
            unused, keys, values, pos = load_group(kv_ref, list_ref, j)
            visible = (pos <= query_pos) & (pos >= first)
            scores = masked_scores(dot(keys, query, NT), visible)
            products = dot(values, grad, NT)
            new_top = jnp.maximum(top, jnp.max(scores, axis=0, keepdims=True))
            weights = jnp.exp2(scores - new_top)
            keep = jnp.exp2(top - new_top)
            total = total * keep + jnp.sum(weights, axis=0, keepdims=True)
            weighted = weighted * keep + jnp.sum(weights * products, axis=0, keepdims=True)
            return new_top, total, weighted

        zero = jnp.zeros((1, ROWS), jnp.float32)
        top, total, weighted = lax.fori_loop(
            0, (count + (GROUP - 1)) // GROUP, step, (zero + NEG_FILL, zero, zero)
        )
        out_ref[pl.ds(slot, 1), :] = top
        out_ref[pl.ds(8 + slot, 1), :] = total
        out_ref[pl.ds(16 + slot, 1), :] = weighted

    query_spans(order_ref, place_ref, body)


def grads_kernel(
    order_ref,
    place_ref,
    episode_ref,
    kv_ref,
    own_ref,
    other_ref,
    stats_ref,
    keep_ref,
    send_ref,
    dkv_ref,
    list_ref,
    log_ref,
    delta_ref,
    acc_ref,
    dq_ref,
):
    starts = episode_starts(episode_ref)
    lane = lax.broadcasted_iota(jnp.int32, (1, HEAD), 1) % SPAN
    parts = stats_ref.shape[0]
    tops = [stats_ref[p, 0:8] for p in range(parts)]
    top = functools.reduce(jnp.maximum, tops)
    shares = [jnp.exp2(t - top) for t in tops]
    total = sum(stats_ref[p, 8:16] * shares[p] for p in range(parts))
    log_ref[...] = top + jnp.log2(total)
    delta_ref[...] = sum(stats_ref[p, 16:24] * shares[p] for p in range(parts)) / total
    acc_ref[...] = jnp.zeros_like(acc_ref)
    my_core = place_ref[2]

    def body(rel, i, slot, base):
        ref = (own_ref, other_ref)[rel]
        row = pl.multiple_of(i * SPAN, SPAN)
        query = by_rows(ref, row, 0)
        grad = by_rows(ref, row, HEADS * HEAD)
        query_pos = base + lane
        first = start_of(starts, query_pos)
        count = list_visible(order_ref, place_ref, starts, base, list_ref)
        log_total = log_ref[pl.ds(slot, 1), :]
        delta = delta_ref[pl.ds(slot, 1), :]
        dq_ref[...] = jnp.zeros_like(dq_ref)

        def step(j, unused):
            spans, keys, values, pos = load_group(kv_ref, list_ref, j)
            visible = (pos <= query_pos) & (pos >= first)
            scores = masked_scores(dot(keys, query, NT), visible)
            products = dot(values, grad, NT)
            probs = jnp.exp2(scores - log_total)
            score_grad = (probs * (products - delta)).astype(jnp.bfloat16)
            dq_ref[...] += dot(keys.T, score_grad, NN)
            dk = dot(score_grad, query, NN)
            dv = dot(probs.astype(jnp.bfloat16), grad, NN)
            for n in range(GROUP):
                acc_ref[spans[n], :, :HEAD] += dk[n * SPAN : (n + 1) * SPAN]
                acc_ref[spans[n], :, HEAD:] += dv[n * SPAN : (n + 1) * SPAN]
            return unused

        lax.fori_loop(0, (count + (GROUP - 1)) // GROUP, step, 0)
        out = dq_ref[...].T * SCALING
        half = pl.multiple_of((i % 2) * SPAN, SPAN)
        mine = i // 2 == my_core

        @pl.when(mine)
        def _():
            for h in range(HEADS):
                keep_ref[rel, pl.ds(half, SPAN), h * HEAD : (h + 1) * HEAD] = out[
                    h * SPAN : (h + 1) * SPAN
                ]

        @pl.when(jnp.logical_not(mine))
        def _():
            for h in range(HEADS):
                send_ref[rel, pl.ds(half, SPAN), h * HEAD : (h + 1) * HEAD] = out[
                    h * SPAN : (h + 1) * SPAN
                ].astype(jnp.bfloat16)

    query_spans(order_ref, place_ref, body)
    dkv_ref[:, :, :HEAD] = (acc_ref[:, :, :HEAD] * SCALING).astype(jnp.bfloat16)
    dkv_ref[:, :, HEAD:] = acc_ref[:, :, HEAD:].astype(jnp.bfloat16)


def swap(block, axis):
    return lax.ppermute(block, axis, [(0, 1), (1, 0)])


def per_device(query_rows, key_rows, stored_value_rows, output_grad, span_order, episode_ids):
    tokens = query_rows.shape[1]
    columns = HEADS * HEAD
    ring = lax.axis_size("y")
    place = jnp.stack([lax.axis_index("y"), lax.axis_index("xl"), lax.axis_index("core")]).astype(
        jnp.int32
    )
    both = jnp.concatenate([query_rows[0], output_grad[0]], axis=1)
    own = lax.all_gather(both, "core", axis=0, tiled=True)
    other = swap(own, "xl")
    kv = jnp.concatenate([key_rows[0], stored_value_rows[0]], axis=1)
    kv_all = lax.all_to_all(
        jnp.broadcast_to(kv[None], (ring, tokens, 2 * HEAD)), "y", 0, 0, tiled=True
    ).reshape(ring * 2, SPAN, 2 * HEAD)

    smem = pl.BlockSpec(memory_space=pltpu.SMEM)
    vmem = pl.BlockSpec(memory_space=pltpu.VMEM)
    params = pltpu.CompilerParams(vmem_limit_bytes=40 * 1024 * 1024)
    stats = pl.pallas_call(
        stats_kernel,
        out_shape=jax.ShapeDtypeStruct((24, ROWS), jnp.float32),
        in_specs=[smem, smem, vmem, vmem, vmem, vmem],
        out_specs=vmem,
        scratch_shapes=[pltpu.SMEM((2, 16 + GROUP), jnp.int32)],
        compiler_params=params,
        name="row_stats",
    )(span_order, place, episode_ids, kv_all, own, other)
    stats_all = lax.all_gather(stats, ("xl", "core"), axis=0)
    keep, send, dkv = pl.pallas_call(
        grads_kernel,
        out_shape=(
            jax.ShapeDtypeStruct((2, tokens, columns), jnp.float32),
            jax.ShapeDtypeStruct((2, tokens, columns), jnp.bfloat16),
            jax.ShapeDtypeStruct((ring * 2, SPAN, 2 * HEAD), jnp.bfloat16),
        ),
        in_specs=[smem, smem, vmem, vmem, vmem, vmem, vmem],
        out_specs=(vmem, vmem, vmem),
        scratch_shapes=[
            pltpu.SMEM((2, 16 + GROUP), jnp.int32),
            pltpu.VMEM((8, ROWS), jnp.float32),
            pltpu.VMEM((8, ROWS), jnp.float32),
            pltpu.VMEM((ring * 2, SPAN, 2 * HEAD), jnp.float32),
            pltpu.VMEM((HEAD, ROWS), jnp.float32),
        ],
        compiler_params=params,
        name="gradients",
    )(span_order, place, episode_ids, kv_all, own, other, stats_all)

    dq = keep + swap(send, "core").astype(jnp.float32)
    dq_other = swap(dq[1].astype(jnp.bfloat16), "xl")
    dkv_parts = lax.all_to_all(dkv.reshape(ring, tokens, 2 * HEAD), "y", 0, 0, tiled=True)
    dkv_sum = jnp.sum(dkv_parts.astype(jnp.float32), axis=0)
    dq_sum = dq[0] + dq_other.astype(jnp.float32)
    done = jnp.concatenate([dq_sum, dkv_sum], axis=1).astype(jnp.bfloat16)
    back = swap(done, "section")[None]
    return (
        back[:, :, :columns],
        back[:, :, columns : columns + HEAD],
        back[:, :, columns + HEAD :],
    )


def solution(mesh):
    devices = mesh.devices
    fine = Mesh(
        devices.reshape(devices.shape[0], devices.shape[1], devices.shape[2] // 4, 2, 2),
        ("section", "tp", "y", "xl", "core"),
    )
    rows = P("section", ("y", "xl", "core"), "tp")
    return jax.shard_map(
        per_device,
        mesh=fine,
        in_specs=(rows, rows, rows, rows, P(), P("section", None)),
        out_specs=(rows, rows, rows),
        check_vma=False,
    )
```

time: 466 us -> 95.3 us (0.20); the launches traced: 460 us -> 94.2 us
  waiting for transfers between devices: 258 us -> 42.6 us
  local copies, waits for them, and re-layouts: 76.8 us -> 2.19 us
  matrix products: 62.8 us -> 0 us
  other arithmetic: 25.4 us -> 1.09 us
  starting transfers between devices: 10.8 us -> 25.8 us
  Pallas kernels: 0 us -> 14 us
  between operations: 13.9 us -> 0.74 us
  loops' own time: 11.8 us -> 0 us
  blocking collectives: 0 us -> 7.84 us
    all_gather x2 -> x0, waiting for transfers between devices: 135 us -> none  [the longest x1 68.3 us: per_device(): lax.all_gather(stored_value_rows[0], 'cp', axis=0, tiled=True)]
    reduce_scatter x1 -> x0, waiting for transfers between devices: 118 us -> none  [per_device(): lax.psum_scatter(partials.reshape(total, 2, columns), 'cp', scatter_dimen...]
    dot_general x56 -> x0, matrix products: 62.8 us -> none  [the longest x16 23.3 us: raw_scores(): jnp.einsum('jrd,cjd->jrc', query_heads, key_block, preferred_element_type...]
    gather x17 -> x0, local copies, waits for them, and re-layouts: 56.1 us -> none  [the longest x16 54.5 us: block_data(): key_episode = jnp.take(episode, key_pos)]
    ppermute x3 -> x4, waiting for transfers between devices: 3.56 us -> 33.5 us  [swap(): return lax.ppermute(block, axis, [(0, 1), (1, 0)])]
    reduce_sum x25 -> x1, other arithmetic: 16.3 us -> 0.07 us  [per_device(): dkv_sum = jnp.sum(dkv_parts.astype(jnp.float32), axis=0)]
    all_to_all x0 -> x2, starting transfers between devices: none -> 15.2 us  [the longest x1 8.02 us: per_device(): lax.all_to_all(dkv.reshape(ring, tokens, 2 * HEAD), 'y', 0, 0, tiled=True)]
    pallas_call x0 -> x2, Pallas kernels: none -> 14 us  [the longest x1 9.2 us: per_device(): pl.pallas_call(grads_kernel, out_shape=(jax.ShapeDtypeStruct((2, tokens,...]
  transfers between devices with their start and end apart: 6 -> 6, of which waited for: 4 -> 4; matrix products, arithmetic and copies ran while one was open for 1% -> 0% of each run, Pallas kernels for 0% -> 0%
where the time goes in v1:
time: 95.3 us; the launch traced here: 94.2 us
  waiting for transfers between devices  42.6 us (45%)
  starting transfers between devices  25.8 us (27%)
  Pallas kernels  14 us (15%)
  blocking collectives  7.84 us (8%)
  local copies, waits for them, and re-layouts  2.19 us (2%)
  other arithmetic  1.09 us (1%)
    ppermute x4, waiting for transfers between devices, swap(): return lax.ppermute(block, axis, [(0, 1), (1, 0)])  33.5 us
    ppermute x4, starting transfers between devices, swap(): return lax.ppermute(block, axis, [(0, 1), (1, 0)])  10.5 us
    pallas_call x1, Pallas kernels, per_device(): pl.pallas_call(grads_kernel, out_shape=(jax.ShapeDtypeStruct((2, tokens,...  9.2 us
    all_to_all x1, waiting for transfers between devices, per_device(): lax.all_to_all(dkv.reshape(ring, tokens, 2 * HEAD), 'y', 0, 0, tiled=True)  9.12 us
    all_to_all x1, starting transfers between devices, per_device(): lax.all_to_all(dkv.reshape(ring, tokens, 2 * HEAD), 'y', 0, 0, tiled=True)  8.02 us
    all_to_all x1, starting transfers between devices, per_device(): lax.all_to_all(jnp.broadcast_to(kv[None], (ring, tokens, 2 * HEAD)), 'y',...  7.23 us
    all_gather x1, blocking collectives, per_device(): stats_all = lax.all_gather(stats, ('xl', 'core'), axis=0)  5.47 us
    pallas_call x1, Pallas kernels, per_device(): pl.pallas_call(stats_kernel, out_shape=jax.ShapeDtypeStruct((24, ROWS), j...  4.83 us
  transfers between devices with their start and end apart: 6, of which 4 were waited for; matrix products, arithmetic and copies ran while one was open for 0% of the time, Pallas kernels for 0%

profile of v1, /device:TPU:6, one launch (start us, length us, event | category | flops | bytes accessed | tf_op | source)
XLA Modules:
  0.0 94.2 jit_solution(7950405301912672429)
XLA Ops:
  0.6 0.8 pad_maximum_fusion.2
  1.4 0.8 broadcast_in_dim.4
  2.2 0.0 copy-start.2
  2.2 0.0 copy-start.3
  2.2 7.2 %all-to-all-start = ((bf16[8,128,256]{2,1,0:T(8,128)(2,1)}), bf16[8,128,256]{2,1,0:T(8,128)(2,1)S(1)}, u32[]{:S(2)}, u32[]{:S(2)}) async-start(bf16[8,128,256]{2,1,0:T(8,128)(2,1)} %broadcast_in_dim.4), calls=%async_computation | async-start | bytes 1048576 | tf_op jit(solution)/shard_map/all_to_all | solution.py:232
  9.5 0.0 copy-done.2
  9.5 0.0 copy-done.3
  9.5 2.4 %all_gather.9.own_ref = bf16[256,1536]{1,0:T(8,128)(2,1)S(1)} all-gather(bf16[128,1536]{1,0:T(8,128)(2,1)S(1)} %pad_maximum_fusion), channel_id=1, replica_groups=mesh['section'=2,'tp'=8,'y'=8,'xl'=2,'core'=2] {'core'}, dimensions={0}, use_global_device_ids=true | all-gather | bytes 1179648 | tf_op jit(solution)/shard_map/all_gather | solution.py:229
  11.9 0.0 copy-start
  11.9 2.9 %collective-permute-start = (bf16[256,1536]{1,0:T(8,128)(2,1)S(1)}, bf16[256,1536]{1,0:T(8,128)(2,1)S(1)}, u32[]{:S(2)}, u32[]{:S(2)}) collective-permute-start(bf16[256,1536]{1,0:T(8,128)(2,1)S(1)} %all_gather.9.own_ref), channel_id=1, source_target_pairs={{0,2},{2,0},{1,3},{3,1},{4,6},{6,4},{5,7},{7,5},{8,10},{10,8},{9,1... | collective-permute-start | bytes 2359304 | tf_op jit(solution)/shard_map/ppermute | solution.py:218
  14.8 0.1 pad_add_fusion.place_ref
  14.8 0.0 copy-start.1
  14.8 18.6 %collective-permute-done.other_ref = bf16[256,1536]{1,0:T(8,128)(2,1)S(1)} collective-permute-done((bf16[256,1536]{1,0:T(8,128)(2,1)S(1)}, bf16[256,1536]{1,0:T(8,128)(2,1)S(1)}, u32[]{:S(2)}, u32[]{:S(2)}) %collective-permute-start) | collective-permute-done | bytes 786464 | tf_op jit(solution)/shard_map/ppermute | solution.py:218
  33.5 0.0 all-to-all-done
  33.5 0.0 copy-done
  33.5 0.0 copy-done.1
  33.5 4.8 %row_stats.1 = f32[24,384]{1,0:T(8,128)S(1)} custom-call(s32[64]{0:T(128)S(1)} %copy-done.1, s32[3]{0:T(128)S(1)} %pad_add_fusion.place_ref, s32[1,4096]{1,0:T(1,128)S(1)} %copy-done, bf16[16,64,256]{2,1,0:T(8,128)(2,1)S(1)} %bitcast.19, bf16[256,1536]{1,0:T(8,128)(2,1)S(1)} %all_gather.9.own_ref, bf16[256,1536]{1,0:T(8,128)(2,1)S(1)} %collective-permute-done.other_ref), custom_call_target="tpu_custom_call" | custom-call | tf_op jit(solution)/shard_map/row_stats/pallas_call | solution.py:239
  38.3 5.5 %all-gather = f32[96,384]{1,0:T(8,128)S(1)} all-gather(f32[24,384]{1,0:T(8,128)S(1)} %row_stats.1), channel_id=2, replica_groups=mesh['section'=2,'tp'=8,'y'=8,'xl'=2,'core'=2] {'xl','core'}, dimensions={0}, use_global_device_ids=true | all-gather | bytes 184320 | tf_op jit(solution)/shard_map/all_gather | solution.py:248
  43.8 9.2 %gradients.1 = (f32[2,128,768]{2,1,0:T(8,128)S(1)}, bf16[2,128,768]{2,1,0:T(8,128)(2,1)S(1)}, bf16[16,64,256]{2,1,0:T(8,128)(2,1)}) custom-call(s32[64]{0:T(128)S(1)} %copy-done.1, s32[3]{0:T(128)S(1)} %pad_add_fusion.place_ref, s32[1,4096]{1,0:T(1,128)S(1)} %copy-done, bf16[16,64,256]{2,1,0:T(8,128)(2,1)S(1)} %bitcast.20, ...), custom_call_target="tpu_custom_call" | custom-call | tf_op jit(solution)/shard_map/gradients/pallas_call | solution.py:249
  53.0 1.9 %collective-permute-start.1 = (bf16[2,128,768]{2,1,0:T(8,128)(2,1)S(1)}, bf16[2,128,768]{2,1,0:T(8,128)(2,1)S(1)}, u32[]{:S(2)}, u32[]{:S(2)}) collective-permute-start(bf16[2,128,768]{2,1,0:T(8,128)(2,1)S(1)} %get-tuple-element.7), channel_id=1, source_target_pairs={{0,1},{1,0},{2,3},{3,2},{4,5},{5,4},{6,7},{7,6},{8,9},{9,8},{10,11... | collective-permute-start | bytes 1179656 | tf_op jit(solution)/shard_map/ppermute | solution.py:218
  54.9 8.0 %all-to-all-start.1 = ((bf16[8,128,256]{2,1,0:T(8,128)(2,1)}), bf16[8,128,256]{2,1,0:T(8,128)(2,1)S(1)}, u32[]{:S(2)}, u32[]{:S(2)}) async-start(bf16[8,128,256]{2,1,0:T(8,128)(2,1)} %bitcast.11), calls=%async_computation.1 | async-start | bytes 1048576 | tf_op jit(solution)/shard_map/all_to_all | solution.py:271
  62.9 0.0 collective-permute-done.1
  63.0 0.1 convert_add_fusion
  63.1 1.9 %collective-permute-start.2 = (bf16[128,768]{1,0:T(8,128)(2,1)S(1)}, bf16[128,768]{1,0:T(8,128)(2,1)S(1)}, u32[]{:S(2)}, u32[]{:S(2)}) collective-permute-start(bf16[128,768]{1,0:T(8,128)(2,1)S(1)} %fusion.2), channel_id=1, source_target_pairs={{0,2},{2,0},{1,3},{3,1},{4,6},{6,4},{5,7},{7,5},{8,10},{10,8},{9,1... | collective-permute-start | bytes 589832 | tf_op jit(solution)/shard_map/ppermute | solution.py:218
  65.0 7.0 %collective-permute-done.2 = bf16[128,768]{1,0:T(8,128)(2,1)S(1)} collective-permute-done((bf16[128,768]{1,0:T(8,128)(2,1)S(1)}, bf16[128,768]{1,0:T(8,128)(2,1)S(1)}, u32[]{:S(2)}, u32[]{:S(2)}) %collective-permute-start.2) | collective-permute-done | bytes 196640 | tf_op jit(solution)/shard_map/ppermute | solution.py:218
  72.0 9.1 %all-to-all-done.1 = bf16[8,128,256]{2,1,0:T(8,128)(2,1)S(1)} async-done(((bf16[8,128,256]{2,1,0:T(8,128)(2,1)}), bf16[8,128,256]{2,1,0:T(8,128)(2,1)S(1)}, u32[]{:S(2)}, u32[]{:S(2)}) %all-to-all-start.1) | async-done | bytes 524320 | tf_op jit(solution)/shard_map/all_to_all | solution.py:271
  81.2 0.1 reduce
  81.3 3.8 %collective-permute-start.3 = (bf16[128,1024]{1,0:T(8,128)(2,1)S(1)}, bf16[128,1024]{1,0:T(8,128)(2,1)S(1)}, u32[]{:S(2)}, u32[]{:S(2)}) collective-permute-start(bf16[128,1024]{1,0:T(8,128)(2,1)S(1)} %pad_maximum_fusion.1), channel_id=1, source_target_pairs={{0,256},{256,0},{1,257},{257,1},{2,258},{258,2},{3,259},{259,3},{4... | collective-permute-start | bytes 786440 | tf_op jit(solution)/shard_map/ppermute | solution.py:218
  85.1 7.8 %collective-permute-done.3 = bf16[128,1024]{1,0:T(8,128)(2,1)S(1)} collective-permute-done((bf16[128,1024]{1,0:T(8,128)(2,1)S(1)}, bf16[128,1024]{1,0:T(8,128)(2,1)S(1)}, u32[]{:S(2)}, u32[]{:S(2)}) %collective-permute-start.3) | collective-permute-done | bytes 262176 | tf_op jit(solution)/shard_map/ppermute | solution.py:218
  92.9 0.6 fusion.3
  93.5 0.7 slice.23
  (4 shorter events, 0.1 us)
Async XLA Ops:
  2.2 7.2 %copy-start.2 = (bf16[1,128,768]{2,1,0:T(8,128)(2,1)S(1)}, bf16[1,128,768]{2,1,0:T(8,128)(2,1)}, u32[]{:S(2)}) copy-start(bf16[1,128,768]{2,1,0:T(8,128)(2,1)} %param.9) | copy-start | bytes 589828
  2.2 7.2 %copy-start.3 = (bf16[1,128,768]{2,1,0:T(8,128)(2,1)S(1)}, bf16[1,128,768]{2,1,0:T(8,128)(2,1)}, u32[]{:S(2)}) copy-start(bf16[1,128,768]{2,1,0:T(8,128)(2,1)} %param.6) | copy-start | bytes 589828
  2.2 31.3 %all-to-all-start = ((bf16[8,128,256]{2,1,0:T(8,128)(2,1)}), bf16[8,128,256]{2,1,0:T(8,128)(2,1)S(1)}, u32[]{:S(2)}, u32[]{:S(2)}) async-start(bf16[8,128,256]{2,1,0:T(8,128)(2,1)} %broadcast_in_dim.4), calls=%async_computation | async-start | bytes 1048576 | tf_op jit(solution)/shard_map/all_to_all | solution.py:232
  11.9 21.6 %copy-start = (s32[1,4096]{1,0:T(1,128)S(1)}, s32[1,4096]{1,0:T(1,128)}, u32[]{:S(2)}) copy-start(s32[1,4096]{1,0:T(1,128)} %episode_ref.3) | copy-start | bytes 49156
  11.9 21.6 %collective-permute-start = (bf16[256,1536]{1,0:T(8,128)(2,1)S(1)}, bf16[256,1536]{1,0:T(8,128)(2,1)S(1)}, u32[]{:S(2)}, u32[]{:S(2)}) collective-permute-start(bf16[256,1536]{1,0:T(8,128)(2,1)S(1)} %all_gather.9.own_ref), channel_id=1, source_target_pairs={{0,2},{2,0},{1,3},{3,1},{4,6},{6,4},{5,7},{7,5},{8,10},{10,8},{9,1... | collective-permute-start | bytes 2359304 | tf_op jit(solution)/shard_map/ppermute | solution.py:218
  14.8 18.7 %copy-start.1 = (s32[64]{0:T(128)S(1)}, s32[64]{0:T(128)}, u32[]{:S(2)}) copy-start(s32[64]{0:T(128)} %order_ref.3) | copy-start | bytes 772
  53.0 9.9 %collective-permute-start.1 = (bf16[2,128,768]{2,1,0:T(8,128)(2,1)S(1)}, bf16[2,128,768]{2,1,0:T(8,128)(2,1)S(1)}, u32[]{:S(2)}, u32[]{:S(2)}) collective-permute-start(bf16[2,128,768]{2,1,0:T(8,128)(2,1)S(1)} %get-tuple-element.7), channel_id=1, source_target_pairs={{0,1},{1,0},{2,3},{3,2},{4,5},{5,4},{6,7},{7,6},{8,9},{9,8},{10,11... | collective-permute-start | bytes 1179656 | tf_op jit(solution)/shard_map/ppermute | solution.py:218
  54.9 26.2 %all-to-all-start.1 = ((bf16[8,128,256]{2,1,0:T(8,128)(2,1)}), bf16[8,128,256]{2,1,0:T(8,128)(2,1)S(1)}, u32[]{:S(2)}, u32[]{:S(2)}) async-start(bf16[8,128,256]{2,1,0:T(8,128)(2,1)} %bitcast.11), calls=%async_computation.1 | async-start | bytes 1048576 | tf_op jit(solution)/shard_map/all_to_all | solution.py:271
  63.1 8.9 %collective-permute-start.2 = (bf16[128,768]{1,0:T(8,128)(2,1)S(1)}, bf16[128,768]{1,0:T(8,128)(2,1)S(1)}, u32[]{:S(2)}, u32[]{:S(2)}) collective-permute-start(bf16[128,768]{1,0:T(8,128)(2,1)S(1)} %fusion.2), channel_id=1, source_target_pairs={{0,2},{2,0},{1,3},{3,1},{4,6},{6,4},{5,7},{7,5},{8,10},{10,8},{9,1... | collective-permute-start | bytes 589832 | tf_op jit(solution)/shard_map/ppermute | solution.py:218
  81.3 11.7 %collective-permute-start.3 = (bf16[128,1024]{1,0:T(8,128)(2,1)S(1)}, bf16[128,1024]{1,0:T(8,128)(2,1)S(1)}, u32[]{:S(2)}, u32[]{:S(2)}) collective-permute-start(bf16[128,1024]{1,0:T(8,128)(2,1)S(1)} %pad_maximum_fusion.1), channel_id=1, source_target_pairs={{0,256},{256,0},{1,257},{257,1},{2,258},{258,2},{3,259},{259,3},{4... | collective-permute-start | bytes 786440 | tf_op jit(solution)/shard_map/ppermute | solution.py:218

commit v2 on v1

v2 whole, which is shorter than its diff:
```python
import functools

import jax
import jax.numpy as jnp
from jax import lax
from jax.experimental import pallas as pl
from jax.experimental.pallas import tpu as pltpu
from jax.sharding import Mesh
from jax.sharding import PartitionSpec as P

HEAD = 128
SPAN = 64
HEADS = 6
ROWS = HEADS * SPAN
SLOTS = 8
KEYS = 16
GROUP = 4
UNROLL = 2
CHUNKS = KEYS // GROUP
STEPS = SLOTS * CHUNKS + UNROLL
SCALING = HEAD ** (-0.5)
LOG2E = 1.4426950408889634
NEG_FILL = -1e30
FAR = 1 << 20
NT = (((1,), (1,)), ((), ()))
NN = (((1,), (0,)), ((), ()))

SLOT = 16
CHUNK = SLOT + STEPS
BASE = CHUNK + STEPS
SPANS = BASE + STEPS
PLACES = SPANS + STEPS * GROUP
TABLE = PLACES + STEPS * GROUP


def dot(a, b, dims):
    return lax.dot_general(a, b, dims, preferred_element_type=jnp.float32)


def start_of(starts, pos):
    first = jnp.zeros_like(pos)
    for s in starts:
        first = jnp.maximum(first, jnp.where(s <= pos, s, 0))
    return first


def prepare_kernel(order_ref, place_ref, episode_ref, own_ref, other_ref, table_ref, q_ref, g_ref):
    y, xl, core = place_ref[0], place_ref[1], place_ref[2]
    ids = episode_ref[...]
    starts = [jnp.sum((ids < v).astype(jnp.int32)) for v in (1, 2, 3)]
    for n, s in enumerate(starts):
        table_ref[1 + n] = s
    key_bases = [
        order_ref[((k // 2) * 4 + xl * 2 + core) * 2 + k % 2] * SPAN for k in range(KEYS)
    ]

    def list_slot(slot, step):
        base = order_ref[y * SLOTS + slot] * SPAN
        first = start_of(starts, base)
        at = step * GROUP
        for k in range(KEYS):
            table_ref[SPANS + at] = k
            table_ref[PLACES + at] = key_bases[k]
            seen = (key_bases[k] <= base) & (key_bases[k] + (SPAN - 1) >= first)
            at = at + seen.astype(jnp.int32)
        count = (at - step * GROUP + GROUP - 1) // GROUP
        for extra in range(GROUP):
            table_ref[SPANS + at + extra] = 0
            table_ref[PLACES + at + extra] = FAR
        for c in range(CHUNKS):
            table_ref[SLOT + step + c] = slot
            table_ref[CHUNK + step + c] = c
            table_ref[BASE + step + c] = base
        return step + count

    steps = lax.fori_loop(0, SLOTS, list_slot, jnp.int32(0))
    for extra in range(UNROLL):
        table_ref[SLOT + steps + extra] = 0
        table_ref[CHUNK + steps + extra] = CHUNKS
        table_ref[BASE + steps + extra] = 0
        for n in range(GROUP):
            table_ref[SPANS + (steps + extra) * GROUP + n] = 0
            table_ref[PLACES + (steps + extra) * GROUP + n] = FAR
    table_ref[0] = (steps + UNROLL - 1) // UNROLL

    for rel, ref in enumerate((own_ref, other_ref)):
        chip = xl if rel == 0 else 1 - xl
        for i in range(SLOTS // 2):
            for h in range(HEADS):
                rows, cols = slice(i * SPAN, (i + 1) * SPAN), slice(h * HEAD, (h + 1) * HEAD)
                out = pl.ds(h * SPAN, SPAN)
                q_ref[chip * 4 + i, out, :] = ref[rows, cols]
                g_ref[chip * 4 + i, out, :] = ref[rows, h * HEAD + HEADS * HEAD : (h + 1 + HEADS) * HEAD]


def load_step(table_ref, kv_ref, q_ref, g_ref, step):
    slot, base = table_ref[SLOT + step], table_ref[BASE + step]
    spans = [table_ref[SPANS + step * GROUP + i] for i in range(GROUP)]
    keys = jnp.concatenate([kv_ref[s, :, :HEAD] for s in spans], axis=0)
    values = jnp.concatenate([kv_ref[s, :, HEAD:] for s in spans], axis=0)
    iota = lax.broadcasted_iota(jnp.int32, (SPAN, HEAD), 0)
    pos = jnp.concatenate(
        [table_ref[PLACES + step * GROUP + i] + iota for i in range(GROUP)], axis=0
    )
    query_pos = base + lax.broadcasted_iota(jnp.int32, (1, HEAD), 1) % SPAN
    first = start_of([table_ref[1 + n] for n in range(3)], query_pos)
    visible = (pos <= query_pos) & (pos >= first)
    query, grad = q_ref[slot], g_ref[slot]
    raw = dot(keys, query, NT)
    scores = jnp.concatenate(
        [
            jnp.where(visible, raw[:, g * HEAD : (g + 1) * HEAD] * (SCALING * LOG2E), NEG_FILL)
            for g in range(ROWS // HEAD)
        ],
        axis=1,
    )
    return slot, spans, keys, query, grad, scores, dot(values, grad, NT)


def run_steps(table_ref, one_step):
    def some(n, unused):
        for u in range(UNROLL):
            one_step(n * UNROLL + u)
        return unused

    lax.fori_loop(0, table_ref[0], some, 0)


def stats_kernel(table_ref, kv_ref, q_ref, g_ref, out_ref, top_ref, total_ref, weighted_ref):
    top_ref[...] = jnp.full_like(top_ref, NEG_FILL)
    total_ref[...] = jnp.zeros_like(total_ref)
    weighted_ref[...] = jnp.zeros_like(weighted_ref)

    def one_step(step):
        slot, spans, keys, query, grad, scores, products = load_step(
            table_ref, kv_ref, q_ref, g_ref, step
        )
        chunk = table_ref[CHUNK + step]
        top = jnp.max(scores, axis=0, keepdims=True)
        weights = jnp.exp2(scores - top)
        row = pl.ds(slot, 1)
        top_ref[chunk, row, :] = top
        total_ref[chunk, row, :] = jnp.sum(weights, axis=0, keepdims=True)
        weighted_ref[chunk, row, :] = jnp.sum(weights * products, axis=0, keepdims=True)

    run_steps(table_ref, one_step)
    parts = range(CHUNKS)
    top = functools.reduce(jnp.maximum, [top_ref[c] for c in parts])
    shares = [jnp.exp2(top_ref[c] - top) for c in parts]
    out_ref[0:8] = top
    out_ref[8:16] = sum(total_ref[c] * shares[c] for c in parts)
    out_ref[16:24] = sum(weighted_ref[c] * shares[c] for c in parts)


def step_gradients(table_ref, kv_ref, q_ref, g_ref, rows_ref, step):
    slot, spans, keys, query, grad, scores, products = load_step(
        table_ref, kv_ref, q_ref, g_ref, step
    )
    probs = jnp.exp2(scores - rows_ref[pl.ds(slot, 1), :])
    score_grad = (probs * (products - rows_ref[pl.ds(8 + slot, 1), :])).astype(jnp.bfloat16)
    return slot, spans, keys, query, grad, probs, score_grad


def key_value_kernel(table_ref, kv_ref, q_ref, g_ref, stats_ref, dkv_ref, rows_ref, acc_ref):
    parts = range(stats_ref.shape[0])
    top = functools.reduce(jnp.maximum, [stats_ref[p, 0:8] for p in parts])
    shares = [jnp.exp2(stats_ref[p, 0:8] - top) for p in parts]
    total = sum(stats_ref[p, 8:16] * shares[p] for p in parts)
    rows_ref[0:8] = top + jnp.log2(total)
    rows_ref[8:16] = sum(stats_ref[p, 16:24] * shares[p] for p in parts) / total
    acc_ref[...] = jnp.zeros_like(acc_ref)

    def one_step(step):
        slot, spans, keys, query, grad, probs, score_grad = step_gradients(
            table_ref, kv_ref, q_ref, g_ref, rows_ref, step
        )
        dk = dot(score_grad, query, NN)
        dv = dot(probs.astype(jnp.bfloat16), grad, NN)
        for n in range(GROUP):
            acc_ref[spans[n], :, :HEAD] += dk[n * SPAN : (n + 1) * SPAN]
            acc_ref[spans[n], :, HEAD:] += dv[n * SPAN : (n + 1) * SPAN]

    run_steps(table_ref, one_step)
    dkv_ref[:, :, :HEAD] = (acc_ref[:, :, :HEAD] * SCALING).astype(jnp.bfloat16)
    dkv_ref[:, :, HEAD:] = acc_ref[:, :, HEAD:].astype(jnp.bfloat16)


def query_kernel(
    place_ref, table_ref, kv_ref, q_ref, g_ref, rows_ref, after_ref, keep_ref, send_ref, acc_ref
):
    acc_ref[...] = jnp.zeros_like(acc_ref)

    def one_step(step):
        slot, spans, keys, query, grad, probs, score_grad = step_gradients(
            table_ref, kv_ref, q_ref, g_ref, rows_ref, step
        )
        acc_ref[slot] += dot(keys.T, score_grad, NN)

    run_steps(table_ref, one_step)
    xl, core = place_ref[1], place_ref[2]
    for rel in range(2):
        chip = xl if rel == 0 else 1 - xl
        for half in range(2):
            rows = slice(half * SPAN, (half + 1) * SPAN)
            mine = acc_ref[chip * 4 + core * 2 + half].T * SCALING
            theirs = acc_ref[chip * 4 + (1 - core) * 2 + half].T * SCALING
            for h in range(HEADS):
                cols, at = slice(h * HEAD, (h + 1) * HEAD), slice(h * SPAN, (h + 1) * SPAN)
                keep_ref[rel, rows, cols] = mine[at]
                send_ref[rel, rows, cols] = theirs[at].astype(jnp.bfloat16)


def swap(block, axis):
    return lax.ppermute(block, axis, [(0, 1), (1, 0)])


def per_device(query_rows, key_rows, stored_value_rows, output_grad, span_order, episode_ids):
    tokens = query_rows.shape[1]
    columns = HEADS * HEAD
    ring = lax.axis_size("y")
    place = jnp.stack([lax.axis_index("y"), lax.axis_index("xl"), lax.axis_index("core")]).astype(
        jnp.int32
    )
    copies = [jnp.broadcast_to(a, (ring, tokens, HEAD)) for a in (key_rows, stored_value_rows)]
    kv_all = lax.all_to_all(jnp.concatenate(copies, axis=2), "y", 0, 0, tiled=True).reshape(
        KEYS, SPAN, 2 * HEAD
    )
    both = jnp.concatenate([query_rows[0], output_grad[0]], axis=1)
    remote = swap(both, "xl")
    own = lax.all_gather(both, "core", axis=0, tiled=True)
    other = lax.all_gather(remote, "core", axis=0, tiled=True)

    smem = pl.BlockSpec(memory_space=pltpu.SMEM)
    vmem = pl.BlockSpec(memory_space=pltpu.VMEM)
    params = pltpu.CompilerParams(vmem_limit_bytes=40 * 1024 * 1024)
    rows_bf16 = jax.ShapeDtypeStruct((SLOTS, ROWS, HEAD), jnp.bfloat16)
    table, q, g = pl.pallas_call(
        prepare_kernel,
        out_shape=(jax.ShapeDtypeStruct((TABLE,), jnp.int32), rows_bf16, rows_bf16),
        in_specs=[smem, smem, vmem, vmem, vmem],
        out_specs=(smem, vmem, vmem),
        compiler_params=params,
        name="prepare",
    )(span_order, place, episode_ids, own, other)
    stats = pl.pallas_call(
        stats_kernel,
        out_shape=jax.ShapeDtypeStruct((24, ROWS), jnp.float32),
        in_specs=[smem, vmem, vmem, vmem],
        out_specs=vmem,
        scratch_shapes=[pltpu.VMEM((CHUNKS + 1, SLOTS, ROWS), jnp.float32)] * 3,
        compiler_params=params,
        name="row_stats",
    )(table, kv_all, q, g)
    stats_all = lax.all_gather(stats, ("xl", "core"), axis=0)
    dkv, rows = pl.pallas_call(
        key_value_kernel,
        out_shape=(
            jax.ShapeDtypeStruct((KEYS, SPAN, 2 * HEAD), jnp.bfloat16),
            jax.ShapeDtypeStruct((16, ROWS), jnp.float32),
        ),
        in_specs=[smem, vmem, vmem, vmem, vmem],
        out_specs=(vmem, vmem),
        scratch_shapes=[pltpu.VMEM((KEYS, SPAN, 2 * HEAD), jnp.float32)],
        compiler_params=params,
        name="key_value_gradients",
    )(table, kv_all, q, g, stats_all)
    dkv_parts = lax.all_to_all(dkv.reshape(ring, tokens, 2 * HEAD), "y", 0, 0, tiled=True)
    keep, send = pl.pallas_call(
        query_kernel,
        out_shape=(
            jax.ShapeDtypeStruct((2, tokens, columns), jnp.float32),
            jax.ShapeDtypeStruct((2, tokens, columns), jnp.bfloat16),
        ),
        in_specs=[smem, smem, vmem, vmem, vmem, vmem, pl.BlockSpec(memory_space=pl.ANY)],
        out_specs=(vmem, vmem),
        scratch_shapes=[pltpu.VMEM((SLOTS, HEAD, ROWS), jnp.float32)],
        compiler_params=params,
        name="query_gradients",
    )(place, table, kv_all, q, g, rows, dkv)
    sent = lax.all_gather(send, "core", axis=0)
    dq = keep + lax.dynamic_index_in_dim(sent, 1 - place[2], 0, False).astype(jnp.float32)
    parts = dq.astype(jnp.bfloat16)
    across = lax.ppermute(parts[1], ("section", "xl"), [(0, 3), (1, 2), (2, 1), (3, 0)])
    straight = swap(parts[0], "section")
    dq_back = (straight.astype(jnp.float32) + across.astype(jnp.float32)).astype(jnp.bfloat16)
    dkv_sum = jnp.sum(dkv_parts.astype(jnp.float32), axis=0).astype(jnp.bfloat16)
    dkv_back = swap(dkv_sum, "section")
    return (dq_back[None], dkv_back[None, :, :HEAD], dkv_back[None, :, HEAD:])


def solution(mesh):
    devices = mesh.devices
    fine = Mesh(
        devices.reshape(devices.shape[0], devices.shape[1], devices.shape[2] // 4, 2, 2),
        ("section", "tp", "y", "xl", "core"),
    )
    rows = P("section", ("y", "xl", "core"), "tp")
    return jax.shard_map(
        per_device,
        mesh=fine,
        in_specs=(rows, rows, rows, rows, P(), P("section", None)),
        out_specs=(rows, rows, rows),
        check_vma=False,
    )
```

time: 95.3 us -> 76.6 us (0.80)
  the two profiles are of different devices: /device:TPU:6 before, /device:TPU:405 now
where the time goes in v2:
time: 76.6 us; the launch traced here: 76.2 us
  starting transfers between devices  23.9 us (31%)
  Pallas kernels  21.1 us (28%)
  blocking collectives  14.3 us (19%)
  waiting for transfers between devices  12.7 us (17%)
  other arithmetic  1.84 us (2%)
  local copies, waits for them, and re-layouts  1.51 us (2%)
    ppermute x3, starting transfers between devices, swap(): return lax.ppermute(block, axis, [(0, 1), (1, 0)])  8.81 us
    pallas_call x1, Pallas kernels, per_device(): pl.pallas_call(key_value_kernel, out_shape=(jax.ShapeDtypeStruct((KEYS, S...  7.65 us
    all_to_all x1, starting transfers between devices, per_device(): lax.all_to_all(jnp.concatenate(copies, axis=2), 'y', 0, 0, tiled=True)  7 us
    pallas_call x1, Pallas kernels, per_device(): pl.pallas_call(query_kernel, out_shape=(jax.ShapeDtypeStruct((2, tokens,...  6.87 us
    all_to_all x1, starting transfers between devices, per_device(): lax.all_to_all(dkv.reshape(ring, tokens, 2 * HEAD), 'y', 0, 0, tiled=True)  6.19 us
    ppermute x1, waiting for transfers between devices, per_device(): lax.ppermute(parts[1], ('section', 'xl'), [(0, 3), (1, 2), (2, 1), (3, 0)])  6.05 us
    ppermute x3, waiting for transfers between devices, swap(): return lax.ppermute(block, axis, [(0, 1), (1, 0)])  5.82 us
    all_gather x1, blocking collectives, per_device(): stats_all = lax.all_gather(stats, ('xl', 'core'), axis=0)  4.32 us
  transfers between devices with their start and end apart: 6, of which 4 were waited for; matrix products, arithmetic and copies ran while one was open for 1% of the time, Pallas kernels for 12%

profile of v2, /device:TPU:405, one launch (start us, length us, event | category | flops | bytes accessed | tf_op | source)
XLA Modules:
  0.0 76.2 jit_solution(15087533624235280214)
XLA Ops:
  0.6 0.0 copy-start.4
  0.6 0.8 %broadcast_in_dim.24 = bf16[8,128,128]{2,1,0:T(8,128)(2,1)S(1)} broadcast(bf16[128,128]{1,0:T(8,128)(2,1)} %bitcast.31), dimensions={1,2} | broadcast | bytes 294912 | tf_op jit(solution)/shard_map/broadcast_in_dim | solution.py:224
  1.4 0.0 copy-done.4
  1.5 0.9 %pad_maximum_fusion = bf16[8,128,256]{2,1,0:T(8,128)(2,1)} fusion(bf16[8,128,128]{2,1,0:T(8,128)(2,1)S(1)} %broadcast_in_dim.26, bf16[8,128,128]{2,1,0:T(8,128)(2,1)S(1)} %broadcast_in_dim.24), kind=kLoop, calls=%fused_computation.2 | loop fusion | flops 1048576 | bytes 1048576 | tf_op jit(solution)/shard_map/concatenate | solution.py:225
  2.3 0.0 copy-start.2
  2.4 0.0 copy-start.3
  2.4 7.0 %all-to-all-start = ((bf16[8,128,256]{2,1,0:T(8,128)(2,1)}), bf16[8,128,256]{2,1,0:T(8,128)(2,1)S(1)}, u32[]{:S(2)}, u32[]{:S(2)}) async-start(bf16[8,128,256]{2,1,0:T(8,128)(2,1)} %pad_maximum_fusion), calls=%async_computation | async-start | bytes 1048576 | tf_op jit(solution)/shard_map/all_to_all | solution.py:225
  9.4 0.0 copy-done.2
  9.4 0.0 copy-done.3
  9.4 2.8 %collective-permute-start = (bf16[128,1536]{1,0:T(8,128)(2,1)S(1)}, bf16[128,1536]{1,0:T(8,128)(2,1)S(1)}, u32[]{:S(2)}, u32[]{:S(2)}) collective-permute-start(bf16[128,1536]{1,0:T(8,128)(2,1)S(1)} %pad_maximum_fusion.1), channel_id=1, source_target_pairs={{0,2},{2,0},{1,3},{3,1},{4,6},{6,4},{5,7},{7,5},{8,10},{10,8},{9,1... | collective-permute-start | bytes 1179656 | tf_op jit(solution)/shard_map/ppermute | solution.py:214
  12.2 0.1 pad_add_fusion.place_ref
  12.3 3.5 %all_gather.18.own_ref = bf16[256,1536]{1,0:T(8,128)(2,1)S(1)} all-gather(bf16[128,1536]{1,0:T(8,128)(2,1)S(1)} %pad_maximum_fusion.1), channel_id=1, replica_groups=mesh['section'=2,'tp'=8,'y'=8,'xl'=2,'core'=2] {'core'}, dimensions={0}, use_global_device_ids=true | all-gather | bytes 1179648 | tf_op jit(solution)/shard_map/all_gather | solution.py:230
  15.8 0.0 copy-start
  15.8 0.0 copy-start.1
  15.8 4.8 %collective-permute-done = bf16[128,1536]{1,0:T(8,128)(2,1)S(1)} collective-permute-done((bf16[128,1536]{1,0:T(8,128)(2,1)S(1)}, bf16[128,1536]{1,0:T(8,128)(2,1)S(1)}, u32[]{:S(2)}, u32[]{:S(2)}) %collective-permute-start) | collective-permute-done | bytes 393248 | tf_op jit(solution)/shard_map/ppermute | solution.py:214
  20.7 4.1 %all_gather.19.other_ref = bf16[256,1536]{1,0:T(8,128)(2,1)S(1)} all-gather(bf16[128,1536]{1,0:T(8,128)(2,1)S(1)} %collective-permute-done), channel_id=1, replica_groups=mesh['section'=2,'tp'=8,'y'=8,'xl'=2,'core'=2] {'core'}, dimensions={0}, use_global_device_ids=true | all-gather | bytes 1179648 | tf_op jit(solution)/shard_map/all_gather | solution.py:231
  24.8 0.0 copy-done
  24.8 0.0 copy-done.1
  24.8 2.3 %prepare.1 = (s32[390]{0:T(512)S(1)}, bf16[8,384,128]{2,1,0:T(8,128)(2,1)S(1)}, bf16[8,384,128]{2,1,0:T(8,128)(2,1)S(1)}) custom-call(s32[64]{0:T(128)S(1)} %copy-done.1, s32[3]{0:T(128)S(1)} %pad_add_fusion.place_ref, s32[1,4096]{1,0:T(1,128)S(1)} %copy-done, bf16[256,1536]{1,0:T(8,128)(2,1)S(1)} %all_gather.18.own_ref, ...), custom_call_target="tpu_custom_call" | custom-call | tf_op jit(solution)/shard_map/prepare/pallas_call | solution.py:237
  27.2 0.0 all-to-all-done
  27.2 4.2 %row_stats.1 = f32[24,384]{1,0:T(8,128)S(1)} custom-call(s32[390]{0:T(512)S(1)} %get-tuple-element.10.table_ref, bf16[16,64,256]{2,1,0:T(8,128)(2,1)S(1)} %bitcast.24, bf16[8,384,128]{2,1,0:T(8,128)(2,1)S(1)} %get-tuple-element.11.q_ref, bf16[8,384,128]{2,1,0:T(8,128)(2,1)S(1)} %get-tuple-element.12.g_ref), custom_call_target="tpu_custom_call" | custom-call | tf_op jit(solution)/shard_map/row_stats/pallas_call | solution.py:245
  31.4 4.3 %all-gather = f32[96,384]{1,0:T(8,128)S(1)} all-gather(f32[24,384]{1,0:T(8,128)S(1)} %row_stats.1), channel_id=2, replica_groups=mesh['section'=2,'tp'=8,'y'=8,'xl'=2,'core'=2] {'xl','core'}, dimensions={0}, use_global_device_ids=true | all-gather | bytes 184320 | tf_op jit(solution)/shard_map/all_gather | solution.py:254
  35.7 7.7 %key_value_gradients.1 = (bf16[16,64,256]{2,1,0:T(8,128)(2,1)}, f32[16,384]{1,0:T(8,128)S(1)}) custom-call(s32[390]{0:T(512)S(1)} %get-tuple-element.10.table_ref, bf16[16,64,256]{2,1,0:T(8,128)(2,1)S(1)} %bitcast.25, bf16[8,384,128]{2,1,0:T(8,128)(2,1)S(1)} %get-tuple-element.11.q_ref, bf16[8,384,128]{2,1,0:T(8,128)(2,1)S(1)} %get-tuple-element.12.g_ref, ...), custom_call_target="tpu_custom_call" | custom-call | tf_op jit(solution)/shard_map/key_value_gradients/pallas_call | solution.py:255
  43.4 6.2 %all-to-all-start.1 = ((bf16[8,128,256]{2,1,0:T(8,128)(2,1)}), bf16[8,128,256]{2,1,0:T(8,128)(2,1)S(1)}, u32[]{:S(2)}, u32[]{:S(2)}) async-start(bf16[8,128,256]{2,1,0:T(8,128)(2,1)} %bitcast.14), calls=%async_computation.1 | async-start | bytes 1048576 | tf_op jit(solution)/shard_map/all_to_all | solution.py:267
  49.6 6.9 %query_gradients.1 = (f32[2,128,768]{2,1,0:T(8,128)S(1)}, bf16[2,128,768]{2,1,0:T(8,128)(2,1)S(1)}) custom-call(s32[3]{0:T(128)S(1)} %pad_add_fusion.place_ref, s32[390]{0:T(512)S(1)} %get-tuple-element.10.table_ref, bf16[16,64,256]{2,1,0:T(8,128)(2,1)S(1)} %bitcast.26, bf16[8,384,128]{2,1,0:T(8,128)(2,1)S(1)} %get-tuple-element.11.q_ref, ...), custom_call_target="tpu_custom_call" | custom-call | tf_op jit(solution)/shard_map/query_gradients/pallas_call | solution.py:268
  56.5 2.4 %all-gather.1 = bf16[4,128,768]{2,1,0:T(8,128)(2,1)S(1)} all-gather(bf16[2,128,768]{2,1,0:T(8,128)(2,1)S(1)} %get-tuple-element.16), channel_id=3, replica_groups=mesh['section'=2,'tp'=8,'y'=8,'xl'=2,'core'=2] {'core'}, dimensions={0}, use_global_device_ids=true | all-gather | bytes 1179648 | tf_op jit(solution)/shard_map/all_gather | solution.py:280
  58.8 0.1 fusion
  59.0 2.1 %collective-permute-start.1 = (bf16[128,768]{1,0:T(8,128)(2,1)S(1)}, bf16[128,768]{1,0:T(8,128)(2,1)S(1)}, u32[]{:S(2)}, u32[]{:S(2)}) collective-permute-start(bf16[128,768]{1,0:T(8,128)(2,1)S(1)} %get-tuple-element.17), channel_id=1, source_target_pairs={{0,256},{256,0},{1,257},{257,1},{2,258},{258,2},{3,259},{259,3},{4... | collective-permute-start | bytes 589832 | tf_op jit(solution)/shard_map/ppermute | solution.py:214
  61.1 1.9 %collective-permute-start.2 = (bf16[128,768]{1,0:T(8,128)(2,1)S(1)}, bf16[128,768]{1,0:T(8,128)(2,1)S(1)}, u32[]{:S(2)}, u32[]{:S(2)}) collective-permute-start(bf16[128,768]{1,0:T(8,128)(2,1)S(1)} %get-tuple-element.18), channel_id=1, source_target_pairs={{0,258},{2,256},{256,2},{258,0},{1,259},{3,257},{257,3},{259,1},{4... | collective-permute-start | bytes 589832 | tf_op jit(solution)/shard_map/ppermute | solution.py:283
  63.0 0.8 %all-to-all-done.1 = bf16[8,128,256]{2,1,0:T(8,128)(2,1)S(1)} async-done(((bf16[8,128,256]{2,1,0:T(8,128)(2,1)}), bf16[8,128,256]{2,1,0:T(8,128)(2,1)S(1)}, u32[]{:S(2)}, u32[]{:S(2)}) %all-to-all-start.1) | async-done | bytes 524320 | tf_op jit(solution)/shard_map/all_to_all | solution.py:267
  63.8 0.1 reduce_sum.12
  63.9 3.9 %collective-permute-start.3 = (bf16[128,256]{1,0:T(8,128)(2,1)S(1)}, bf16[128,256]{1,0:T(8,128)(2,1)S(1)}, u32[]{:S(2)}, u32[]{:S(2)}) collective-permute-start(bf16[128,256]{1,0:T(8,128)(2,1)S(1)} %reduce_sum.12), channel_id=1, source_target_pairs={{0,256},{256,0},{1,257},{257,1},{2,258},{258,2},{3,259},{259,3},{4... | collective-permute-start | bytes 196616 | tf_op jit(solution)/shard_map/ppermute | solution.py:214
  67.8 1.0 %collective-permute-done.1 = bf16[128,768]{1,0:T(8,128)(2,1)S(1)} collective-permute-done((bf16[128,768]{1,0:T(8,128)(2,1)S(1)}, bf16[128,768]{1,0:T(8,128)(2,1)S(1)}, u32[]{:S(2)}, u32[]{:S(2)}) %collective-permute-start.1) | collective-permute-done | bytes 196640 | tf_op jit(solution)/shard_map/ppermute | solution.py:214
  68.8 6.0 %collective-permute-done.2 = bf16[128,768]{1,0:T(8,128)(2,1)S(1)} collective-permute-done((bf16[128,768]{1,0:T(8,128)(2,1)S(1)}, bf16[128,768]{1,0:T(8,128)(2,1)S(1)}, u32[]{:S(2)}, u32[]{:S(2)}) %collective-permute-start.2) | collective-permute-done | bytes 196640 | tf_op jit(solution)/shard_map/ppermute | solution.py:283
  74.8 0.7 fusion.1
  75.5 0.0 collective-permute-done.3
  75.5 0.6 slice_bitcast_fusion.2
  (3 shorter events, 0.1 us)
Async XLA Ops:
  0.6 0.8 %copy-start.4 = (bf16[1,128,128]{2,1,0:T(8,128)(2,1)S(1)}, bf16[1,128,128]{2,1,0:T(8,128)(2,1)}, u32[]{:S(2)}) copy-start(bf16[1,128,128]{2,1,0:T(8,128)(2,1)} %param.8) | copy-start | bytes 98308
  2.3 7.0 %copy-start.2 = (bf16[1,128,768]{2,1,0:T(8,128)(2,1)S(1)}, bf16[1,128,768]{2,1,0:T(8,128)(2,1)}, u32[]{:S(2)}) copy-start(bf16[1,128,768]{2,1,0:T(8,128)(2,1)} %param.9) | copy-start | bytes 589828
  2.4 7.0 %copy-start.3 = (bf16[1,128,768]{2,1,0:T(8,128)(2,1)S(1)}, bf16[1,128,768]{2,1,0:T(8,128)(2,1)}, u32[]{:S(2)}) copy-start(bf16[1,128,768]{2,1,0:T(8,128)(2,1)} %param.6) | copy-start | bytes 589828
  2.4 24.8 %all-to-all-start = ((bf16[8,128,256]{2,1,0:T(8,128)(2,1)}), bf16[8,128,256]{2,1,0:T(8,128)(2,1)S(1)}, u32[]{:S(2)}, u32[]{:S(2)}) async-start(bf16[8,128,256]{2,1,0:T(8,128)(2,1)} %pad_maximum_fusion), calls=%async_computation | async-start | bytes 1048576 | tf_op jit(solution)/shard_map/all_to_all | solution.py:225
  9.4 11.3 %collective-permute-start = (bf16[128,1536]{1,0:T(8,128)(2,1)S(1)}, bf16[128,1536]{1,0:T(8,128)(2,1)S(1)}, u32[]{:S(2)}, u32[]{:S(2)}) collective-permute-start(bf16[128,1536]{1,0:T(8,128)(2,1)S(1)} %pad_maximum_fusion.1), channel_id=1, source_target_pairs={{0,2},{2,0},{1,3},{3,1},{4,6},{6,4},{5,7},{7,5},{8,10},{10,8},{9,1... | collective-permute-start | bytes 1179656 | tf_op jit(solution)/shard_map/ppermute | solution.py:214
  15.8 9.0 %copy-start = (s32[1,4096]{1,0:T(1,128)S(1)}, s32[1,4096]{1,0:T(1,128)}, u32[]{:S(2)}) copy-start(s32[1,4096]{1,0:T(1,128)} %episode_ref.1) | copy-start | bytes 49156
  15.8 9.0 %copy-start.1 = (s32[64]{0:T(128)S(1)}, s32[64]{0:T(128)}, u32[]{:S(2)}) copy-start(s32[64]{0:T(128)} %order_ref.1) | copy-start | bytes 772
  43.4 20.4 %all-to-all-start.1 = ((bf16[8,128,256]{2,1,0:T(8,128)(2,1)}), bf16[8,128,256]{2,1,0:T(8,128)(2,1)S(1)}, u32[]{:S(2)}, u32[]{:S(2)}) async-start(bf16[8,128,256]{2,1,0:T(8,128)(2,1)} %bitcast.14), calls=%async_computation.1 | async-start | bytes 1048576 | tf_op jit(solution)/shard_map/all_to_all | solution.py:267
  59.0 9.8 %collective-permute-start.1 = (bf16[128,768]{1,0:T(8,128)(2,1)S(1)}, bf16[128,768]{1,0:T(8,128)(2,1)S(1)}, u32[]{:S(2)}, u32[]{:S(2)}) collective-permute-start(bf16[128,768]{1,0:T(8,128)(2,1)S(1)} %get-tuple-element.17), channel_id=1, source_target_pairs={{0,256},{256,0},{1,257},{257,1},{2,258},{258,2},{3,259},{259,3},{4... | collective-permute-start | bytes 589832 | tf_op jit(solution)/shard_map/ppermute | solution.py:214
  61.1 13.7 %collective-permute-start.2 = (bf16[128,768]{1,0:T(8,128)(2,1)S(1)}, bf16[128,768]{1,0:T(8,128)(2,1)S(1)}, u32[]{:S(2)}, u32[]{:S(2)}) collective-permute-start(bf16[128,768]{1,0:T(8,128)(2,1)S(1)} %get-tuple-element.18), channel_id=1, source_target_pairs={{0,258},{2,256},{256,2},{258,0},{1,259},{3,257},{257,3},{259,1},{4... | collective-permute-start | bytes 589832 | tf_op jit(solution)/shard_map/ppermute | solution.py:283
  63.9 11.7 %collective-permute-start.3 = (bf16[128,256]{1,0:T(8,128)(2,1)S(1)}, bf16[128,256]{1,0:T(8,128)(2,1)S(1)}, u32[]{:S(2)}, u32[]{:S(2)}) collective-permute-start(bf16[128,256]{1,0:T(8,128)(2,1)S(1)} %reduce_sum.12), channel_id=1, source_target_pairs={{0,256},{256,0},{1,257},{257,1},{2,258},{258,2},{3,259},{259,3},{4... | collective-permute-start | bytes 196616 | tf_op jit(solution)/shard_map/ppermute | solution.py:214

commit v3 on v2

--- a/solution.py
+++ b/solution.py
@@ -15,9 +15,9 @@
 SLOTS = 8
 KEYS = 16
 GROUP = 4
-UNROLL = 2
+UNROLL = 4
 CHUNKS = KEYS // GROUP
-STEPS = SLOTS * CHUNKS + UNROLL
+STEPS = SLOTS * CHUNKS + CHUNKS
 SCALING = HEAD ** (-0.5)
 LOG2E = 1.4426950408889634
 NEG_FILL = -1e30
@@ -44,7 +44,9 @@
     return first
 
 
-def prepare_kernel(order_ref, place_ref, episode_ref, own_ref, other_ref, table_ref, q_ref, g_ref):
+def prepare_kernel(
+    order_ref, place_ref, episode_ref, own_ref, table_ref, q_ref, g_ref
+):
     y, xl, core = place_ref[0], place_ref[1], place_ref[2]
     ids = episode_ref[...]
     starts = [jnp.sum((ids < v).astype(jnp.int32)) for v in (1, 2, 3)]
@@ -73,24 +75,17 @@
             table_ref[BASE + step + c] = base
         return step + count
 
-    steps = lax.fori_loop(0, SLOTS, list_slot, jnp.int32(0))
-    for extra in range(UNROLL):
-        table_ref[SLOT + steps + extra] = 0
-        table_ref[CHUNK + steps + extra] = CHUNKS
-        table_ref[BASE + steps + extra] = 0
-        for n in range(GROUP):
-            table_ref[SPANS + (steps + extra) * GROUP + n] = 0
-            table_ref[PLACES + (steps + extra) * GROUP + n] = FAR
-    table_ref[0] = (steps + UNROLL - 1) // UNROLL
-
-    for rel, ref in enumerate((own_ref, other_ref)):
-        chip = xl if rel == 0 else 1 - xl
+    table_ref[0] = lax.fori_loop(0, SLOTS, list_slot, jnp.int32(0))
+    lay_out(own_ref, q_ref, g_ref, xl)
+
+
+def lay_out(ref, q_ref, g_ref, chip):
+    for n, out_ref in enumerate((q_ref, g_ref)):
         for i in range(SLOTS // 2):
             for h in range(HEADS):
-                rows, cols = slice(i * SPAN, (i + 1) * SPAN), slice(h * HEAD, (h + 1) * HEAD)
-                out = pl.ds(h * SPAN, SPAN)
-                q_ref[chip * 4 + i, out, :] = ref[rows, cols]
-                g_ref[chip * 4 + i, out, :] = ref[rows, h * HEAD + HEADS * HEAD : (h + 1 + HEADS) * HEAD]
+                out_ref[chip * 4 + i, h * SPAN : (h + 1) * SPAN, :] = ref[
+                    i * SPAN : (i + 1) * SPAN, (n * HEADS + h) * HEAD : (n * HEADS + h + 1) * HEAD
+                ]
 
 
 def load_step(table_ref, kv_ref, q_ref, g_ref, step):
@@ -123,10 +118,27 @@
             one_step(n * UNROLL + u)
         return unused
 
-    lax.fori_loop(0, table_ref[0], some, 0)
-
-
-def stats_kernel(table_ref, kv_ref, q_ref, g_ref, out_ref, top_ref, total_ref, weighted_ref):
+    count = table_ref[0]
+    whole = count // UNROLL
+    lax.fori_loop(0, whole, some, 0)
+    lax.fori_loop(whole * UNROLL, count, lambda step, unused: (one_step(step), unused)[1], 0)
+
+
+def stats_kernel(
+    place_ref,
+    table_ref,
+    kv_ref,
+    other_ref,
+    q_in_ref,
+    g_in_ref,
+    q_ref,
+    g_ref,
+    out_ref,
+    top_ref,
+    total_ref,
+    weighted_ref,
+):
+    lay_out(other_ref, q_ref, g_ref, 1 - place_ref[1])
     top_ref[...] = jnp.full_like(top_ref, NEG_FILL)
     total_ref[...] = jnp.zeros_like(total_ref)
     weighted_ref[...] = jnp.zeros_like(weighted_ref)
@@ -214,74 +226,102 @@
     return lax.ppermute(block, axis, [(0, 1), (1, 0)])
 
 
+def call(kernel, name, out_shape, in_specs, out_specs, scratch=(), aliases={}):
+    return pl.pallas_call(
+        kernel,
+        out_shape=out_shape,
+        in_specs=in_specs,
+        out_specs=out_specs,
+        scratch_shapes=scratch,
+        input_output_aliases=aliases,
+        compiler_params=pltpu.CompilerParams(vmem_limit_bytes=40 * 1024 * 1024),
+        name=name,
+    )
+
+
+SMEM = pl.BlockSpec(memory_space=pltpu.SMEM)
+VMEM = pl.BlockSpec(memory_space=pltpu.VMEM)
+
+
+LAID_OUT = jax.ShapeDtypeStruct((SLOTS, ROWS, HEAD), jnp.bfloat16)
+
+
+def prepare(order, place, episodes, own):
+    return call(
+        prepare_kernel,
+        "prepare",
+        (jax.ShapeDtypeStruct((TABLE,), jnp.int32), LAID_OUT, LAID_OUT),
+        [SMEM, SMEM, VMEM, VMEM],
+        (SMEM, VMEM, VMEM),
+    )(order, place, episodes, own)
+
+
+def row_stats(place, table, kv_all, other, q, g):
+    return call(
+        stats_kernel,
+        "row_stats",
+        (LAID_OUT, LAID_OUT, jax.ShapeDtypeStruct((24, ROWS), jnp.float32)),
+        [SMEM, SMEM, VMEM, VMEM, VMEM, VMEM],
+        (VMEM, VMEM, VMEM),
+        [pltpu.VMEM((CHUNKS, SLOTS, ROWS), jnp.float32)] * 3,
+        {4: 0, 5: 1},
+    )(place, table, kv_all, other, q, g)
+
+
+def key_value_gradients(table, kv_all, q, g, stats_all):
+    return call(
+        key_value_kernel,
+        "key_value_gradients",
+        (
+            jax.ShapeDtypeStruct((KEYS, SPAN, 2 * HEAD), jnp.bfloat16),
+            jax.ShapeDtypeStruct((16, ROWS), jnp.float32),
+        ),
+        [SMEM, VMEM, VMEM, VMEM, VMEM],
+        (VMEM, VMEM),
+        [pltpu.VMEM((KEYS, SPAN, 2 * HEAD), jnp.float32)],
+    )(table, kv_all, q, g, stats_all)
+
+
+def query_gradients(place, table, kv_all, q, g, rows, after):
+    shape = (2, 2 * SPAN, HEADS * HEAD)
+    return call(
+        query_kernel,
+        "query_gradients",
+        (
+            jax.ShapeDtypeStruct(shape, jnp.float32),
+            jax.ShapeDtypeStruct(shape, jnp.bfloat16),
+        ),
+        [SMEM, SMEM, VMEM, VMEM, VMEM, VMEM, pl.BlockSpec(memory_space=pl.ANY)],
+        (VMEM, VMEM),
+        [pltpu.VMEM((SLOTS, HEAD, ROWS), jnp.float32)],
+    )(place, table, kv_all, q, g, rows, after)
+
+
 def per_device(query_rows, key_rows, stored_value_rows, output_grad, span_order, episode_ids):
     tokens = query_rows.shape[1]
-    columns = HEADS * HEAD
     ring = lax.axis_size("y")
     place = jnp.stack([lax.axis_index("y"), lax.axis_index("xl"), lax.axis_index("core")]).astype(
         jnp.int32
     )
-    copies = [jnp.broadcast_to(a, (ring, tokens, HEAD)) for a in (key_rows, stored_value_rows)]
-    kv_all = lax.all_to_all(jnp.concatenate(copies, axis=2), "y", 0, 0, tiled=True).reshape(
-        KEYS, SPAN, 2 * HEAD
-    )
+    kv = jnp.concatenate([key_rows[0], stored_value_rows[0]], axis=1)
+    kv_all = lax.all_to_all(
+        jnp.broadcast_to(kv[None], (ring, tokens, 2 * HEAD)), "y", 0, 0, tiled=True
+    ).reshape(KEYS, SPAN, 2 * HEAD)
     both = jnp.concatenate([query_rows[0], output_grad[0]], axis=1)
     remote = swap(both, "xl")
     own = lax.all_gather(both, "core", axis=0, tiled=True)
     other = lax.all_gather(remote, "core", axis=0, tiled=True)
-
-    smem = pl.BlockSpec(memory_space=pltpu.SMEM)
-    vmem = pl.BlockSpec(memory_space=pltpu.VMEM)
-    params = pltpu.CompilerParams(vmem_limit_bytes=40 * 1024 * 1024)
-    rows_bf16 = jax.ShapeDtypeStruct((SLOTS, ROWS, HEAD), jnp.bfloat16)
-    table, q, g = pl.pallas_call(
-        prepare_kernel,
-        out_shape=(jax.ShapeDtypeStruct((TABLE,), jnp.int32), rows_bf16, rows_bf16),
-        in_specs=[smem, smem, vmem, vmem, vmem],
-        out_specs=(smem, vmem, vmem),
-        compiler_params=params,
-        name="prepare",
-    )(span_order, place, episode_ids, own, other)
-    stats = pl.pallas_call(
-        stats_kernel,
-        out_shape=jax.ShapeDtypeStruct((24, ROWS), jnp.float32),
-        in_specs=[smem, vmem, vmem, vmem],
-        out_specs=vmem,
-        scratch_shapes=[pltpu.VMEM((CHUNKS + 1, SLOTS, ROWS), jnp.float32)] * 3,
-        compiler_params=params,
-        name="row_stats",
-    )(table, kv_all, q, g)
+    table, q, g = prepare(span_order, place, episode_ids, own)
+    q, g, stats = row_stats(place, table, kv_all, other, q, g)
     stats_all = lax.all_gather(stats, ("xl", "core"), axis=0)
-    dkv, rows = pl.pallas_call(
-        key_value_kernel,
-        out_shape=(
-            jax.ShapeDtypeStruct((KEYS, SPAN, 2 * HEAD), jnp.bfloat16),
-            jax.ShapeDtypeStruct((16, ROWS), jnp.float32),
-        ),
-        in_specs=[smem, vmem, vmem, vmem, vmem],
-        out_specs=(vmem, vmem),
-        scratch_shapes=[pltpu.VMEM((KEYS, SPAN, 2 * HEAD), jnp.float32)],
-        compiler_params=params,
-        name="key_value_gradients",
-    )(table, kv_all, q, g, stats_all)
+    dkv, rows = key_value_gradients(table, kv_all, q, g, stats_all)
     dkv_parts = lax.all_to_all(dkv.reshape(ring, tokens, 2 * HEAD), "y", 0, 0, tiled=True)
-    keep, send = pl.pallas_call(
-        query_kernel,
-        out_shape=(
-            jax.ShapeDtypeStruct((2, tokens, columns), jnp.float32),
-            jax.ShapeDtypeStruct((2, tokens, columns), jnp.bfloat16),
-        ),
-        in_specs=[smem, smem, vmem, vmem, vmem, vmem, pl.BlockSpec(memory_space=pl.ANY)],
-        out_specs=(vmem, vmem),
-        scratch_shapes=[pltpu.VMEM((SLOTS, HEAD, ROWS), jnp.float32)],
-        compiler_params=params,
-        name="query_gradients",
-    )(place, table, kv_all, q, g, rows, dkv)
+    keep, send = query_gradients(place, table, kv_all, q, g, rows, dkv)
     sent = lax.all_gather(send, "core", axis=0)
     dq = keep + lax.dynamic_index_in_dim(sent, 1 - place[2], 0, False).astype(jnp.float32)
     parts = dq.astype(jnp.bfloat16)
+    straight = swap(parts[0], "section")
     across = lax.ppermute(parts[1], ("section", "xl"), [(0, 3), (1, 2), (2, 1), (3, 0)])
-    straight = swap(parts[0], "section")
     dq_back = (straight.astype(jnp.float32) + across.astype(jnp.float32)).astype(jnp.bfloat16)
     dkv_sum = jnp.sum(dkv_parts.astype(jnp.float32), axis=0).astype(jnp.bfloat16)
     dkv_back = swap(dkv_sum, "section")

time: 76.6 us -> 72.5 us (0.946)
  the two profiles are of different devices: /device:TPU:405 before, /device:TPU:6 now
where the time goes in v3:
time: 72.5 us; the launch traced here: 72 us
  starting transfers between devices  21.6 us (30%)
  Pallas kernels  16 us (22%)
  waiting for transfers between devices  16 us (22%)
  blocking collectives  14.4 us (20%)
  other arithmetic  1.77 us (2%)
  local copies, waits for them, and re-layouts  1.5 us (2%)
  between operations  0.75 us (1%)
    ppermute x3, starting transfers between devices, swap(): return lax.ppermute(block, axis, [(0, 1), (1, 0)])  7.38 us
    all_to_all x1, starting transfers between devices, per_device(): lax.all_to_all(jnp.broadcast_to(kv[None], (ring, tokens, 2 * HEAD)), 'y',...  7.23 us
    ppermute x3, waiting for transfers between devices, swap(): return lax.ppermute(block, axis, [(0, 1), (1, 0)])  6.8 us
    pallas_call x1, Pallas kernels, key_value_gradients(): call(key_value_kernel, 'key_value_gradients', (jax.ShapeDtypeStruct((KEYS...  5.66 us
    all_gather x1, blocking collectives, per_device(): stats_all = lax.all_gather(stats, ('xl', 'core'), axis=0)  5.47 us
    pallas_call x1, Pallas kernels, query_gradients(): call(query_kernel, 'query_gradients', (jax.ShapeDtypeStruct(shape, jnp.fl...  5 us
    all_to_all x1, waiting for transfers between devices, per_device(): lax.all_to_all(dkv.reshape(ring, tokens, 2 * HEAD), 'y', 0, 0, tiled=True)  4.2 us
    all_gather x1, blocking collectives, per_device(): sent = lax.all_gather(send, 'core', axis=0)  4.09 us
  transfers between devices with their start and end apart: 6, of which 5 were waited for; matrix products, arithmetic and copies ran while one was open for 1% of the time, Pallas kernels for 10%

profile of v3, /device:TPU:6, one launch (start us, length us, event | category | flops | bytes accessed | tf_op | source)
XLA Modules:
  0.0 72.0 jit_solution(7361714607699713171)
XLA Ops:
  0.6 0.8 %pad_maximum_fusion.1 = bf16[128,256]{1,0:T(8,128)(2,1)S(1)} fusion(bf16[128,128]{1,0:T(8,128)(2,1)} %bitcast.31, bf16[128,128]{1,0:T(8,128)(2,1)} %bitcast.32), kind=kLoop, calls=%fused_computation.7 | loop fusion | flops 131072 | bytes 131072 | tf_op jit(solution)/shard_map/concatenate | solution.py:306
  1.4 0.8 %broadcast_in_dim.15 = bf16[8,128,256]{2,1,0:T(8,128)(2,1)} broadcast(bf16[128,256]{1,0:T(8,128)(2,1)S(1)} %pad_maximum_fusion.1), dimensions={1,2} | broadcast | bytes 589824 | tf_op jit(solution)/shard_map/broadcast_in_dim | solution.py:308
  2.2 0.0 copy-start.2
  2.2 0.0 copy-start.3
  2.2 7.2 %all-to-all-start = ((bf16[8,128,256]{2,1,0:T(8,128)(2,1)}), bf16[8,128,256]{2,1,0:T(8,128)(2,1)S(1)}, u32[]{:S(2)}, u32[]{:S(2)}) async-start(bf16[8,128,256]{2,1,0:T(8,128)(2,1)} %broadcast_in_dim.15), calls=%async_computation | async-start | bytes 1048576 | tf_op jit(solution)/shard_map/all_to_all | solution.py:307
  9.5 0.0 copy-done.2
  9.5 0.0 copy-done.3
  9.5 2.7 %collective-permute-start = (bf16[128,1536]{1,0:T(8,128)(2,1)S(1)}, bf16[128,1536]{1,0:T(8,128)(2,1)S(1)}, u32[]{:S(2)}, u32[]{:S(2)}) collective-permute-start(bf16[128,1536]{1,0:T(8,128)(2,1)S(1)} %pad_maximum_fusion), channel_id=1, source_target_pairs={{0,2},{2,0},{1,3},{3,1},{4,6},{6,4},{5,7},{7,5},{8,10},{10,8},{9,1... | collective-permute-start | bytes 1179656 | tf_op jit(solution)/shard_map/ppermute | solution.py:226
  12.3 0.1 pad_add_fusion.place_ref
  12.4 0.0 copy-start
  12.4 0.0 copy-start.1
  12.4 2.5 %all_gather.18.own_ref = bf16[256,1536]{1,0:T(8,128)(2,1)S(1)} all-gather(bf16[128,1536]{1,0:T(8,128)(2,1)S(1)} %pad_maximum_fusion), channel_id=1, replica_groups=mesh['section'=2,'tp'=8,'y'=8,'xl'=2,'core'=2] {'core'}, dimensions={0}, use_global_device_ids=true | all-gather | bytes 1179648 | tf_op jit(solution)/shard_map/all_gather | solution.py:312
  14.8 0.0 copy-done
  14.9 0.0 copy-done.1
  14.9 2.2 %prepare.1 = (s32[412]{0:T(512)S(1)}, bf16[8,384,128]{2,1,0:T(8,128)(2,1)S(1)}, bf16[8,384,128]{2,1,0:T(8,128)(2,1)S(1)}) custom-call(s32[64]{0:T(128)S(1)} %copy-done.1, s32[3]{0:T(128)S(1)} %pad_add_fusion.place_ref, s32[1,4096]{1,0:T(1,128)S(1)} %copy-done, bf16[256,1536]{1,0:T(8,128)(2,1)S(1)} %all_gather.18.own_ref), custom_call_target="tpu_custom_call" | custom-call | tf_op jit(solution)/shard_map/prepare/pallas_call | solution.py:250
  17.0 4.9 %collective-permute-done = bf16[128,1536]{1,0:T(8,128)(2,1)S(1)} collective-permute-done((bf16[128,1536]{1,0:T(8,128)(2,1)S(1)}, bf16[128,1536]{1,0:T(8,128)(2,1)S(1)}, u32[]{:S(2)}, u32[]{:S(2)}) %collective-permute-start) | collective-permute-done | bytes 393248 | tf_op jit(solution)/shard_map/ppermute | solution.py:226
  22.0 2.4 %all_gather.19.other_ref = bf16[256,1536]{1,0:T(8,128)(2,1)S(1)} all-gather(bf16[128,1536]{1,0:T(8,128)(2,1)S(1)} %collective-permute-done), channel_id=1, replica_groups=mesh['section'=2,'tp'=8,'y'=8,'xl'=2,'core'=2] {'core'}, dimensions={0}, use_global_device_ids=true | all-gather | bytes 1179648 | tf_op jit(solution)/shard_map/all_gather | solution.py:313
  24.4 2.6 %all-to-all-done = bf16[8,128,256]{2,1,0:T(8,128)(2,1)S(1)} async-done(((bf16[8,128,256]{2,1,0:T(8,128)(2,1)}), bf16[8,128,256]{2,1,0:T(8,128)(2,1)S(1)}, u32[]{:S(2)}, u32[]{:S(2)}) %all-to-all-start) | async-done | bytes 524320 | tf_op jit(solution)/shard_map/all_to_all | solution.py:307
  27.0 3.2 %row_stats.1 = (bf16[8,384,128]{2,1,0:T(8,128)(2,1)S(1)}, bf16[8,384,128]{2,1,0:T(8,128)(2,1)S(1)}, f32[24,384]{1,0:T(8,128)S(1)}) custom-call(s32[3]{0:T(128)S(1)} %pad_add_fusion.place_ref, s32[412]{0:T(512)S(1)} %get-tuple-element.13.table_ref, bf16[16,64,256]{2,1,0:T(8,128)(2,1)S(1)} %bitcast.24, ...), custom_call_target="tpu_custom_call", output_to_operand_aliasing={{0}: (4, {}), {1}: (5, {})} | custom-call | tf_op jit(solution)/shard_map/row_stats/pallas_call | solution.py:260
  30.2 5.5 %all-gather = f32[96,384]{1,0:T(8,128)S(1)} all-gather(f32[24,384]{1,0:T(8,128)S(1)} %get-tuple-element.18), channel_id=2, replica_groups=mesh['section'=2,'tp'=8,'y'=8,'xl'=2,'core'=2] {'xl','core'}, dimensions={0}, use_global_device_ids=true | all-gather | bytes 184320 | tf_op jit(solution)/shard_map/all_gather | solution.py:316
  35.6 5.7 %key_value_gradients.1 = (bf16[16,64,256]{2,1,0:T(8,128)(2,1)}, f32[16,384]{1,0:T(8,128)S(1)}) custom-call(s32[412]{0:T(512)S(1)} %get-tuple-element.13.table_ref, bf16[16,64,256]{2,1,0:T(8,128)(2,1)S(1)} %bitcast.25, bf16[8,384,128]{2,1,0:T(8,128)(2,1)S(1)} %get-tuple-element.16.q_ref, bf16[8,384,128]{2,1,0:T(8,128)(2,1)S(1)} %get-tuple-element.17.g_ref, ...), custom_call_target="tpu_custom_call" | custom-call | tf_op jit(solution)/shard_map/key_value_gradients/pallas_call | solution.py:272
  41.3 3.5 %all-to-all-start.1 = ((bf16[8,128,256]{2,1,0:T(8,128)(2,1)}), bf16[8,128,256]{2,1,0:T(8,128)(2,1)S(1)}, u32[]{:S(2)}, u32[]{:S(2)}) async-start(bf16[8,128,256]{2,1,0:T(8,128)(2,1)} %bitcast.14), calls=%async_computation.1 | async-start | bytes 1048576 | tf_op jit(solution)/shard_map/all_to_all | solution.py:318
  44.8 5.0 %query_gradients.1 = (f32[2,128,768]{2,1,0:T(8,128)S(1)}, bf16[2,128,768]{2,1,0:T(8,128)(2,1)S(1)}) custom-call(s32[3]{0:T(128)S(1)} %pad_add_fusion.place_ref, s32[412]{0:T(512)S(1)} %get-tuple-element.13.table_ref, bf16[16,64,256]{2,1,0:T(8,128)(2,1)S(1)} %bitcast.26, bf16[8,384,128]{2,1,0:T(8,128)(2,1)S(1)} %get-tuple-element.16.q_ref, ...), custom_call_target="tpu_custom_call" | custom-call | tf_op jit(solution)/shard_map/query_gradients/pallas_call | solution.py:287
  49.8 4.1 %all-gather.1 = bf16[4,128,768]{2,1,0:T(8,128)(2,1)S(1)} all-gather(bf16[2,128,768]{2,1,0:T(8,128)(2,1)S(1)} %get-tuple-element.22), channel_id=3, replica_groups=mesh['section'=2,'tp'=8,'y'=8,'xl'=2,'core'=2] {'core'}, dimensions={0}, use_global_device_ids=true | all-gather | bytes 1179648 | tf_op jit(solution)/shard_map/all_gather | solution.py:320
  53.9 0.1 fusion
  54.0 1.9 %collective-permute-start.1 = (bf16[128,768]{1,0:T(8,128)(2,1)S(1)}, bf16[128,768]{1,0:T(8,128)(2,1)S(1)}, u32[]{:S(2)}, u32[]{:S(2)}) collective-permute-start(bf16[128,768]{1,0:T(8,128)(2,1)S(1)} %get-tuple-element.23), channel_id=1, source_target_pairs={{0,256},{256,0},{1,257},{257,1},{2,258},{258,2},{3,259},{259,3},{4... | collective-permute-start | bytes 589832 | tf_op jit(solution)/shard_map/ppermute | solution.py:226
  55.9 3.5 %collective-permute-start.2 = (bf16[128,768]{1,0:T(8,128)(2,1)S(1)}, bf16[128,768]{1,0:T(8,128)(2,1)S(1)}, u32[]{:S(2)}, u32[]{:S(2)}) collective-permute-start(bf16[128,768]{1,0:T(8,128)(2,1)S(1)} %get-tuple-element.24), channel_id=1, source_target_pairs={{0,258},{2,256},{256,2},{258,0},{1,259},{3,257},{257,3},{259,1},{4... | collective-permute-start | bytes 589832 | tf_op jit(solution)/shard_map/ppermute | solution.py:324
  59.4 4.2 %all-to-all-done.1 = bf16[8,128,256]{2,1,0:T(8,128)(2,1)S(1)} async-done(((bf16[8,128,256]{2,1,0:T(8,128)(2,1)}), bf16[8,128,256]{2,1,0:T(8,128)(2,1)S(1)}, u32[]{:S(2)}, u32[]{:S(2)}) %all-to-all-start.1) | async-done | bytes 524320 | tf_op jit(solution)/shard_map/all_to_all | solution.py:318
  63.6 0.1 reduce_sum.12
  63.7 2.7 %collective-permute-start.3 = (bf16[128,256]{1,0:T(8,128)(2,1)S(1)}, bf16[128,256]{1,0:T(8,128)(2,1)S(1)}, u32[]{:S(2)}, u32[]{:S(2)}) collective-permute-start(bf16[128,256]{1,0:T(8,128)(2,1)S(1)} %reduce_sum.12), channel_id=1, source_target_pairs={{0,256},{256,0},{1,257},{257,1},{2,258},{258,2},{3,259},{259,3},{4... | collective-permute-start | bytes 196616 | tf_op jit(solution)/shard_map/ppermute | solution.py:226
  66.4 0.0 collective-permute-done.1
  66.5 2.4 %collective-permute-done.2 = bf16[128,768]{1,0:T(8,128)(2,1)S(1)} collective-permute-done((bf16[128,768]{1,0:T(8,128)(2,1)S(1)}, bf16[128,768]{1,0:T(8,128)(2,1)S(1)}, u32[]{:S(2)}, u32[]{:S(2)}) %collective-permute-start.2) | collective-permute-done | bytes 196640 | tf_op jit(solution)/shard_map/ppermute | solution.py:324
  68.8 0.7 %fusion.1 = bf16[1,128,768]{2,1,0:T(8,128)(2,1)} fusion(bf16[128,768]{1,0:T(8,128)(2,1)S(1)} %collective-permute-done.2, bf16[128,768]{1,0:T(8,128)(2,1)S(1)} %collective-permute-done.1), kind=kLoop, calls=%fused_computation.4 | loop fusion | flops 393216 | bytes 589824 | tf_op jit(solution)/shard_map/broadcast_in_dim | solution.py:328
  69.5 1.8 %collective-permute-done.3 = bf16[128,256]{1,0:T(8,128)(2,1)S(1)} collective-permute-done((bf16[128,256]{1,0:T(8,128)(2,1)S(1)}, bf16[128,256]{1,0:T(8,128)(2,1)S(1)}, u32[]{:S(2)}, u32[]{:S(2)}) %collective-permute-start.3) | collective-permute-done | bytes 65568 | tf_op jit(solution)/shard_map/ppermute | solution.py:226
  71.4 0.6 slice_bitcast_fusion.2
  (2 shorter events, 0.1 us)
Async XLA Ops:
  2.2 7.2 %copy-start.2 = (bf16[1,128,768]{2,1,0:T(8,128)(2,1)S(1)}, bf16[1,128,768]{2,1,0:T(8,128)(2,1)}, u32[]{:S(2)}) copy-start(bf16[1,128,768]{2,1,0:T(8,128)(2,1)} %param.9) | copy-start | bytes 589828
  2.2 7.2 %copy-start.3 = (bf16[1,128,768]{2,1,0:T(8,128)(2,1)S(1)}, bf16[1,128,768]{2,1,0:T(8,128)(2,1)}, u32[]{:S(2)}) copy-start(bf16[1,128,768]{2,1,0:T(8,128)(2,1)} %param.6) | copy-start | bytes 589828
  2.2 24.7 %all-to-all-start = ((bf16[8,128,256]{2,1,0:T(8,128)(2,1)}), bf16[8,128,256]{2,1,0:T(8,128)(2,1)S(1)}, u32[]{:S(2)}, u32[]{:S(2)}) async-start(bf16[8,128,256]{2,1,0:T(8,128)(2,1)} %broadcast_in_dim.15), calls=%async_computation | async-start | bytes 1048576 | tf_op jit(solution)/shard_map/all_to_all | solution.py:307
  9.5 12.5 %collective-permute-start = (bf16[128,1536]{1,0:T(8,128)(2,1)S(1)}, bf16[128,1536]{1,0:T(8,128)(2,1)S(1)}, u32[]{:S(2)}, u32[]{:S(2)}) collective-permute-start(bf16[128,1536]{1,0:T(8,128)(2,1)S(1)} %pad_maximum_fusion), channel_id=1, source_target_pairs={{0,2},{2,0},{1,3},{3,1},{4,6},{6,4},{5,7},{7,5},{8,10},{10,8},{9,1... | collective-permute-start | bytes 1179656 | tf_op jit(solution)/shard_map/ppermute | solution.py:226
  12.4 2.5 %copy-start = (s32[1,4096]{1,0:T(1,128)S(1)}, s32[1,4096]{1,0:T(1,128)}, u32[]{:S(2)}) copy-start(s32[1,4096]{1,0:T(1,128)} %episode_ref.1) | copy-start | bytes 49156
  12.4 2.5 %copy-start.1 = (s32[64]{0:T(128)S(1)}, s32[64]{0:T(128)}, u32[]{:S(2)}) copy-start(s32[64]{0:T(128)} %order_ref.1) | copy-start | bytes 772
  41.3 22.3 %all-to-all-start.1 = ((bf16[8,128,256]{2,1,0:T(8,128)(2,1)}), bf16[8,128,256]{2,1,0:T(8,128)(2,1)S(1)}, u32[]{:S(2)}, u32[]{:S(2)}) async-start(bf16[8,128,256]{2,1,0:T(8,128)(2,1)} %bitcast.14), calls=%async_computation.1 | async-start | bytes 1048576 | tf_op jit(solution)/shard_map/all_to_all | solution.py:318
  54.0 12.4 %collective-permute-start.1 = (bf16[128,768]{1,0:T(8,128)(2,1)S(1)}, bf16[128,768]{1,0:T(8,128)(2,1)S(1)}, u32[]{:S(2)}, u32[]{:S(2)}) collective-permute-start(bf16[128,768]{1,0:T(8,128)(2,1)S(1)} %get-tuple-element.23), channel_id=1, source_target_pairs={{0,256},{256,0},{1,257},{257,1},{2,258},{258,2},{3,259},{259,3},{4... | collective-permute-start | bytes 589832 | tf_op jit(solution)/shard_map/ppermute | solution.py:226
  55.9 12.9 %collective-permute-start.2 = (bf16[128,768]{1,0:T(8,128)(2,1)S(1)}, bf16[128,768]{1,0:T(8,128)(2,1)S(1)}, u32[]{:S(2)}, u32[]{:S(2)}) collective-permute-start(bf16[128,768]{1,0:T(8,128)(2,1)S(1)} %get-tuple-element.24), channel_id=1, source_target_pairs={{0,258},{2,256},{256,2},{258,0},{1,259},{3,257},{257,3},{259,1},{4... | collective-permute-start | bytes 589832 | tf_op jit(solution)/shard_map/ppermute | solution.py:324
  63.7 7.7 %collective-permute-start.3 = (bf16[128,256]{1,0:T(8,128)(2,1)S(1)}, bf16[128,256]{1,0:T(8,128)(2,1)S(1)}, u32[]{:S(2)}, u32[]{:S(2)}) collective-permute-start(bf16[128,256]{1,0:T(8,128)(2,1)S(1)} %reduce_sum.12), channel_id=1, source_target_pairs={{0,256},{256,0},{1,257},{257,1},{2,258},{258,2},{3,259},{259,3},{4... | collective-permute-start | bytes 196616 | tf_op jit(solution)/shard_map/ppermute | solution.py:226

commit v4 on v3

--- a/solution.py
+++ b/solution.py
@@ -15,7 +15,7 @@
 SLOTS = 8
 KEYS = 16
 GROUP = 4
-UNROLL = 4
+UNROLLS = (8, 4, 2, 1)
 CHUNKS = KEYS // GROUP
 STEPS = SLOTS * CHUNKS + CHUNKS
 SCALING = HEAD ** (-0.5)
@@ -61,7 +61,7 @@
         first = start_of(starts, base)
         at = step * GROUP
         for k in range(KEYS):
-            table_ref[SPANS + at] = k
+            table_ref[SPANS + at] = (k // 2) * 4 + k % 2
             table_ref[PLACES + at] = key_bases[k]
             seen = (key_bases[k] <= base) & (key_bases[k] + (SPAN - 1) >= first)
             at = at + seen.astype(jnp.int32)
@@ -88,11 +88,16 @@
                 ]
 
 
+def load_keys(table_ref, kv_ref, step):
+    spans = [table_ref[SPANS + step * GROUP + i] for i in range(GROUP)]
+    keys = jnp.concatenate([kv_ref[s] for s in spans], axis=0)
+    values = jnp.concatenate([kv_ref[s + 2] for s in spans], axis=0)
+    return spans, keys, values
+
+
 def load_step(table_ref, kv_ref, q_ref, g_ref, step):
     slot, base = table_ref[SLOT + step], table_ref[BASE + step]
-    spans = [table_ref[SPANS + step * GROUP + i] for i in range(GROUP)]
-    keys = jnp.concatenate([kv_ref[s, :, :HEAD] for s in spans], axis=0)
-    values = jnp.concatenate([kv_ref[s, :, HEAD:] for s in spans], axis=0)
+    spans, keys, values = load_keys(table_ref, kv_ref, step)
     iota = lax.broadcasted_iota(jnp.int32, (SPAN, HEAD), 0)
     pos = jnp.concatenate(
         [table_ref[PLACES + step * GROUP + i] + iota for i in range(GROUP)], axis=0
@@ -113,15 +118,17 @@
 
 
 def run_steps(table_ref, one_step):
-    def some(n, unused):
-        for u in range(UNROLL):
-            one_step(n * UNROLL + u)
-        return unused
-
-    count = table_ref[0]
-    whole = count // UNROLL
-    lax.fori_loop(0, whole, some, 0)
-    lax.fori_loop(whole * UNROLL, count, lambda step, unused: (one_step(step), unused)[1], 0)
+    at, count = jnp.int32(0), table_ref[0]
+    for steps in UNROLLS:
+
+        def some(n, unused, at=at, steps=steps):
+            for i in range(steps):
+                one_step(at + n * steps + i)
+            return unused
+
+        turns = (count - at) // steps
+        lax.fori_loop(0, turns, some, 0)
+        at = at + turns * steps
 
 
 def stats_kernel(
@@ -189,24 +196,54 @@
         dk = dot(score_grad, query, NN)
         dv = dot(probs.astype(jnp.bfloat16), grad, NN)
         for n in range(GROUP):
-            acc_ref[spans[n], :, :HEAD] += dk[n * SPAN : (n + 1) * SPAN]
-            acc_ref[spans[n], :, HEAD:] += dv[n * SPAN : (n + 1) * SPAN]
+            acc_ref[spans[n]] += dk[n * SPAN : (n + 1) * SPAN]
+            acc_ref[spans[n] + 2] += dv[n * SPAN : (n + 1) * SPAN]
 
     run_steps(table_ref, one_step)
-    dkv_ref[:, :, :HEAD] = (acc_ref[:, :, :HEAD] * SCALING).astype(jnp.bfloat16)
-    dkv_ref[:, :, HEAD:] = acc_ref[:, :, HEAD:].astype(jnp.bfloat16)
+    for n in range(2 * KEYS):
+        scaling = SCALING if n % 4 < 2 else 1.0
+        dkv_ref[n] = (acc_ref[n] * scaling).astype(jnp.bfloat16)
 
 
 def query_kernel(
-    place_ref, table_ref, kv_ref, q_ref, g_ref, rows_ref, after_ref, keep_ref, send_ref, acc_ref
+    place_ref,
+    table_ref,
+    kv_ref,
+    q_ref,
+    g_ref,
+    rows_ref,
+    after_ref,
+    keep_ref,
+    send_ref,
+    acc_ref,
+    log_ref,
+    delta_ref,
 ):
     acc_ref[...] = jnp.zeros_like(acc_ref)
+    for slot in range(SLOTS):
+        log_ref[slot] = jnp.broadcast_to(rows_ref[slot : slot + 1], (HEAD, ROWS)).T
+        delta_ref[slot] = jnp.broadcast_to(rows_ref[8 + slot : 9 + slot], (HEAD, ROWS)).T
 
     def one_step(step):
-        slot, spans, keys, query, grad, probs, score_grad = step_gradients(
-            table_ref, kv_ref, q_ref, g_ref, rows_ref, step
-        )
-        acc_ref[slot] += dot(keys.T, score_grad, NN)
+        slot, base = table_ref[SLOT + step], table_ref[BASE + step]
+        spans, keys, values = load_keys(table_ref, kv_ref, step)
+        query_pos = base + lax.broadcasted_iota(jnp.int32, (SPAN, HEAD), 0)
+        first = start_of([table_ref[1 + n] for n in range(3)], query_pos)
+        lane = lax.broadcasted_iota(jnp.int32, (1, HEAD), 1)
+        raw = dot(q_ref[slot], keys, NT)
+        products = dot(g_ref[slot], values, NT)
+        log_total, delta = log_ref[slot], delta_ref[slot]
+        parts = []
+        for n in range(GROUP // 2):
+            low, high = (table_ref[PLACES + step * GROUP + 2 * n + i] for i in range(2))
+            pos = jnp.where(lane < SPAN, low, high) + lane % SPAN
+            visible = (pos <= query_pos) & (pos >= first)
+            cols = slice(n * HEAD, (n + 1) * HEAD)
+            scores = raw[:, cols].reshape(HEADS, SPAN, HEAD) * (SCALING * LOG2E)
+            scores = jnp.where(visible[None], scores, NEG_FILL).reshape(ROWS, HEAD)
+            probs = jnp.exp2(scores - log_total)
+            parts.append((probs * (products[:, cols] - delta)).astype(jnp.bfloat16))
+        acc_ref[slot] += dot(jnp.concatenate(parts, axis=1), keys, NN)
 
     run_steps(table_ref, one_step)
     xl, core = place_ref[1], place_ref[2]
@@ -214,12 +251,12 @@
         chip = xl if rel == 0 else 1 - xl
         for half in range(2):
             rows = slice(half * SPAN, (half + 1) * SPAN)
-            mine = acc_ref[chip * 4 + core * 2 + half].T * SCALING
-            theirs = acc_ref[chip * 4 + (1 - core) * 2 + half].T * SCALING
+            mine = chip * 4 + core * 2 + half
+            theirs = chip * 4 + (1 - core) * 2 + half
             for h in range(HEADS):
                 cols, at = slice(h * HEAD, (h + 1) * HEAD), slice(h * SPAN, (h + 1) * SPAN)
-                keep_ref[rel, rows, cols] = mine[at]
-                send_ref[rel, rows, cols] = theirs[at].astype(jnp.bfloat16)
+                keep_ref[rel, rows, cols] = acc_ref[mine, at, :] * SCALING
+                send_ref[rel, rows, cols] = (acc_ref[theirs, at, :] * SCALING).astype(jnp.bfloat16)
 
 
 def swap(block, axis):
@@ -243,6 +280,7 @@
 VMEM = pl.BlockSpec(memory_space=pltpu.VMEM)
 
 
+KEYS_VALUES = (2 * KEYS, SPAN, HEAD)
 LAID_OUT = jax.ShapeDtypeStruct((SLOTS, ROWS, HEAD), jnp.bfloat16)
 
 
@@ -273,12 +311,12 @@
         key_value_kernel,
         "key_value_gradients",
         (
-            jax.ShapeDtypeStruct((KEYS, SPAN, 2 * HEAD), jnp.bfloat16),
+            jax.ShapeDtypeStruct(KEYS_VALUES, jnp.bfloat16),
             jax.ShapeDtypeStruct((16, ROWS), jnp.float32),
         ),
         [SMEM, VMEM, VMEM, VMEM, VMEM],
         (VMEM, VMEM),
-        [pltpu.VMEM((KEYS, SPAN, 2 * HEAD), jnp.float32)],
+        [pltpu.VMEM(KEYS_VALUES, jnp.float32)],
     )(table, kv_all, q, g, stats_all)
 
 
@@ -293,7 +331,7 @@
         ),
         [SMEM, SMEM, VMEM, VMEM, VMEM, VMEM, pl.BlockSpec(memory_space=pl.ANY)],
         (VMEM, VMEM),
-        [pltpu.VMEM((SLOTS, HEAD, ROWS), jnp.float32)],
+        [pltpu.VMEM((SLOTS, ROWS, HEAD), jnp.float32)] * 3,
     )(place, table, kv_all, q, g, rows, after)
 
 
@@ -303,10 +341,9 @@
     place = jnp.stack([lax.axis_index("y"), lax.axis_index("xl"), lax.axis_index("core")]).astype(
         jnp.int32
     )
-    kv = jnp.concatenate([key_rows[0], stored_value_rows[0]], axis=1)
-    kv_all = lax.all_to_all(
-        jnp.broadcast_to(kv[None], (ring, tokens, 2 * HEAD)), "y", 0, 0, tiled=True
-    ).reshape(KEYS, SPAN, 2 * HEAD)
+    part = lax.broadcasted_iota(jnp.int32, (ring, 2, tokens, HEAD), 1)
+    kv = jnp.where(part == 0, key_rows[None], stored_value_rows[None])
+    kv_all = lax.all_to_all(kv, "y", 0, 0, tiled=True).reshape(KEYS_VALUES)
     both = jnp.concatenate([query_rows[0], output_grad[0]], axis=1)
     remote = swap(both, "xl")
     own = lax.all_gather(both, "core", axis=0, tiled=True)
@@ -315,7 +352,7 @@
     q, g, stats = row_stats(place, table, kv_all, other, q, g)
     stats_all = lax.all_gather(stats, ("xl", "core"), axis=0)
     dkv, rows = key_value_gradients(table, kv_all, q, g, stats_all)
-    dkv_parts = lax.all_to_all(dkv.reshape(ring, tokens, 2 * HEAD), "y", 0, 0, tiled=True)
+    dkv_parts = lax.all_to_all(dkv.reshape(ring, 2 * tokens, HEAD), "y", 0, 0, tiled=True)
     keep, send = query_gradients(place, table, kv_all, q, g, rows, dkv)
     sent = lax.all_gather(send, "core", axis=0)
     dq = keep + lax.dynamic_index_in_dim(sent, 1 - place[2], 0, False).astype(jnp.float32)
@@ -325,7 +362,7 @@
     dq_back = (straight.astype(jnp.float32) + across.astype(jnp.float32)).astype(jnp.bfloat16)
     dkv_sum = jnp.sum(dkv_parts.astype(jnp.float32), axis=0).astype(jnp.bfloat16)
     dkv_back = swap(dkv_sum, "section")
-    return (dq_back[None], dkv_back[None, :, :HEAD], dkv_back[None, :, HEAD:])
+    return (dq_back[None], dkv_back[None, :tokens], dkv_back[None, tokens:])
 
 
 def solution(mesh):

time: 72.5 us -> 72.3 us (level)
  the two profiles are of different devices: /device:TPU:6 before, /device:TPU:450 now
where the time goes in v4:
time: 72.3 us; the launch traced here: 71.8 us
  starting transfers between devices  23.2 us (32%)
  waiting for transfers between devices  17.4 us (24%)
  blocking collectives  13.6 us (19%)
  Pallas kernels  13.5 us (19%)
  other arithmetic  2.66 us (4%)
  between operations  0.75 us (1%)
    ppermute x3, waiting for transfers between devices, swap(): return lax.ppermute(block, axis, [(0, 1), (1, 0)])  8.72 us
    ppermute x3, starting transfers between devices, swap(): return lax.ppermute(block, axis, [(0, 1), (1, 0)])  8.32 us
    all_to_all x1, starting transfers between devices, per_device(): kv_all = lax.all_to_all(kv, 'y', 0, 0, tiled=True).reshape(KEYS_VALUES)  7.23 us
    all_gather x1, blocking collectives, per_device(): stats_all = lax.all_gather(stats, ('xl', 'core'), axis=0)  5.47 us
    all_to_all x1, waiting for transfers between devices, per_device(): lax.all_to_all(dkv.reshape(ring, 2 * tokens, HEAD), 'y', 0, 0, tiled=True)  5.41 us
    all_to_all x1, starting transfers between devices, per_device(): lax.all_to_all(dkv.reshape(ring, 2 * tokens, HEAD), 'y', 0, 0, tiled=True)  4.91 us
    pallas_call x1, Pallas kernels, key_value_gradients(): call(key_value_kernel, 'key_value_gradients', (jax.ShapeDtypeStruct(KEYS_...  4.56 us
    pallas_call x1, Pallas kernels, query_gradients(): call(query_kernel, 'query_gradients', (jax.ShapeDtypeStruct(shape, jnp.fl...  4.26 us
  transfers between devices with their start and end apart: 6, of which 5 were waited for; matrix products, arithmetic and copies ran while one was open for 1% of the time, Pallas kernels for 9%

profile of v4, /device:TPU:450, one launch (start us, length us, event | category | flops | bytes accessed | tf_op | source)
XLA Modules:
  0.0 71.8 jit_solution(5342573520253190240)
XLA Ops:
  0.6 1.7 %broadcast_select_fusion = bf16[8,2,128,128]{3,2,1,0:T(8,128)(2,1)} fusion(pred[2]{0:T(512)(128)(4,1)S(1)} %iota_compare_fusion, bf16[128,128]{1,0:T(8,128)(2,1)} %bitcast.31, bf16[128,128]{1,0:T(8,128)(2,1)} %bitcast.32), kind=kLoop, calls=%fused_computation.2 | loop fusion | flops 262144 | bytes 589826 | tf_op jit(solution)/shard_map/jit(_where)/select_n | solution.py:345
  2.3 0.0 copy-start.2
  2.3 0.0 copy-start.3
  2.3 7.2 %all-to-all-start = ((bf16[8,2,128,128]{3,2,1,0:T(8,128)(2,1)}), bf16[8,2,128,128]{3,2,1,0:T(8,128)(2,1)S(1)}, u32[]{:S(2)}, u32[]{:S(2)}) async-start(bf16[8,2,128,128]{3,2,1,0:T(8,128)(2,1)} %broadcast_select_fusion), calls=%async_computation | async-start | bytes 1048576 | tf_op jit(solution)/shard_map/all_to_all | solution.py:346
  9.6 0.0 copy-done.2
  9.6 0.0 copy-done.3
  9.6 2.4 %collective-permute-start = (bf16[128,1536]{1,0:T(8,128)(2,1)S(1)}, bf16[128,1536]{1,0:T(8,128)(2,1)S(1)}, u32[]{:S(2)}, u32[]{:S(2)}) collective-permute-start(bf16[128,1536]{1,0:T(8,128)(2,1)S(1)} %pad_maximum_fusion), channel_id=1, source_target_pairs={{0,2},{2,0},{1,3},{3,1},{4,6},{6,4},{5,7},{7,5},{8,10},{10,8},{9,1... | collective-permute-start | bytes 1179656 | tf_op jit(solution)/shard_map/ppermute | solution.py:263
  12.1 0.1 pad_add_fusion.place_ref
  12.1 0.0 copy-start
  12.1 0.0 copy-start.1
  12.1 2.5 %all_gather.18.own_ref = bf16[256,1536]{1,0:T(8,128)(2,1)S(1)} all-gather(bf16[128,1536]{1,0:T(8,128)(2,1)S(1)} %pad_maximum_fusion), channel_id=1, replica_groups=mesh['section'=2,'tp'=8,'y'=8,'xl'=2,'core'=2] {'core'}, dimensions={0}, use_global_device_ids=true | all-gather | bytes 1179648 | tf_op jit(solution)/shard_map/all_gather | solution.py:349
  14.6 0.0 copy-done
  14.6 0.0 copy-done.1
  14.6 2.2 %prepare.1 = (s32[412]{0:T(512)S(1)}, bf16[8,384,128]{2,1,0:T(8,128)(2,1)S(1)}, bf16[8,384,128]{2,1,0:T(8,128)(2,1)S(1)}) custom-call(s32[64]{0:T(128)S(1)} %copy-done.1, s32[3]{0:T(128)S(1)} %pad_add_fusion.place_ref, s32[1,4096]{1,0:T(1,128)S(1)} %copy-done, bf16[256,1536]{1,0:T(8,128)(2,1)S(1)} %all_gather.18.own_ref), custom_call_target="tpu_custom_call" | custom-call | tf_op jit(solution)/shard_map/prepare/pallas_call | solution.py:288
  16.8 5.3 %collective-permute-done = bf16[128,1536]{1,0:T(8,128)(2,1)S(1)} collective-permute-done((bf16[128,1536]{1,0:T(8,128)(2,1)S(1)}, bf16[128,1536]{1,0:T(8,128)(2,1)S(1)}, u32[]{:S(2)}, u32[]{:S(2)}) %collective-permute-start) | collective-permute-done | bytes 393248 | tf_op jit(solution)/shard_map/ppermute | solution.py:263
  22.1 2.4 %all_gather.19.other_ref = bf16[256,1536]{1,0:T(8,128)(2,1)S(1)} all-gather(bf16[128,1536]{1,0:T(8,128)(2,1)S(1)} %collective-permute-done), channel_id=1, replica_groups=mesh['section'=2,'tp'=8,'y'=8,'xl'=2,'core'=2] {'core'}, dimensions={0}, use_global_device_ids=true | all-gather | bytes 1179648 | tf_op jit(solution)/shard_map/all_gather | solution.py:350
  24.4 2.6 %all-to-all-done = bf16[8,2,128,128]{3,2,1,0:T(8,128)(2,1)S(1)} async-done(((bf16[8,2,128,128]{3,2,1,0:T(8,128)(2,1)}), bf16[8,2,128,128]{3,2,1,0:T(8,128)(2,1)S(1)}, u32[]{:S(2)}, u32[]{:S(2)}) %all-to-all-start) | async-done | bytes 524320 | tf_op jit(solution)/shard_map/all_to_all | solution.py:346
  27.0 2.5 %row_stats.1 = (bf16[8,384,128]{2,1,0:T(8,128)(2,1)S(1)}, bf16[8,384,128]{2,1,0:T(8,128)(2,1)S(1)}, f32[24,384]{1,0:T(8,128)S(1)}) custom-call(s32[3]{0:T(128)S(1)} %pad_add_fusion.place_ref, s32[412]{0:T(512)S(1)} %get-tuple-element.13.table_ref, bf16[32,64,128]{2,1,0:T(8,128)(2,1)S(1)} %bitcast.24, ...), custom_call_target="tpu_custom_call", output_to_operand_aliasing={{0}: (4, {}), {1}: (5, {})} | custom-call | tf_op jit(solution)/shard_map/row_stats/pallas_call | solution.py:298
  29.5 5.5 %all-gather = f32[96,384]{1,0:T(8,128)S(1)} all-gather(f32[24,384]{1,0:T(8,128)S(1)} %get-tuple-element.18), channel_id=2, replica_groups=mesh['section'=2,'tp'=8,'y'=8,'xl'=2,'core'=2] {'xl','core'}, dimensions={0}, use_global_device_ids=true | all-gather | bytes 184320 | tf_op jit(solution)/shard_map/all_gather | solution.py:353
  35.0 4.6 %key_value_gradients.1 = (bf16[32,64,128]{2,1,0:T(8,128)(2,1)}, f32[16,384]{1,0:T(8,128)S(1)}) custom-call(s32[412]{0:T(512)S(1)} %get-tuple-element.13.table_ref, bf16[32,64,128]{2,1,0:T(8,128)(2,1)S(1)} %bitcast.25, bf16[8,384,128]{2,1,0:T(8,128)(2,1)S(1)} %get-tuple-element.16.q_ref, bf16[8,384,128]{2,1,0:T(8,128)(2,1)S(1)} %get-tuple-element.17.g_ref, ...), custom_call_target="tpu_custom_call" | custom-call | tf_op jit(solution)/shard_map/key_value_gradients/pallas_call | solution.py:310
  39.5 4.9 %all-to-all-start.1 = ((bf16[8,256,128]{2,1,0:T(8,128)(2,1)}), bf16[8,256,128]{2,1,0:T(8,128)(2,1)S(1)}, u32[]{:S(2)}, u32[]{:S(2)}) async-start(bf16[8,256,128]{2,1,0:T(8,128)(2,1)} %bitcast.14), calls=%async_computation.1 | async-start | bytes 1048576 | tf_op jit(solution)/shard_map/all_to_all | solution.py:355
  44.5 4.3 %query_gradients.1 = (f32[2,128,768]{2,1,0:T(8,128)S(1)}, bf16[2,128,768]{2,1,0:T(8,128)(2,1)S(1)}) custom-call(s32[3]{0:T(128)S(1)} %pad_add_fusion.place_ref, s32[412]{0:T(512)S(1)} %get-tuple-element.13.table_ref, bf16[32,64,128]{2,1,0:T(8,128)(2,1)S(1)} %bitcast.26, bf16[8,384,128]{2,1,0:T(8,128)(2,1)S(1)} %get-tuple-element.16.q_ref, ...), custom_call_target="tpu_custom_call" | custom-call | tf_op jit(solution)/shard_map/query_gradients/pallas_call | solution.py:325
  48.7 3.3 %all-gather.1 = bf16[4,128,768]{2,1,0:T(8,128)(2,1)S(1)} all-gather(bf16[2,128,768]{2,1,0:T(8,128)(2,1)S(1)} %get-tuple-element.22), channel_id=3, replica_groups=mesh['section'=2,'tp'=8,'y'=8,'xl'=2,'core'=2] {'core'}, dimensions={0}, use_global_device_ids=true | all-gather | bytes 1179648 | tf_op jit(solution)/shard_map/all_gather | solution.py:357
  52.0 0.1 fusion
  52.2 3.1 %collective-permute-start.1 = (bf16[128,768]{1,0:T(8,128)(2,1)S(1)}, bf16[128,768]{1,0:T(8,128)(2,1)S(1)}, u32[]{:S(2)}, u32[]{:S(2)}) collective-permute-start(bf16[128,768]{1,0:T(8,128)(2,1)S(1)} %get-tuple-element.23), channel_id=1, source_target_pairs={{0,256},{256,0},{1,257},{257,1},{2,258},{258,2},{3,259},{259,3},{4... | collective-permute-start | bytes 589832 | tf_op jit(solution)/shard_map/ppermute | solution.py:263
  55.3 2.7 %collective-permute-start.2 = (bf16[128,768]{1,0:T(8,128)(2,1)S(1)}, bf16[128,768]{1,0:T(8,128)(2,1)S(1)}, u32[]{:S(2)}, u32[]{:S(2)}) collective-permute-start(bf16[128,768]{1,0:T(8,128)(2,1)S(1)} %get-tuple-element.24), channel_id=1, source_target_pairs={{0,258},{2,256},{256,2},{258,0},{1,259},{3,257},{257,3},{259,1},{4... | collective-permute-start | bytes 589832 | tf_op jit(solution)/shard_map/ppermute | solution.py:361
  58.0 5.4 %all-to-all-done.1 = bf16[8,256,128]{2,1,0:T(8,128)(2,1)S(1)} async-done(((bf16[8,256,128]{2,1,0:T(8,128)(2,1)}), bf16[8,256,128]{2,1,0:T(8,128)(2,1)S(1)}, u32[]{:S(2)}, u32[]{:S(2)}) %all-to-all-start.1) | async-done | bytes 524320 | tf_op jit(solution)/shard_map/all_to_all | solution.py:355
  63.4 0.1 reduce_sum.12
  63.5 2.8 %collective-permute-start.3 = (bf16[256,128]{1,0:T(8,128)(2,1)S(1)}, bf16[256,128]{1,0:T(8,128)(2,1)S(1)}, u32[]{:S(2)}, u32[]{:S(2)}) collective-permute-start(bf16[256,128]{1,0:T(8,128)(2,1)S(1)} %reduce_sum.12), channel_id=1, source_target_pairs={{0,256},{256,0},{1,257},{257,1},{2,258},{258,2},{3,259},{259,3},{4... | collective-permute-start | bytes 196616 | tf_op jit(solution)/shard_map/ppermute | solution.py:263
  66.3 0.0 collective-permute-done.1
  66.3 0.7 collective-permute-done.2
  67.0 0.7 %fusion.1 = bf16[1,128,768]{2,1,0:T(8,128)(2,1)} fusion(bf16[128,768]{1,0:T(8,128)(2,1)S(1)} %collective-permute-done.2, bf16[128,768]{1,0:T(8,128)(2,1)S(1)} %collective-permute-done.1), kind=kLoop, calls=%fused_computation.5 | loop fusion | flops 393216 | bytes 589824 | tf_op jit(solution)/shard_map/broadcast_in_dim | solution.py:365
  67.7 3.5 %collective-permute-done.3 = bf16[256,128]{1,0:T(8,128)(2,1)S(1)} collective-permute-done((bf16[256,128]{1,0:T(8,128)(2,1)S(1)}, bf16[256,128]{1,0:T(8,128)(2,1)S(1)}, u32[]{:S(2)}, u32[]{:S(2)}) %collective-permute-start.3) | collective-permute-done | bytes 65568 | tf_op jit(solution)/shard_map/ppermute | solution.py:263
  71.1 0.6 slice_bitcast_fusion.2
  (3 shorter events, 0.1 us)
Async XLA Ops:
  2.3 7.2 %copy-start.2 = (bf16[1,128,768]{2,1,0:T(8,128)(2,1)S(1)}, bf16[1,128,768]{2,1,0:T(8,128)(2,1)}, u32[]{:S(2)}) copy-start(bf16[1,128,768]{2,1,0:T(8,128)(2,1)} %param.9) | copy-start | bytes 589828
  2.3 7.2 %copy-start.3 = (bf16[1,128,768]{2,1,0:T(8,128)(2,1)S(1)}, bf16[1,128,768]{2,1,0:T(8,128)(2,1)}, u32[]{:S(2)}) copy-start(bf16[1,128,768]{2,1,0:T(8,128)(2,1)} %param.6) | copy-start | bytes 589828
  2.3 24.7 %all-to-all-start = ((bf16[8,2,128,128]{3,2,1,0:T(8,128)(2,1)}), bf16[8,2,128,128]{3,2,1,0:T(8,128)(2,1)S(1)}, u32[]{:S(2)}, u32[]{:S(2)}) async-start(bf16[8,2,128,128]{3,2,1,0:T(8,128)(2,1)} %broadcast_select_fusion), calls=%async_computation | async-start | bytes 1048576 | tf_op jit(solution)/shard_map/all_to_all | solution.py:346
  9.6 12.5 %collective-permute-start = (bf16[128,1536]{1,0:T(8,128)(2,1)S(1)}, bf16[128,1536]{1,0:T(8,128)(2,1)S(1)}, u32[]{:S(2)}, u32[]{:S(2)}) collective-permute-start(bf16[128,1536]{1,0:T(8,128)(2,1)S(1)} %pad_maximum_fusion), channel_id=1, source_target_pairs={{0,2},{2,0},{1,3},{3,1},{4,6},{6,4},{5,7},{7,5},{8,10},{10,8},{9,1... | collective-permute-start | bytes 1179656 | tf_op jit(solution)/shard_map/ppermute | solution.py:263
  12.1 2.5 %copy-start = (s32[1,4096]{1,0:T(1,128)S(1)}, s32[1,4096]{1,0:T(1,128)}, u32[]{:S(2)}) copy-start(s32[1,4096]{1,0:T(1,128)} %episode_ref.1) | copy-start | bytes 49156
  12.1 2.5 %copy-start.1 = (s32[64]{0:T(128)S(1)}, s32[64]{0:T(128)}, u32[]{:S(2)}) copy-start(s32[64]{0:T(128)} %order_ref.1) | copy-start | bytes 772
  39.5 23.9 %all-to-all-start.1 = ((bf16[8,256,128]{2,1,0:T(8,128)(2,1)}), bf16[8,256,128]{2,1,0:T(8,128)(2,1)S(1)}, u32[]{:S(2)}, u32[]{:S(2)}) async-start(bf16[8,256,128]{2,1,0:T(8,128)(2,1)} %bitcast.14), calls=%async_computation.1 | async-start | bytes 1048576 | tf_op jit(solution)/shard_map/all_to_all | solution.py:355
  52.2 14.1 %collective-permute-start.1 = (bf16[128,768]{1,0:T(8,128)(2,1)S(1)}, bf16[128,768]{1,0:T(8,128)(2,1)S(1)}, u32[]{:S(2)}, u32[]{:S(2)}) collective-permute-start(bf16[128,768]{1,0:T(8,128)(2,1)S(1)} %get-tuple-element.23), channel_id=1, source_target_pairs={{0,256},{256,0},{1,257},{257,1},{2,258},{258,2},{3,259},{259,3},{4... | collective-permute-start | bytes 589832 | tf_op jit(solution)/shard_map/ppermute | solution.py:263
  55.3 11.7 %collective-permute-start.2 = (bf16[128,768]{1,0:T(8,128)(2,1)S(1)}, bf16[128,768]{1,0:T(8,128)(2,1)S(1)}, u32[]{:S(2)}, u32[]{:S(2)}) collective-permute-start(bf16[128,768]{1,0:T(8,128)(2,1)S(1)} %get-tuple-element.24), channel_id=1, source_target_pairs={{0,258},{2,256},{256,2},{258,0},{1,259},{3,257},{257,3},{259,1},{4... | collective-permute-start | bytes 589832 | tf_op jit(solution)/shard_map/ppermute | solution.py:361
  63.5 7.7 %collective-permute-start.3 = (bf16[256,128]{1,0:T(8,128)(2,1)S(1)}, bf16[256,128]{1,0:T(8,128)(2,1)S(1)}, u32[]{:S(2)}, u32[]{:S(2)}) collective-permute-start(bf16[256,128]{1,0:T(8,128)(2,1)S(1)} %reduce_sum.12), channel_id=1, source_target_pairs={{0,256},{256,0},{1,257},{257,1},{2,258},{258,2},{3,259},{259,3},{4... | collective-permute-start | bytes 196616 | tf_op jit(solution)/shard_map/ppermute | solution.py:263

commit v5 on v4

--- a/solution.py
+++ b/solution.py
@@ -357,12 +357,17 @@
     sent = lax.all_gather(send, "core", axis=0)
     dq = keep + lax.dynamic_index_in_dim(sent, 1 - place[2], 0, False).astype(jnp.float32)
     parts = dq.astype(jnp.bfloat16)
+    across = lax.ppermute(parts[1], ("section", "xl"), [(0, 3), (1, 2), (2, 1), (3, 0)])
     straight = swap(parts[0], "section")
-    across = lax.ppermute(parts[1], ("section", "xl"), [(0, 3), (1, 2), (2, 1), (3, 0)])
+    dkv_sum = jnp.sum(dkv_parts.astype(jnp.float32), axis=0).astype(jnp.bfloat16)
+    both_dkv = lax.all_gather(dkv_sum, "section", axis=0)
+    dkv_back = lax.dynamic_slice_in_dim(both_dkv, 1 - lax.axis_index("section"), 1, 0)
+    dk_back, dv_back = dkv_back[:, :tokens], dkv_back[:, tokens:]
+    straight, across, dk_back, dv_back = lax.optimization_barrier(
+        (straight, across, dk_back, dv_back)
+    )
     dq_back = (straight.astype(jnp.float32) + across.astype(jnp.float32)).astype(jnp.bfloat16)
-    dkv_sum = jnp.sum(dkv_parts.astype(jnp.float32), axis=0).astype(jnp.bfloat16)
-    dkv_back = swap(dkv_sum, "section")
-    return (dq_back[None], dkv_back[None, :tokens], dkv_back[None, tokens:])
+    return (dq_back[None], dk_back, dv_back)
 
 
 def solution(mesh):

time: 72.3 us -> 71.8 us (level)
  the two profiles are of different devices: /device:TPU:450 before, /device:TPU:6 now
where the time goes in v5:
time: 71.8 us; the launch traced here: 70.7 us
  starting transfers between devices  23.7 us (33%)
  blocking collectives  19.8 us (28%)
  Pallas kernels  14.1 us (20%)
  waiting for transfers between devices  9.05 us (13%)
  other arithmetic  2.67 us (4%)
  between operations  0.74 us (1%)
    ppermute x2, starting transfers between devices, swap(): return lax.ppermute(block, axis, [(0, 1), (1, 0)])  8.17 us
    all_to_all x1, starting transfers between devices, per_device(): kv_all = lax.all_to_all(kv, 'y', 0, 0, tiled=True).reshape(KEYS_VALUES)  7.23 us
    all_gather x1, blocking collectives, per_device(): both_dkv = lax.all_gather(dkv_sum, 'section', axis=0)  6.45 us
    all_gather x1, blocking collectives, per_device(): stats_all = lax.all_gather(stats, ('xl', 'core'), axis=0)  5.47 us
    ppermute x2, waiting for transfers between devices, swap(): return lax.ppermute(block, axis, [(0, 1), (1, 0)])  4.96 us
    pallas_call x1, Pallas kernels, key_value_gradients(): call(key_value_kernel, 'key_value_gradients', (jax.ShapeDtypeStruct(KEYS_...  4.85 us
    pallas_call x1, Pallas kernels, query_gradients(): call(query_kernel, 'query_gradients', (jax.ShapeDtypeStruct(shape, jnp.fl...  4.47 us
    all_to_all x1, starting transfers between devices, per_device(): lax.all_to_all(dkv.reshape(ring, 2 * tokens, HEAD), 'y', 0, 0, tiled=True)  4.31 us
  transfers between devices with their start and end apart: 5, of which 3 were waited for; matrix products, arithmetic and copies ran while one was open for 1% of the time, Pallas kernels for 9%

profile of v5, /device:TPU:6, one launch (start us, length us, event | category | flops | bytes accessed | tf_op | source)
XLA Modules:
  0.0 70.7 jit_solution(15537202343316183965)
XLA Ops:
  0.6 1.7 %broadcast_select_fusion = bf16[8,2,128,128]{3,2,1,0:T(8,128)(2,1)} fusion(pred[2]{0:T(512)(128)(4,1)S(1)} %iota_compare_fusion, bf16[128,128]{1,0:T(8,128)(2,1)} %bitcast.29, bf16[128,128]{1,0:T(8,128)(2,1)} %bitcast.30), kind=kLoop, calls=%fused_computation.2 | loop fusion | flops 262144 | bytes 589826 | tf_op jit(solution)/shard_map/jit(_where)/select_n | solution.py:345
  2.3 0.0 copy-start.2
  2.3 0.0 copy-start.3
  2.3 7.2 %all-to-all-start = ((bf16[8,2,128,128]{3,2,1,0:T(8,128)(2,1)}), bf16[8,2,128,128]{3,2,1,0:T(8,128)(2,1)S(1)}, u32[]{:S(2)}, u32[]{:S(2)}) async-start(bf16[8,2,128,128]{3,2,1,0:T(8,128)(2,1)} %broadcast_select_fusion), calls=%async_computation | async-start | bytes 1048576 | tf_op jit(solution)/shard_map/all_to_all | solution.py:346
  9.6 0.0 copy-done.2
  9.6 0.0 copy-done.3
  9.6 2.7 %collective-permute-start = (bf16[128,1536]{1,0:T(8,128)(2,1)S(1)}, bf16[128,1536]{1,0:T(8,128)(2,1)S(1)}, u32[]{:S(2)}, u32[]{:S(2)}) collective-permute-start(bf16[128,1536]{1,0:T(8,128)(2,1)S(1)} %pad_maximum_fusion), channel_id=1, source_target_pairs={{0,2},{2,0},{1,3},{3,1},{4,6},{6,4},{5,7},{7,5},{8,10},{10,8},{9,1... | collective-permute-start | bytes 1179656 | tf_op jit(solution)/shard_map/ppermute | solution.py:263
  12.4 0.1 pad_add_fusion.place_ref
  12.4 0.0 copy-start
  12.4 0.0 copy-start.1
  12.4 2.5 %all_gather.24.own_ref = bf16[256,1536]{1,0:T(8,128)(2,1)S(1)} all-gather(bf16[128,1536]{1,0:T(8,128)(2,1)S(1)} %pad_maximum_fusion), channel_id=1, replica_groups=mesh['section'=2,'tp'=8,'y'=8,'xl'=2,'core'=2] {'core'}, dimensions={0}, use_global_device_ids=true | all-gather | bytes 1179648 | tf_op jit(solution)/shard_map/all_gather | solution.py:349
  14.9 0.0 copy-done
  14.9 0.0 copy-done.1
  14.9 2.2 %prepare.1 = (s32[412]{0:T(512)S(1)}, bf16[8,384,128]{2,1,0:T(8,128)(2,1)S(1)}, bf16[8,384,128]{2,1,0:T(8,128)(2,1)S(1)}) custom-call(s32[64]{0:T(128)S(1)} %copy-done.1, s32[3]{0:T(128)S(1)} %pad_add_fusion.place_ref, s32[1,4096]{1,0:T(1,128)S(1)} %copy-done, bf16[256,1536]{1,0:T(8,128)(2,1)S(1)} %all_gather.24.own_ref), custom_call_target="tpu_custom_call" | custom-call | tf_op jit(solution)/shard_map/prepare/pallas_call | solution.py:288
  17.1 5.0 %collective-permute-done = bf16[128,1536]{1,0:T(8,128)(2,1)S(1)} collective-permute-done((bf16[128,1536]{1,0:T(8,128)(2,1)S(1)}, bf16[128,1536]{1,0:T(8,128)(2,1)S(1)}, u32[]{:S(2)}, u32[]{:S(2)}) %collective-permute-start) | collective-permute-done | bytes 393248 | tf_op jit(solution)/shard_map/ppermute | solution.py:263
  22.1 2.4 %all_gather.25.other_ref = bf16[256,1536]{1,0:T(8,128)(2,1)S(1)} all-gather(bf16[128,1536]{1,0:T(8,128)(2,1)S(1)} %collective-permute-done), channel_id=1, replica_groups=mesh['section'=2,'tp'=8,'y'=8,'xl'=2,'core'=2] {'core'}, dimensions={0}, use_global_device_ids=true | all-gather | bytes 1179648 | tf_op jit(solution)/shard_map/all_gather | solution.py:350
  24.4 2.6 %all-to-all-done = bf16[8,2,128,128]{3,2,1,0:T(8,128)(2,1)S(1)} async-done(((bf16[8,2,128,128]{3,2,1,0:T(8,128)(2,1)}), bf16[8,2,128,128]{3,2,1,0:T(8,128)(2,1)S(1)}, u32[]{:S(2)}, u32[]{:S(2)}) %all-to-all-start) | async-done | bytes 524320 | tf_op jit(solution)/shard_map/all_to_all | solution.py:346
  27.0 2.6 %row_stats.1 = (bf16[8,384,128]{2,1,0:T(8,128)(2,1)S(1)}, bf16[8,384,128]{2,1,0:T(8,128)(2,1)S(1)}, f32[24,384]{1,0:T(8,128)S(1)}) custom-call(s32[3]{0:T(128)S(1)} %pad_add_fusion.place_ref, s32[412]{0:T(512)S(1)} %get-tuple-element.17.table_ref, bf16[32,64,128]{2,1,0:T(8,128)(2,1)S(1)} %bitcast.21, ...), custom_call_target="tpu_custom_call", output_to_operand_aliasing={{0}: (4, {}), {1}: (5, {})} | custom-call | tf_op jit(solution)/shard_map/row_stats/pallas_call | solution.py:298
  29.6 5.5 %all-gather = f32[96,384]{1,0:T(8,128)S(1)} all-gather(f32[24,384]{1,0:T(8,128)S(1)} %get-tuple-element.22), channel_id=2, replica_groups=mesh['section'=2,'tp'=8,'y'=8,'xl'=2,'core'=2] {'xl','core'}, dimensions={0}, use_global_device_ids=true | all-gather | bytes 184320 | tf_op jit(solution)/shard_map/all_gather | solution.py:353
  35.1 4.8 %key_value_gradients.1 = (bf16[32,64,128]{2,1,0:T(8,128)(2,1)}, f32[16,384]{1,0:T(8,128)S(1)}) custom-call(s32[412]{0:T(512)S(1)} %get-tuple-element.17.table_ref, bf16[32,64,128]{2,1,0:T(8,128)(2,1)S(1)} %bitcast.22, bf16[8,384,128]{2,1,0:T(8,128)(2,1)S(1)} %get-tuple-element.20.q_ref, bf16[8,384,128]{2,1,0:T(8,128)(2,1)S(1)} %get-tuple-element.21.g_ref, ...), custom_call_target="tpu_custom_call" | custom-call | tf_op jit(solution)/shard_map/key_value_gradients/pallas_call | solution.py:310
  40.0 4.3 %all-to-all-start.1 = ((bf16[8,256,128]{2,1,0:T(8,128)(2,1)}), bf16[8,256,128]{2,1,0:T(8,128)(2,1)S(1)}, u32[]{:S(2)}, u32[]{:S(2)}) async-start(bf16[8,256,128]{2,1,0:T(8,128)(2,1)} %bitcast.13), calls=%async_computation.1 | async-start | bytes 1048576 | tf_op jit(solution)/shard_map/all_to_all | solution.py:355
  44.3 4.5 %query_gradients.1 = (f32[2,128,768]{2,1,0:T(8,128)S(1)}, bf16[2,128,768]{2,1,0:T(8,128)(2,1)S(1)}) custom-call(s32[3]{0:T(128)S(1)} %pad_add_fusion.place_ref, s32[412]{0:T(512)S(1)} %get-tuple-element.17.table_ref, bf16[32,64,128]{2,1,0:T(8,128)(2,1)S(1)} %bitcast.23, bf16[8,384,128]{2,1,0:T(8,128)(2,1)S(1)} %get-tuple-element.20.q_ref, ...), custom_call_target="tpu_custom_call" | custom-call | tf_op jit(solution)/shard_map/query_gradients/pallas_call | solution.py:325
  48.8 3.0 %all-gather.1 = bf16[4,128,768]{2,1,0:T(8,128)(2,1)S(1)} all-gather(bf16[2,128,768]{2,1,0:T(8,128)(2,1)S(1)} %get-tuple-element.26), channel_id=3, replica_groups=mesh['section'=2,'tp'=8,'y'=8,'xl'=2,'core'=2] {'core'}, dimensions={0}, use_global_device_ids=true | all-gather | bytes 1179648 | tf_op jit(solution)/shard_map/all_gather | solution.py:357
  51.8 0.1 fusion
  51.9 5.4 %collective-permute-start.1 = (bf16[128,768]{1,0:T(8,128)(2,1)S(1)}, bf16[128,768]{1,0:T(8,128)(2,1)S(1)}, u32[]{:S(2)}, u32[]{:S(2)}) collective-permute-start(bf16[128,768]{1,0:T(8,128)(2,1)S(1)} %get-tuple-element.32), channel_id=1, source_target_pairs={{0,256},{256,0},{1,257},{257,1},{2,258},{258,2},{3,259},{259,3},{4... | collective-permute-start | bytes 589832 | tf_op jit(solution)/shard_map/ppermute | solution.py:263
  57.3 4.0 %collective-permute-start.2 = (bf16[128,768]{1,0:T(8,128)(2,1)S(1)}, bf16[128,768]{1,0:T(8,128)(2,1)S(1)}, u32[]{:S(2)}, u32[]{:S(2)}) collective-permute-start(bf16[128,768]{1,0:T(8,128)(2,1)S(1)} %get-tuple-element.31), channel_id=1, source_target_pairs={{0,258},{2,256},{256,2},{258,0},{1,259},{3,257},{257,3},{259,1},{4... | collective-permute-start | bytes 589832 | tf_op jit(solution)/shard_map/ppermute | solution.py:360
  61.3 1.5 %all-to-all-done.1 = bf16[8,256,128]{2,1,0:T(8,128)(2,1)S(1)} async-done(((bf16[8,256,128]{2,1,0:T(8,128)(2,1)}), bf16[8,256,128]{2,1,0:T(8,128)(2,1)S(1)}, u32[]{:S(2)}, u32[]{:S(2)}) %all-to-all-start.1) | async-done | bytes 524320 | tf_op jit(solution)/shard_map/all_to_all | solution.py:355
  62.8 0.1 reduce_sum.12
  62.9 6.4 %all-gather.2 = bf16[512,128]{1,0:T(8,128)(2,1)S(1)} all-gather(bf16[256,128]{1,0:T(8,128)(2,1)S(1)} %reduce_sum.12), channel_id=4, replica_groups=mesh['section'=2,'tp'=8,'y'=8,'xl'=2,'core'=2] {'section'}, dimensions={0}, use_global_device_ids=true | all-gather | bytes 196608 | tf_op jit(solution)/shard_map/all_gather | solution.py:363
  69.3 0.6 constant_dynamic-slice_fusion.1
  70.0 0.0 collective-permute-done.1
  70.0 0.0 collective-permute-done.2
  70.0 0.7 %fusion.1 = bf16[1,128,768]{2,1,0:T(8,128)(2,1)} fusion(bf16[128,768]{1,0:T(8,128)(2,1)S(1)} %collective-permute-done.2, bf16[128,768]{1,0:T(8,128)(2,1)S(1)} %collective-permute-done.1), kind=kLoop, calls=%fused_computation.5 | loop fusion | flops 393216 | bytes 589824 | tf_op jit(solution)/shard_map/broadcast_in_dim | solution.py:370
  (3 shorter events, 0.1 us)
Async XLA Ops:
  2.3 7.2 %copy-start.2 = (bf16[1,128,768]{2,1,0:T(8,128)(2,1)S(1)}, bf16[1,128,768]{2,1,0:T(8,128)(2,1)}, u32[]{:S(2)}) copy-start(bf16[1,128,768]{2,1,0:T(8,128)(2,1)} %param.9) | copy-start | bytes 589828
  2.3 7.2 %copy-start.3 = (bf16[1,128,768]{2,1,0:T(8,128)(2,1)S(1)}, bf16[1,128,768]{2,1,0:T(8,128)(2,1)}, u32[]{:S(2)}) copy-start(bf16[1,128,768]{2,1,0:T(8,128)(2,1)} %param.6) | copy-start | bytes 589828
  2.3 24.7 %all-to-all-start = ((bf16[8,2,128,128]{3,2,1,0:T(8,128)(2,1)}), bf16[8,2,128,128]{3,2,1,0:T(8,128)(2,1)S(1)}, u32[]{:S(2)}, u32[]{:S(2)}) async-start(bf16[8,2,128,128]{3,2,1,0:T(8,128)(2,1)} %broadcast_select_fusion), calls=%async_computation | async-start | bytes 1048576 | tf_op jit(solution)/shard_map/all_to_all | solution.py:346
  9.6 12.5 %collective-permute-start = (bf16[128,1536]{1,0:T(8,128)(2,1)S(1)}, bf16[128,1536]{1,0:T(8,128)(2,1)S(1)}, u32[]{:S(2)}, u32[]{:S(2)}) collective-permute-start(bf16[128,1536]{1,0:T(8,128)(2,1)S(1)} %pad_maximum_fusion), channel_id=1, source_target_pairs={{0,2},{2,0},{1,3},{3,1},{4,6},{6,4},{5,7},{7,5},{8,10},{10,8},{9,1... | collective-permute-start | bytes 1179656 | tf_op jit(solution)/shard_map/ppermute | solution.py:263
  12.4 2.5 %copy-start = (s32[1,4096]{1,0:T(1,128)S(1)}, s32[1,4096]{1,0:T(1,128)}, u32[]{:S(2)}) copy-start(s32[1,4096]{1,0:T(1,128)} %episode_ref.1) | copy-start | bytes 49156
  12.4 2.5 %copy-start.1 = (s32[64]{0:T(128)S(1)}, s32[64]{0:T(128)}, u32[]{:S(2)}) copy-start(s32[64]{0:T(128)} %order_ref.1) | copy-start | bytes 772
  40.0 22.8 %all-to-all-start.1 = ((bf16[8,256,128]{2,1,0:T(8,128)(2,1)}), bf16[8,256,128]{2,1,0:T(8,128)(2,1)S(1)}, u32[]{:S(2)}, u32[]{:S(2)}) async-start(bf16[8,256,128]{2,1,0:T(8,128)(2,1)} %bitcast.13), calls=%async_computation.1 | async-start | bytes 1048576 | tf_op jit(solution)/shard_map/all_to_all | solution.py:355
  51.9 18.1 %collective-permute-start.1 = (bf16[128,768]{1,0:T(8,128)(2,1)S(1)}, bf16[128,768]{1,0:T(8,128)(2,1)S(1)}, u32[]{:S(2)}, u32[]{:S(2)}) collective-permute-start(bf16[128,768]{1,0:T(8,128)(2,1)S(1)} %get-tuple-element.32), channel_id=1, source_target_pairs={{0,256},{256,0},{1,257},{257,1},{2,258},{258,2},{3,259},{259,3},{4... | collective-permute-start | bytes 589832 | tf_op jit(solution)/shard_map/ppermute | solution.py:263
  57.3 12.6 %collective-permute-start.2 = (bf16[128,768]{1,0:T(8,128)(2,1)S(1)}, bf16[128,768]{1,0:T(8,128)(2,1)S(1)}, u32[]{:S(2)}, u32[]{:S(2)}) collective-permute-start(bf16[128,768]{1,0:T(8,128)(2,1)S(1)} %get-tuple-element.31), channel_id=1, source_target_pairs={{0,258},{2,256},{256,2},{258,0},{1,259},{3,257},{257,3},{259,1},{4... | collective-permute-start | bytes 589832 | tf_op jit(solution)/shard_map/ppermute | solution.py:360

commit v6 on v5

--- a/solution.py
+++ b/solution.py
@@ -17,7 +17,7 @@
 GROUP = 4
 UNROLLS = (8, 4, 2, 1)
 CHUNKS = KEYS // GROUP
-STEPS = SLOTS * CHUNKS + CHUNKS
+STEPS = SLOTS * CHUNKS + 2 * CHUNKS
 SCALING = HEAD ** (-0.5)
 LOG2E = 1.4426950408889634
 NEG_FILL = -1e30
@@ -44,38 +44,56 @@
     return first
 
 
+def list_span(table_ref, starts, step, slot, base, keys, chunk):
+    first = start_of(starts, base)
+    at = step * GROUP
+    for number, place in keys:
+        table_ref[SPANS + at] = number
+        table_ref[PLACES + at] = place
+        seen = (place <= base) & (place + (SPAN - 1) >= first)
+        at = at + seen.astype(jnp.int32)
+    count = (at - step * GROUP + GROUP - 1) // GROUP
+    for extra in range(GROUP):
+        table_ref[SPANS + at + extra] = 0
+        table_ref[PLACES + at + extra] = FAR
+    for c in range(len(keys) // GROUP):
+        table_ref[SLOT + step + c] = slot
+        table_ref[CHUNK + step + c] = c if chunk is None else chunk
+        table_ref[BASE + step + c] = base
+    return step + count
+
+
 def prepare_kernel(
-    order_ref, place_ref, episode_ref, own_ref, table_ref, q_ref, g_ref
+    order_ref, place_ref, episode_ref, own_ref, table_ref, query_table_ref, q_ref, g_ref
 ):
     y, xl, core = place_ref[0], place_ref[1], place_ref[2]
     ids = episode_ref[...]
     starts = [jnp.sum((ids < v).astype(jnp.int32)) for v in (1, 2, 3)]
     for n, s in enumerate(starts):
         table_ref[1 + n] = s
-    key_bases = [
-        order_ref[((k // 2) * 4 + xl * 2 + core) * 2 + k % 2] * SPAN for k in range(KEYS)
-    ]
+        query_table_ref[1 + n] = s
+
+    def keys_of(side):
+        return [
+            ((k // 2) * 4 + k % 2, order_ref[((k // 2) * 4 + xl * 2 + side) * 2 + k % 2] * SPAN)
+            for k in range(KEYS)
+        ]
+
+    keys = keys_of(core)
 
     def list_slot(slot, step):
         base = order_ref[y * SLOTS + slot] * SPAN
-        first = start_of(starts, base)
-        at = step * GROUP
-        for k in range(KEYS):
-            table_ref[SPANS + at] = (k // 2) * 4 + k % 2
-            table_ref[PLACES + at] = key_bases[k]
-            seen = (key_bases[k] <= base) & (key_bases[k] + (SPAN - 1) >= first)
-            at = at + seen.astype(jnp.int32)
-        count = (at - step * GROUP + GROUP - 1) // GROUP
-        for extra in range(GROUP):
-            table_ref[SPANS + at + extra] = 0
-            table_ref[PLACES + at + extra] = FAR
-        for c in range(CHUNKS):
-            table_ref[SLOT + step + c] = slot
-            table_ref[CHUNK + step + c] = c
-            table_ref[BASE + step + c] = base
-        return step + count
+        return list_span(table_ref, starts, step, slot, base, keys, None)
 
     table_ref[0] = lax.fori_loop(0, SLOTS, list_slot, jnp.int32(0))
+    both = keys + [(2 * KEYS + number, place) for number, place in keys_of(1 - core)]
+
+    def list_own_slot(n, step):
+        slot = n // 2 * 4 + core * 2 + n % 2
+        base = order_ref[y * SLOTS + slot] * SPAN
+        return list_span(query_table_ref, starts, step, slot, base, both, n)
+
+    query_table_ref[0] = lax.fori_loop(0, SLOTS // 2, list_own_slot, jnp.int32(0))
     lay_out(own_ref, q_ref, g_ref, xl)
 
 
@@ -208,31 +226,36 @@
 def query_kernel(
     place_ref,
     table_ref,
-    kv_ref,
+    own_ref,
+    far_ref,
     q_ref,
     g_ref,
     rows_ref,
-    after_ref,
-    keep_ref,
-    send_ref,
+    out_ref,
     acc_ref,
     log_ref,
     delta_ref,
+    kv_ref,
 ):
+    xl, core = place_ref[1], place_ref[2]
+    kv_ref[: 2 * KEYS] = own_ref[...]
+    kv_ref[2 * KEYS :] = far_ref[...]
     acc_ref[...] = jnp.zeros_like(acc_ref)
-    for slot in range(SLOTS):
-        log_ref[slot] = jnp.broadcast_to(rows_ref[slot : slot + 1], (HEAD, ROWS)).T
-        delta_ref[slot] = jnp.broadcast_to(rows_ref[8 + slot : 9 + slot], (HEAD, ROWS)).T
+    for n in range(SLOTS // 2):
+        slot = n // 2 * 4 + core * 2 + n % 2
+        log_ref[n] = jnp.broadcast_to(rows_ref[pl.ds(slot, 1), :], (HEAD, ROWS)).T
+        delta_ref[n] = jnp.broadcast_to(rows_ref[pl.ds(8 + slot, 1), :], (HEAD, ROWS)).T
 
     def one_step(step):
-        slot, base = table_ref[SLOT + step], table_ref[BASE + step]
+        slot, own = table_ref[SLOT + step], table_ref[CHUNK + step]
+        base = table_ref[BASE + step]
         spans, keys, values = load_keys(table_ref, kv_ref, step)
         query_pos = base + lax.broadcasted_iota(jnp.int32, (SPAN, HEAD), 0)
         first = start_of([table_ref[1 + n] for n in range(3)], query_pos)
         lane = lax.broadcasted_iota(jnp.int32, (1, HEAD), 1)
         raw = dot(q_ref[slot], keys, NT)
         products = dot(g_ref[slot], values, NT)
-        log_total, delta = log_ref[slot], delta_ref[slot]
+        log_total, delta = log_ref[own], delta_ref[own]
         parts = []
         for n in range(GROUP // 2):
             low, high = (table_ref[PLACES + step * GROUP + 2 * n + i] for i in range(2))
@@ -243,20 +266,16 @@
             scores = jnp.where(visible[None], scores, NEG_FILL).reshape(ROWS, HEAD)
             probs = jnp.exp2(scores - log_total)
             parts.append((probs * (products[:, cols] - delta)).astype(jnp.bfloat16))
-        acc_ref[slot] += dot(jnp.concatenate(parts, axis=1), keys, NN)
+        acc_ref[own] += dot(jnp.concatenate(parts, axis=1), keys, NN)
 
     run_steps(table_ref, one_step)
-    xl, core = place_ref[1], place_ref[2]
     for rel in range(2):
         chip = xl if rel == 0 else 1 - xl
         for half in range(2):
-            rows = slice(half * SPAN, (half + 1) * SPAN)
-            mine = chip * 4 + core * 2 + half
-            theirs = chip * 4 + (1 - core) * 2 + half
             for h in range(HEADS):
-                cols, at = slice(h * HEAD, (h + 1) * HEAD), slice(h * SPAN, (h + 1) * SPAN)
-                keep_ref[rel, rows, cols] = acc_ref[mine, at, :] * SCALING
-                send_ref[rel, rows, cols] = (acc_ref[theirs, at, :] * SCALING).astype(jnp.bfloat16)
+                block = acc_ref[chip * 2 + half, h * SPAN : (h + 1) * SPAN, :] * SCALING
+                rows, cols = slice(half * SPAN, (half + 1) * SPAN), slice(h * HEAD, (h + 1) * HEAD)
+                out_ref[rel, rows, cols] = block.astype(jnp.bfloat16)
 
 
 def swap(block, axis):
@@ -288,9 +307,9 @@
     return call(
         prepare_kernel,
         "prepare",
-        (jax.ShapeDtypeStruct((TABLE,), jnp.int32), LAID_OUT, LAID_OUT),
+        (*[jax.ShapeDtypeStruct((TABLE,), jnp.int32)] * 2, LAID_OUT, LAID_OUT),
         [SMEM, SMEM, VMEM, VMEM],
-        (SMEM, VMEM, VMEM),
+        (SMEM, SMEM, VMEM, VMEM),
     )(order, place, episodes, own)
 
 
@@ -320,19 +339,16 @@
     )(table, kv_all, q, g, stats_all)
 
 
-def query_gradients(place, table, kv_all, q, g, rows, after):
-    shape = (2, 2 * SPAN, HEADS * HEAD)
+def query_gradients(place, table, kv_own, kv_far, q, g, rows):
     return call(
         query_kernel,
         "query_gradients",
-        (
-            jax.ShapeDtypeStruct(shape, jnp.float32),
-            jax.ShapeDtypeStruct(shape, jnp.bfloat16),
-        ),
-        [SMEM, SMEM, VMEM, VMEM, VMEM, VMEM, pl.BlockSpec(memory_space=pl.ANY)],
-        (VMEM, VMEM),
-        [pltpu.VMEM((SLOTS, ROWS, HEAD), jnp.float32)] * 3,
-    )(place, table, kv_all, q, g, rows, after)
+        jax.ShapeDtypeStruct((2, 2 * SPAN, HEADS * HEAD), jnp.bfloat16),
+        [SMEM, SMEM, VMEM, VMEM, VMEM, VMEM, VMEM],
+        VMEM,
+        [pltpu.VMEM((SLOTS // 2, ROWS, HEAD), jnp.float32)] * 3
+        + [pltpu.VMEM((4 * KEYS, SPAN, HEAD), jnp.bfloat16)],
+    )(place, table, kv_own, kv_far, q, g, rows)
 
 
 def per_device(query_rows, key_rows, stored_value_rows, output_grad, span_order, episode_ids):
@@ -348,15 +364,14 @@
     remote = swap(both, "xl")
     own = lax.all_gather(both, "core", axis=0, tiled=True)
     other = lax.all_gather(remote, "core", axis=0, tiled=True)
-    table, q, g = prepare(span_order, place, episode_ids, own)
+    table, query_table, q, g = prepare(span_order, place, episode_ids, own)
     q, g, stats = row_stats(place, table, kv_all, other, q, g)
     stats_all = lax.all_gather(stats, ("xl", "core"), axis=0)
     dkv, rows = key_value_gradients(table, kv_all, q, g, stats_all)
     dkv_parts = lax.all_to_all(dkv.reshape(ring, 2 * tokens, HEAD), "y", 0, 0, tiled=True)
-    keep, send = query_gradients(place, table, kv_all, q, g, rows, dkv)
-    sent = lax.all_gather(send, "core", axis=0)
-    dq = keep + lax.dynamic_index_in_dim(sent, 1 - place[2], 0, False).astype(jnp.float32)
-    parts = dq.astype(jnp.bfloat16)
+    kv_late, unused = lax.optimization_barrier((kv_all, dkv))
+    kv_far = swap(kv_late, "core")
+    parts = query_gradients(place, query_table, kv_all, kv_far, q, g, rows)
     across = lax.ppermute(parts[1], ("section", "xl"), [(0, 3), (1, 2), (2, 1), (3, 0)])
     straight = swap(parts[0], "section")
     dkv_sum = jnp.sum(dkv_parts.astype(jnp.float32), axis=0).astype(jnp.bfloat16)

time: 71.8 us -> 72.2 us (level)
  waiting for transfers between devices: 9.05 us -> 12.4 us
  blocking collectives: 19.8 us -> 16.8 us
  starting transfers between devices: 23.7 us -> 25.1 us
  Pallas kernels: 14.1 us -> 12.8 us
    all_gather x1 -> x0, blocking collectives: 3.01 us -> none  [per_device(): sent = lax.all_gather(send, 'core', axis=0)]
    all_to_all x1, waiting for transfers between devices: 1.47 us -> 3.74 us  [per_device(): lax.all_to_all(dkv.reshape(ring, 2 * tokens, HEAD), 'y', 0, 0, tiled=True)]
    all_to_all x1, starting transfers between devices: 4.31 us -> 5.63 us  [per_device(): lax.all_to_all(dkv.reshape(ring, 2 * tokens, HEAD), 'y', 0, 0, tiled=True)]
    ppermute x2 -> x3, waiting for transfers between devices: 4.96 us -> 6.08 us  [swap(): return lax.ppermute(block, axis, [(0, 1), (1, 0)])]
    pallas_call x2, Pallas kernels: 6.64 us -> 5.77 us  [the longest x1 2.88 us: query_gradients(): call(query_kernel, 'query_gradients', jax.ShapeDtypeStruct((2, 2 * SPAN,...]
    ppermute x2 -> x3, starting transfers between devices: 8.17 us -> 8.21 us  [swap(): return lax.ppermute(block, axis, [(0, 1), (1, 0)])]
  transfers between devices with their start and end apart: 5 -> 6, of which waited for: 3 -> 4; matrix products, arithmetic and copies ran while one was open for 1% -> 1% of each run, Pallas kernels for 9% -> 8%
where the time goes in v6:
time: 72.2 us; the launch traced here: 71.1 us
  starting transfers between devices  25.1 us (35%)
  blocking collectives  16.8 us (23%)
  Pallas kernels  12.8 us (18%)
  waiting for transfers between devices  12.4 us (17%)
  other arithmetic  2.58 us (4%)
  between operations  0.74 us (1%)
    ppermute x3, starting transfers between devices, swap(): return lax.ppermute(block, axis, [(0, 1), (1, 0)])  8.21 us
    all_to_all x1, starting transfers between devices, per_device(): kv_all = lax.all_to_all(kv, 'y', 0, 0, tiled=True).reshape(KEYS_VALUES)  7.23 us
    all_gather x1, blocking collectives, per_device(): both_dkv = lax.all_gather(dkv_sum, 'section', axis=0)  6.45 us
    ppermute x3, waiting for transfers between devices, swap(): return lax.ppermute(block, axis, [(0, 1), (1, 0)])  6.08 us
    all_to_all x1, starting transfers between devices, per_device(): lax.all_to_all(dkv.reshape(ring, 2 * tokens, HEAD), 'y', 0, 0, tiled=True)  5.63 us
    all_gather x1, blocking collectives, per_device(): stats_all = lax.all_gather(stats, ('xl', 'core'), axis=0)  5.47 us
    pallas_call x1, Pallas kernels, key_value_gradients(): call(key_value_kernel, 'key_value_gradients', (jax.ShapeDtypeStruct(KEYS_...  4.56 us
    ppermute x1, starting transfers between devices, per_device(): lax.ppermute(parts[1], ('section', 'xl'), [(0, 3), (1, 2), (2, 1), (3, 0)])  4.01 us
  transfers between devices with their start and end apart: 6, of which 4 were waited for; matrix products, arithmetic and copies ran while one was open for 1% of the time, Pallas kernels for 8%

profile of v6, /device:TPU:6, one launch (start us, length us, event | category | flops | bytes accessed | tf_op | source)
XLA Modules:
  0.0 71.1 jit_solution(1367711929710146357)
XLA Ops:
  0.6 1.7 %broadcast_select_fusion = bf16[8,2,128,128]{3,2,1,0:T(8,128)(2,1)} fusion(pred[2]{0:T(512)(128)(4,1)S(1)} %iota_compare_fusion, bf16[128,128]{1,0:T(8,128)(2,1)} %bitcast.25, bf16[128,128]{1,0:T(8,128)(2,1)} %bitcast.26), kind=kLoop, calls=%fused_computation | loop fusion | flops 262144 | bytes 589826 | tf_op jit(solution)/shard_map/jit(_where)/select_n | solution.py:361
  2.3 0.0 copy-start.2
  2.3 0.0 copy-start.3
  2.3 7.2 %all-to-all-start = ((bf16[8,2,128,128]{3,2,1,0:T(8,128)(2,1)}), bf16[8,2,128,128]{3,2,1,0:T(8,128)(2,1)S(1)}, u32[]{:S(2)}, u32[]{:S(2)}) async-start(bf16[8,2,128,128]{3,2,1,0:T(8,128)(2,1)} %broadcast_select_fusion), calls=%async_computation | async-start | bytes 1048576 | tf_op jit(solution)/shard_map/all_to_all | solution.py:362
  9.6 0.0 copy-done.2
  9.6 0.0 copy-done.3
  9.6 2.7 %collective-permute-start = (bf16[128,1536]{1,0:T(8,128)(2,1)S(1)}, bf16[128,1536]{1,0:T(8,128)(2,1)S(1)}, u32[]{:S(2)}, u32[]{:S(2)}) collective-permute-start(bf16[128,1536]{1,0:T(8,128)(2,1)S(1)} %pad_maximum_fusion), channel_id=1, source_target_pairs={{0,2},{2,0},{1,3},{3,1},{4,6},{6,4},{5,7},{7,5},{8,10},{10,8},{9,1... | collective-permute-start | bytes 1179656 | tf_op jit(solution)/shard_map/ppermute | solution.py:282
  12.4 0.1 pad_add_fusion.place_ref
  12.4 0.0 copy-start
  12.4 0.0 copy-start.1
  12.4 2.5 %all_gather.18.own_ref = bf16[256,1536]{1,0:T(8,128)(2,1)S(1)} all-gather(bf16[128,1536]{1,0:T(8,128)(2,1)S(1)} %pad_maximum_fusion), channel_id=1, replica_groups=mesh['section'=2,'tp'=8,'y'=8,'xl'=2,'core'=2] {'core'}, dimensions={0}, use_global_device_ids=true | all-gather | bytes 1179648 | tf_op jit(solution)/shard_map/all_gather | solution.py:365
  14.9 0.0 copy-done
  14.9 0.0 copy-done.1
  14.9 2.9 %prepare.1 = (s32[456]{0:T(512)S(1)}, s32[456]{0:T(512)S(1)}, bf16[8,384,128]{2,1,0:T(8,128)(2,1)S(1)}, bf16[8,384,128]{2,1,0:T(8,128)(2,1)S(1)}) custom-call(s32[64]{0:T(128)S(1)} %copy-done.1, s32[3]{0:T(128)S(1)} %pad_add_fusion.place_ref, s32[1,4096]{1,0:T(1,128)S(1)} %copy-done, bf16[256,1536]{1,0:T(8,128)(2,1)S(1)} %all_gather.18.own_ref), custom_call_target="tpu_custom_call" | custom-call | tf_op jit(solution)/shard_map/prepare/pallas_call | solution.py:307
  17.8 4.3 %collective-permute-done = bf16[128,1536]{1,0:T(8,128)(2,1)S(1)} collective-permute-done((bf16[128,1536]{1,0:T(8,128)(2,1)S(1)}, bf16[128,1536]{1,0:T(8,128)(2,1)S(1)}, u32[]{:S(2)}, u32[]{:S(2)}) %collective-permute-start) | collective-permute-done | bytes 393248 | tf_op jit(solution)/shard_map/ppermute | solution.py:282
  22.1 2.4 %all_gather.19.other_ref = bf16[256,1536]{1,0:T(8,128)(2,1)S(1)} all-gather(bf16[128,1536]{1,0:T(8,128)(2,1)S(1)} %collective-permute-done), channel_id=1, replica_groups=mesh['section'=2,'tp'=8,'y'=8,'xl'=2,'core'=2] {'core'}, dimensions={0}, use_global_device_ids=true | all-gather | bytes 1179648 | tf_op jit(solution)/shard_map/all_gather | solution.py:366
  24.4 2.6 %all-to-all-done = bf16[8,2,128,128]{3,2,1,0:T(8,128)(2,1)S(1)} async-done(((bf16[8,2,128,128]{3,2,1,0:T(8,128)(2,1)}), bf16[8,2,128,128]{3,2,1,0:T(8,128)(2,1)S(1)}, u32[]{:S(2)}, u32[]{:S(2)}) %all-to-all-start) | async-done | bytes 524320 | tf_op jit(solution)/shard_map/all_to_all | solution.py:362
  27.0 2.5 %row_stats.1 = (bf16[8,384,128]{2,1,0:T(8,128)(2,1)S(1)}, bf16[8,384,128]{2,1,0:T(8,128)(2,1)S(1)}, f32[24,384]{1,0:T(8,128)S(1)}) custom-call(s32[3]{0:T(128)S(1)} %pad_add_fusion.place_ref, s32[456]{0:T(512)S(1)} %get-tuple-element.18.table_ref, bf16[32,64,128]{2,1,0:T(8,128)(2,1)S(1)} %bitcast.17, ...), custom_call_target="tpu_custom_call", output_to_operand_aliasing={{0}: (4, {}), {1}: (5, {})} | custom-call | tf_op jit(solution)/shard_map/row_stats/pallas_call | solution.py:317
  29.5 5.5 %all-gather = f32[96,384]{1,0:T(8,128)S(1)} all-gather(f32[24,384]{1,0:T(8,128)S(1)} %get-tuple-element.23), channel_id=2, replica_groups=mesh['section'=2,'tp'=8,'y'=8,'xl'=2,'core'=2] {'xl','core'}, dimensions={0}, use_global_device_ids=true | all-gather | bytes 184320 | tf_op jit(solution)/shard_map/all_gather | solution.py:369
  35.0 4.6 %key_value_gradients.1 = (bf16[32,64,128]{2,1,0:T(8,128)(2,1)}, f32[16,384]{1,0:T(8,128)S(1)}) custom-call(s32[456]{0:T(512)S(1)} %get-tuple-element.18.table_ref, bf16[32,64,128]{2,1,0:T(8,128)(2,1)S(1)} %bitcast.18, bf16[8,384,128]{2,1,0:T(8,128)(2,1)S(1)} %get-tuple-element.21.q_ref, bf16[8,384,128]{2,1,0:T(8,128)(2,1)S(1)} %get-tuple-element.22.g_ref, ...), custom_call_target="tpu_custom_call" | custom-call | tf_op jit(solution)/shard_map/key_value_gradients/pallas_call | solution.py:329
  39.5 5.6 %all-to-all-start.1 = ((bf16[8,256,128]{2,1,0:T(8,128)(2,1)}), bf16[8,256,128]{2,1,0:T(8,128)(2,1)S(1)}, u32[]{:S(2)}, u32[]{:S(2)}) async-start(bf16[8,256,128]{2,1,0:T(8,128)(2,1)} %bitcast.11), calls=%async_computation.1 | async-start | bytes 1048576 | tf_op jit(solution)/shard_map/all_to_all | solution.py:371
  45.2 2.0 %collective-permute-start.1 = (bf16[32,64,128]{2,1,0:T(8,128)(2,1)S(1)}, bf16[32,64,128]{2,1,0:T(8,128)(2,1)S(1)}, u32[]{:S(2)}, u32[]{:S(2)}) collective-permute-start(bf16[32,64,128]{2,1,0:T(8,128)(2,1)S(1)} %bitcast.19), channel_id=1, source_target_pairs={{0,1},{1,0},{2,3},{3,2},{4,5},{5,4},{6,7},{7,6},{8,9},{9,8},{10,11... | collective-permute-start | bytes 1572872 | tf_op jit(solution)/shard_map/ppermute | solution.py:282
  47.1 1.8 %collective-permute-done.1.far_ref = bf16[32,64,128]{2,1,0:T(8,128)(2,1)S(1)} collective-permute-done((bf16[32,64,128]{2,1,0:T(8,128)(2,1)S(1)}, bf16[32,64,128]{2,1,0:T(8,128)(2,1)S(1)}, u32[]{:S(2)}, u32[]{:S(2)}) %collective-permute-start.1) | collective-permute-done | bytes 524320 | tf_op jit(solution)/shard_map/ppermute | solution.py:282
  49.0 2.9 %query_gradients.1 = bf16[2,128,768]{2,1,0:T(8,128)(2,1)S(1)} custom-call(s32[3]{0:T(128)S(1)} %pad_add_fusion.place_ref, s32[456]{0:T(512)S(1)} %get-tuple-element.17.table_ref, bf16[32,64,128]{2,1,0:T(8,128)(2,1)S(1)} %bitcast.20, bf16[32,64,128]{2,1,0:T(8,128)(2,1)S(1)} %collective-permute-done.1.far_ref, ...), custom_call_target="tpu_custom_call" | custom-call | tf_op jit(solution)/shard_map/query_gradients/pallas_call | solution.py:343
  51.9 3.5 %collective-permute-start.2 = (bf16[128,768]{1,0:T(8,128)(2,1)S(1)}, bf16[128,768]{1,0:T(8,128)(2,1)S(1)}, u32[]{:S(2)}, u32[]{:S(2)}) collective-permute-start(bf16[128,768]{1,0:T(8,128)(2,1)S(1)} %get-tuple-element.32), channel_id=1, source_target_pairs={{0,256},{256,0},{1,257},{257,1},{2,258},{258,2},{3,259},{259,3},{4... | collective-permute-start | bytes 589832 | tf_op jit(solution)/shard_map/ppermute | solution.py:282
  55.4 4.0 %collective-permute-start.3 = (bf16[128,768]{1,0:T(8,128)(2,1)S(1)}, bf16[128,768]{1,0:T(8,128)(2,1)S(1)}, u32[]{:S(2)}, u32[]{:S(2)}) collective-permute-start(bf16[128,768]{1,0:T(8,128)(2,1)S(1)} %get-tuple-element.31), channel_id=1, source_target_pairs={{0,258},{2,256},{256,2},{258,0},{1,259},{3,257},{257,3},{259,1},{4... | collective-permute-start | bytes 589832 | tf_op jit(solution)/shard_map/ppermute | solution.py:375
  59.4 3.7 %all-to-all-done.1 = bf16[8,256,128]{2,1,0:T(8,128)(2,1)S(1)} async-done(((bf16[8,256,128]{2,1,0:T(8,128)(2,1)}), bf16[8,256,128]{2,1,0:T(8,128)(2,1)S(1)}, u32[]{:S(2)}, u32[]{:S(2)}) %all-to-all-start.1) | async-done | bytes 524320 | tf_op jit(solution)/shard_map/all_to_all | solution.py:371
  63.2 0.1 reduce_sum.12
  63.3 6.4 %all-gather.1 = bf16[512,128]{1,0:T(8,128)(2,1)S(1)} all-gather(bf16[256,128]{1,0:T(8,128)(2,1)S(1)} %reduce_sum.12), channel_id=3, replica_groups=mesh['section'=2,'tp'=8,'y'=8,'xl'=2,'core'=2] {'section'}, dimensions={0}, use_global_device_ids=true | all-gather | bytes 196608 | tf_op jit(solution)/shard_map/all_gather | solution.py:378
  69.7 0.6 constant_dynamic-slice_fusion.1
  70.3 0.0 collective-permute-done.2
  70.3 0.0 collective-permute-done.3
  70.3 0.7 %fusion = bf16[1,128,768]{2,1,0:T(8,128)(2,1)} fusion(bf16[128,768]{1,0:T(8,128)(2,1)S(1)} %collective-permute-done.3, bf16[128,768]{1,0:T(8,128)(2,1)S(1)} %collective-permute-done.2), kind=kLoop, calls=%fused_computation.3 | loop fusion | flops 393216 | bytes 589824 | tf_op jit(solution)/shard_map/broadcast_in_dim | solution.py:385
  (3 shorter events, 0.1 us)
Async XLA Ops:
  2.3 7.2 %copy-start.2 = (bf16[1,128,768]{2,1,0:T(8,128)(2,1)S(1)}, bf16[1,128,768]{2,1,0:T(8,128)(2,1)}, u32[]{:S(2)}) copy-start(bf16[1,128,768]{2,1,0:T(8,128)(2,1)} %param.9) | copy-start | bytes 589828
  2.3 7.2 %copy-start.3 = (bf16[1,128,768]{2,1,0:T(8,128)(2,1)S(1)}, bf16[1,128,768]{2,1,0:T(8,128)(2,1)}, u32[]{:S(2)}) copy-start(bf16[1,128,768]{2,1,0:T(8,128)(2,1)} %param.6) | copy-start | bytes 589828
  2.3 24.7 %all-to-all-start = ((bf16[8,2,128,128]{3,2,1,0:T(8,128)(2,1)}), bf16[8,2,128,128]{3,2,1,0:T(8,128)(2,1)S(1)}, u32[]{:S(2)}, u32[]{:S(2)}) async-start(bf16[8,2,128,128]{3,2,1,0:T(8,128)(2,1)} %broadcast_select_fusion), calls=%async_computation | async-start | bytes 1048576 | tf_op jit(solution)/shard_map/all_to_all | solution.py:362
  9.6 12.5 %collective-permute-start = (bf16[128,1536]{1,0:T(8,128)(2,1)S(1)}, bf16[128,1536]{1,0:T(8,128)(2,1)S(1)}, u32[]{:S(2)}, u32[]{:S(2)}) collective-permute-start(bf16[128,1536]{1,0:T(8,128)(2,1)S(1)} %pad_maximum_fusion), channel_id=1, source_target_pairs={{0,2},{2,0},{1,3},{3,1},{4,6},{6,4},{5,7},{7,5},{8,10},{10,8},{9,1... | collective-permute-start | bytes 1179656 | tf_op jit(solution)/shard_map/ppermute | solution.py:282
  12.4 2.5 %copy-start = (s32[1,4096]{1,0:T(1,128)S(1)}, s32[1,4096]{1,0:T(1,128)}, u32[]{:S(2)}) copy-start(s32[1,4096]{1,0:T(1,128)} %episode_ref.1) | copy-start | bytes 49156
  12.4 2.5 %copy-start.1 = (s32[64]{0:T(128)S(1)}, s32[64]{0:T(128)}, u32[]{:S(2)}) copy-start(s32[64]{0:T(128)} %order_ref.1) | copy-start | bytes 772
  39.5 23.6 %all-to-all-start.1 = ((bf16[8,256,128]{2,1,0:T(8,128)(2,1)}), bf16[8,256,128]{2,1,0:T(8,128)(2,1)S(1)}, u32[]{:S(2)}, u32[]{:S(2)}) async-start(bf16[8,256,128]{2,1,0:T(8,128)(2,1)} %bitcast.11), calls=%async_computation.1 | async-start | bytes 1048576 | tf_op jit(solution)/shard_map/all_to_all | solution.py:371
  45.2 3.8 %collective-permute-start.1 = (bf16[32,64,128]{2,1,0:T(8,128)(2,1)S(1)}, bf16[32,64,128]{2,1,0:T(8,128)(2,1)S(1)}, u32[]{:S(2)}, u32[]{:S(2)}) collective-permute-start(bf16[32,64,128]{2,1,0:T(8,128)(2,1)S(1)} %bitcast.19), channel_id=1, source_target_pairs={{0,1},{1,0},{2,3},{3,2},{4,5},{5,4},{6,7},{7,6},{8,9},{9,8},{10,11... | collective-permute-start | bytes 1572872 | tf_op jit(solution)/shard_map/ppermute | solution.py:282
  51.9 18.4 %collective-permute-start.2 = (bf16[128,768]{1,0:T(8,128)(2,1)S(1)}, bf16[128,768]{1,0:T(8,128)(2,1)S(1)}, u32[]{:S(2)}, u32[]{:S(2)}) collective-permute-start(bf16[128,768]{1,0:T(8,128)(2,1)S(1)} %get-tuple-element.32), channel_id=1, source_target_pairs={{0,256},{256,0},{1,257},{257,1},{2,258},{258,2},{3,259},{259,3},{4... | collective-permute-start | bytes 589832 | tf_op jit(solution)/shard_map/ppermute | solution.py:282
  55.4 14.9 %collective-permute-start.3 = (bf16[128,768]{1,0:T(8,128)(2,1)S(1)}, bf16[128,768]{1,0:T(8,128)(2,1)S(1)}, u32[]{:S(2)}, u32[]{:S(2)}) collective-permute-start(bf16[128,768]{1,0:T(8,128)(2,1)S(1)} %get-tuple-element.31), channel_id=1, source_target_pairs={{0,258},{2,256},{256,2},{258,0},{1,259},{3,257},{257,3},{259,1},{4... | collective-permute-start | bytes 589832 | tf_op jit(solution)/shard_map/ppermute | solution.py:375

commit v7 on v6

--- a/solution.py
+++ b/solution.py
@@ -64,14 +64,14 @@
 
 
 def prepare_kernel(
-    order_ref, place_ref, episode_ref, own_ref, table_ref, query_table_ref, q_ref, g_ref
+    order_ref, place_ref, episode_ref, own_ref, table_ref, near_ref, far_ref, q_ref, g_ref
 ):
     y, xl, core = place_ref[0], place_ref[1], place_ref[2]
     ids = episode_ref[...]
     starts = [jnp.sum((ids < v).astype(jnp.int32)) for v in (1, 2, 3)]
     for n, s in enumerate(starts):
-        table_ref[1 + n] = s
-        query_table_ref[1 + n] = s
+        for ref in (table_ref, near_ref, far_ref):
+            ref[1 + n] = s
 
     def keys_of(side):
         return [
@@ -86,14 +86,14 @@
         return list_span(table_ref, starts, step, slot, base, keys, None)
 
     table_ref[0] = lax.fori_loop(0, SLOTS, list_slot, jnp.int32(0))
-    both = keys + [(2 * KEYS + number, place) for number, place in keys_of(1 - core)]
-
-    def list_own_slot(n, step):
-        slot = n // 2 * 4 + core * 2 + n % 2
-        base = order_ref[y * SLOTS + slot] * SPAN
-        return list_span(query_table_ref, starts, step, slot, base, both, n)
-
-    query_table_ref[0] = lax.fori_loop(0, SLOTS // 2, list_own_slot, jnp.int32(0))
+    for ref, some_keys in ((near_ref, keys), (far_ref, keys_of(1 - core))):
+
+        def list_own_slot(n, step, ref=ref, some_keys=some_keys):
+            slot = n // 2 * 4 + core * 2 + n % 2
+            base = order_ref[y * SLOTS + slot] * SPAN
+            return list_span(ref, starts, step, slot, base, some_keys, n)
+
+        ref[0] = lax.fori_loop(0, SLOTS // 2, list_own_slot, jnp.int32(0))
     lay_out(own_ref, q_ref, g_ref, xl)
 
 
@@ -223,29 +223,18 @@
         dkv_ref[n] = (acc_ref[n] * scaling).astype(jnp.bfloat16)
 
 
-def query_kernel(
-    place_ref,
-    table_ref,
-    own_ref,
-    far_ref,
-    q_ref,
-    g_ref,
-    rows_ref,
-    out_ref,
-    acc_ref,
-    log_ref,
-    delta_ref,
-    kv_ref,
+def near_kernel(
+    place_ref, table_ref, kv_ref, q_ref, g_ref, rows_ref, acc_ref, log_ref, delta_ref
 ):
-    xl, core = place_ref[1], place_ref[2]
-    kv_ref[: 2 * KEYS] = own_ref[...]
-    kv_ref[2 * KEYS :] = far_ref[...]
     acc_ref[...] = jnp.zeros_like(acc_ref)
     for n in range(SLOTS // 2):
-        slot = n // 2 * 4 + core * 2 + n % 2
+        slot = n // 2 * 4 + place_ref[2] * 2 + n % 2
         log_ref[n] = jnp.broadcast_to(rows_ref[pl.ds(slot, 1), :], (HEAD, ROWS)).T
         delta_ref[n] = jnp.broadcast_to(rows_ref[pl.ds(8 + slot, 1), :], (HEAD, ROWS)).T
-
+    add_query_gradients(table_ref, kv_ref, q_ref, g_ref, log_ref, delta_ref, acc_ref)
+
+
+def add_query_gradients(table_ref, kv_ref, q_ref, g_ref, log_ref, delta_ref, acc_ref):
     def one_step(step):
         slot, own = table_ref[SLOT + step], table_ref[CHUNK + step]
         base = table_ref[BASE + step]
@@ -269,6 +258,14 @@
         acc_ref[own] += dot(jnp.concatenate(parts, axis=1), keys, NN)
 
     run_steps(table_ref, one_step)
+
+
+def far_kernel(
+    place_ref, table_ref, kv_ref, q_ref, g_ref, sum_ref, log_ref, delta_ref, out_ref, acc_ref
+):
+    acc_ref[...] = sum_ref[...]
+    add_query_gradients(table_ref, kv_ref, q_ref, g_ref, log_ref, delta_ref, acc_ref)
+    xl = place_ref[1]
     for rel in range(2):
         chip = xl if rel == 0 else 1 - xl
         for half in range(2):
@@ -307,9 +304,9 @@
     return call(
         prepare_kernel,
         "prepare",
-        (*[jax.ShapeDtypeStruct((TABLE,), jnp.int32)] * 2, LAID_OUT, LAID_OUT),
+        (*[jax.ShapeDtypeStruct((TABLE,), jnp.int32)] * 3, LAID_OUT, LAID_OUT),
         [SMEM, SMEM, VMEM, VMEM],
-        (SMEM, SMEM, VMEM, VMEM),
+        (SMEM, SMEM, SMEM, VMEM, VMEM),
     )(order, place, episodes, own)
 
 
@@ -339,16 +336,28 @@
     )(table, kv_all, q, g, stats_all)
 
 
-def query_gradients(place, table, kv_own, kv_far, q, g, rows):
+OWN_ROWS = (SLOTS // 2, ROWS, HEAD)
+
+
+def near_query_gradients(place, table, kv, q, g, rows):
     return call(
-        query_kernel,
-        "query_gradients",
+        near_kernel,
+        "near_query_gradients",
+        [jax.ShapeDtypeStruct(OWN_ROWS, jnp.float32)] * 3,
+        [SMEM, SMEM, VMEM, VMEM, VMEM, VMEM],
+        [VMEM] * 3,
+    )(place, table, kv, q, g, rows)
+
+
+def far_query_gradients(place, table, kv, q, g, near):
+    return call(
+        far_kernel,
+        "far_query_gradients",
         jax.ShapeDtypeStruct((2, 2 * SPAN, HEADS * HEAD), jnp.bfloat16),
-        [SMEM, SMEM, VMEM, VMEM, VMEM, VMEM, VMEM],
+        [SMEM, SMEM, VMEM, VMEM, VMEM, VMEM, VMEM, VMEM],
         VMEM,
-        [pltpu.VMEM((SLOTS // 2, ROWS, HEAD), jnp.float32)] * 3
-        + [pltpu.VMEM((4 * KEYS, SPAN, HEAD), jnp.bfloat16)],
-    )(place, table, kv_own, kv_far, q, g, rows)
+        [pltpu.VMEM(OWN_ROWS, jnp.float32)],
+    )(place, table, kv, q, g, *near)
 
 
 def per_device(query_rows, key_rows, stored_value_rows, output_grad, span_order, episode_ids):
@@ -364,14 +373,15 @@
     remote = swap(both, "xl")
     own = lax.all_gather(both, "core", axis=0, tiled=True)
     other = lax.all_gather(remote, "core", axis=0, tiled=True)
-    table, query_table, q, g = prepare(span_order, place, episode_ids, own)
+    table, near_table, far_table, q, g = prepare(span_order, place, episode_ids, own)
     q, g, stats = row_stats(place, table, kv_all, other, q, g)
     stats_all = lax.all_gather(stats, ("xl", "core"), axis=0)
     dkv, rows = key_value_gradients(table, kv_all, q, g, stats_all)
     dkv_parts = lax.all_to_all(dkv.reshape(ring, 2 * tokens, HEAD), "y", 0, 0, tiled=True)
     kv_late, unused = lax.optimization_barrier((kv_all, dkv))
     kv_far = swap(kv_late, "core")
-    parts = query_gradients(place, query_table, kv_all, kv_far, q, g, rows)
+    near = near_query_gradients(place, near_table, kv_late, q, g, rows)
+    parts = far_query_gradients(place, far_table, kv_far, q, g, near)
     across = lax.ppermute(parts[1], ("section", "xl"), [(0, 3), (1, 2), (2, 1), (3, 0)])
     straight = swap(parts[0], "section")
     dkv_sum = jnp.sum(dkv_parts.astype(jnp.float32), axis=0).astype(jnp.bfloat16)

time: 72.2 us -> 71.3 us (0.988)
  Pallas kernels: 12.8 us -> 16.7 us
  starting transfers between devices: 25.1 us -> 22.2 us
  waiting for transfers between devices: 12.4 us -> 10.7 us
    pallas_call x1 -> x2, Pallas kernels: 2.88 us -> 5.42 us  [the longest x1 2.96 us: near_query_gradients(): call(near_kernel, 'near_query_gradients', [jax.ShapeDtypeStruct(OWN_ROWS,...]
    all_to_all x1, starting transfers between devices: 5.63 us -> 3.49 us  [per_device(): lax.all_to_all(dkv.reshape(ring, 2 * tokens, HEAD), 'y', 0, 0, tiled=True)]
    ppermute x3, waiting for transfers between devices: 6.08 us -> 4.15 us  [swap(): return lax.ppermute(block, axis, [(0, 1), (1, 0)])]
    ppermute x1, starting transfers between devices: 4.01 us -> 2.94 us  [per_device(): lax.ppermute(parts[1], ('section', 'xl'), [(0, 3), (1, 2), (2, 1), (3, 0)])]
    pallas_call x1, Pallas kernels: 4.56 us -> 5.45 us  [key_value_gradients(): call(key_value_kernel, 'key_value_gradients', (jax.ShapeDtypeStruct(KEYS_...]
  transfers between devices with their start and end apart: 6 -> 6, of which waited for: 4 -> 3; matrix products, arithmetic and copies ran while one was open for 1% -> 1% of each run, Pallas kernels for 8% -> 12%
where the time goes in v7:
time: 71.3 us; the launch traced here: 70.4 us
  starting transfers between devices  22.2 us (31%)
  blocking collectives  16.8 us (24%)
  Pallas kernels  16.7 us (23%)
  waiting for transfers between devices  10.7 us (15%)
  other arithmetic  2.58 us (4%)
  between operations  0.77 us (1%)
    ppermute x3, starting transfers between devices, swap(): return lax.ppermute(block, axis, [(0, 1), (1, 0)])  8.5 us
    all_to_all x1, starting transfers between devices, per_device(): kv_all = lax.all_to_all(kv, 'y', 0, 0, tiled=True).reshape(KEYS_VALUES)  7.23 us
    all_gather x1, blocking collectives, per_device(): both_dkv = lax.all_gather(dkv_sum, 'section', axis=0)  6.45 us
    all_gather x1, blocking collectives, per_device(): stats_all = lax.all_gather(stats, ('xl', 'core'), axis=0)  5.47 us
    pallas_call x1, Pallas kernels, key_value_gradients(): call(key_value_kernel, 'key_value_gradients', (jax.ShapeDtypeStruct(KEYS_...  5.45 us
    ppermute x3, waiting for transfers between devices, swap(): return lax.ppermute(block, axis, [(0, 1), (1, 0)])  4.15 us
    all_to_all x1, waiting for transfers between devices, per_device(): lax.all_to_all(dkv.reshape(ring, 2 * tokens, HEAD), 'y', 0, 0, tiled=True)  3.91 us
    all_to_all x1, starting transfers between devices, per_device(): lax.all_to_all(dkv.reshape(ring, 2 * tokens, HEAD), 'y', 0, 0, tiled=True)  3.49 us
  transfers between devices with their start and end apart: 6, of which 3 were waited for; matrix products, arithmetic and copies ran while one was open for 1% of the time, Pallas kernels for 12%

profile of v7, /device:TPU:6, one launch (start us, length us, event | category | flops | bytes accessed | tf_op | source)
XLA Modules:
  0.0 70.4 jit_solution(14406305085232714297)
XLA Ops:
  0.6 1.7 %broadcast_select_fusion = bf16[8,2,128,128]{3,2,1,0:T(8,128)(2,1)} fusion(pred[2]{0:T(512)(128)(4,1)S(1)} %iota_compare_fusion, bf16[128,128]{1,0:T(8,128)(2,1)} %bitcast.25, bf16[128,128]{1,0:T(8,128)(2,1)} %bitcast.26), kind=kLoop, calls=%fused_computation | loop fusion | flops 262144 | bytes 589826 | tf_op jit(solution)/shard_map/jit(_where)/select_n | solution.py:370
  2.3 0.0 copy-start.2
  2.3 0.0 copy-start.3
  2.3 7.2 %all-to-all-start = ((bf16[8,2,128,128]{3,2,1,0:T(8,128)(2,1)}), bf16[8,2,128,128]{3,2,1,0:T(8,128)(2,1)S(1)}, u32[]{:S(2)}, u32[]{:S(2)}) async-start(bf16[8,2,128,128]{3,2,1,0:T(8,128)(2,1)} %broadcast_select_fusion), calls=%async_computation | async-start | bytes 1048576 | tf_op jit(solution)/shard_map/all_to_all | solution.py:371
  9.6 0.0 copy-done.2
  9.6 0.0 copy-done.3
  9.6 2.7 %collective-permute-start = (bf16[128,1536]{1,0:T(8,128)(2,1)S(1)}, bf16[128,1536]{1,0:T(8,128)(2,1)S(1)}, u32[]{:S(2)}, u32[]{:S(2)}) collective-permute-start(bf16[128,1536]{1,0:T(8,128)(2,1)S(1)} %pad_maximum_fusion), channel_id=1, source_target_pairs={{0,2},{2,0},{1,3},{3,1},{4,6},{6,4},{5,7},{7,5},{8,10},{10,8},{9,1... | collective-permute-start | bytes 1179656 | tf_op jit(solution)/shard_map/ppermute | solution.py:279
  12.4 0.1 pad_add_fusion.place_ref
  12.4 0.0 copy-start
  12.4 0.0 copy-start.1
  12.4 2.5 %all_gather.18.own_ref = bf16[256,1536]{1,0:T(8,128)(2,1)S(1)} all-gather(bf16[128,1536]{1,0:T(8,128)(2,1)S(1)} %pad_maximum_fusion), channel_id=1, replica_groups=mesh['section'=2,'tp'=8,'y'=8,'xl'=2,'core'=2] {'core'}, dimensions={0}, use_global_device_ids=true | all-gather | bytes 1179648 | tf_op jit(solution)/shard_map/all_gather | solution.py:374
  14.9 0.0 copy-done
  14.9 0.0 copy-done.1
  14.9 3.0 %prepare.1 = (s32[456]{0:T(512)S(1)}, s32[456]{0:T(512)S(1)}, s32[456]{0:T(512)S(1)}, bf16[8,384,128]{2,1,0:T(8,128)(2,1)S(1)}, bf16[8,384,128]{2,1,0:T(8,128)(2,1)S(1)}) custom-call(s32[64]{0:T(128)S(1)} %copy-done.1, s32[3]{0:T(128)S(1)} %pad_add_fusion.place_ref, s32[1,4096]{1,0:T(1,128)S(1)} %copy-done, bf16[256,1536]{1,0:T(8,128)(2,1)S(1)} %all_gather.18.own_ref), custom_call_target="tpu_custom_call" | custom-call | tf_op jit(solution)/shard_map/prepare/pallas_call | solution.py:304
  17.9 4.1 %collective-permute-done = bf16[128,1536]{1,0:T(8,128)(2,1)S(1)} collective-permute-done((bf16[128,1536]{1,0:T(8,128)(2,1)S(1)}, bf16[128,1536]{1,0:T(8,128)(2,1)S(1)}, u32[]{:S(2)}, u32[]{:S(2)}) %collective-permute-start) | collective-permute-done | bytes 393248 | tf_op jit(solution)/shard_map/ppermute | solution.py:279
  22.1 2.4 %all_gather.19.other_ref = bf16[256,1536]{1,0:T(8,128)(2,1)S(1)} all-gather(bf16[128,1536]{1,0:T(8,128)(2,1)S(1)} %collective-permute-done), channel_id=1, replica_groups=mesh['section'=2,'tp'=8,'y'=8,'xl'=2,'core'=2] {'core'}, dimensions={0}, use_global_device_ids=true | all-gather | bytes 1179648 | tf_op jit(solution)/shard_map/all_gather | solution.py:375
  24.4 2.6 %all-to-all-done = bf16[8,2,128,128]{3,2,1,0:T(8,128)(2,1)S(1)} async-done(((bf16[8,2,128,128]{3,2,1,0:T(8,128)(2,1)}), bf16[8,2,128,128]{3,2,1,0:T(8,128)(2,1)S(1)}, u32[]{:S(2)}, u32[]{:S(2)}) %all-to-all-start) | async-done | bytes 524320 | tf_op jit(solution)/shard_map/all_to_all | solution.py:371
  27.0 2.9 %row_stats.1 = (bf16[8,384,128]{2,1,0:T(8,128)(2,1)S(1)}, bf16[8,384,128]{2,1,0:T(8,128)(2,1)S(1)}, f32[24,384]{1,0:T(8,128)S(1)}) custom-call(s32[3]{0:T(128)S(1)} %pad_add_fusion.place_ref, s32[456]{0:T(512)S(1)} %get-tuple-element.22.table_ref, bf16[32,64,128]{2,1,0:T(8,128)(2,1)S(1)} %bitcast.17, ...), custom_call_target="tpu_custom_call", output_to_operand_aliasing={{0}: (4, {}), {1}: (5, {})} | custom-call | tf_op jit(solution)/shard_map/row_stats/pallas_call | solution.py:314
  29.9 5.5 %all-gather = f32[96,384]{1,0:T(8,128)S(1)} all-gather(f32[24,384]{1,0:T(8,128)S(1)} %get-tuple-element.27), channel_id=2, replica_groups=mesh['section'=2,'tp'=8,'y'=8,'xl'=2,'core'=2] {'xl','core'}, dimensions={0}, use_global_device_ids=true | all-gather | bytes 184320 | tf_op jit(solution)/shard_map/all_gather | solution.py:378
  35.4 5.4 %key_value_gradients.1 = (bf16[32,64,128]{2,1,0:T(8,128)(2,1)}, f32[16,384]{1,0:T(8,128)S(1)}) custom-call(s32[456]{0:T(512)S(1)} %get-tuple-element.22.table_ref, bf16[32,64,128]{2,1,0:T(8,128)(2,1)S(1)} %bitcast.18, bf16[8,384,128]{2,1,0:T(8,128)(2,1)S(1)} %get-tuple-element.25.q_ref, bf16[8,384,128]{2,1,0:T(8,128)(2,1)S(1)} %get-tuple-element.26.g_ref, ...), custom_call_target="tpu_custom_call" | custom-call | tf_op jit(solution)/shard_map/key_value_gradients/pallas_call | solution.py:326
  40.9 3.5 %all-to-all-start.1 = ((bf16[8,256,128]{2,1,0:T(8,128)(2,1)}), bf16[8,256,128]{2,1,0:T(8,128)(2,1)S(1)}, u32[]{:S(2)}, u32[]{:S(2)}) async-start(bf16[8,256,128]{2,1,0:T(8,128)(2,1)} %bitcast.11), calls=%async_computation.1 | async-start | bytes 1048576 | tf_op jit(solution)/shard_map/all_to_all | solution.py:380
  44.4 2.1 %collective-permute-start.1 = (bf16[32,64,128]{2,1,0:T(8,128)(2,1)S(1)}, bf16[32,64,128]{2,1,0:T(8,128)(2,1)S(1)}, u32[]{:S(2)}, u32[]{:S(2)}) collective-permute-start(bf16[32,64,128]{2,1,0:T(8,128)(2,1)S(1)} %bitcast.19), channel_id=1, source_target_pairs={{0,1},{1,0},{2,3},{3,2},{4,5},{5,4},{6,7},{7,6},{8,9},{9,8},{10,11... | collective-permute-start | bytes 1572872 | tf_op jit(solution)/shard_map/ppermute | solution.py:279
  46.5 3.0 %near_query_gradients.1 = (f32[4,384,128]{2,1,0:T(8,128)S(1)}, f32[4,384,128]{2,1,0:T(8,128)S(1)}, f32[4,384,128]{2,1,0:T(8,128)S(1)}) custom-call(s32[3]{0:T(128)S(1)} %pad_add_fusion.place_ref, s32[456]{0:T(512)S(1)} %get-tuple-element.30.table_ref, bf16[32,64,128]{2,1,0:T(8,128)(2,1)S(1)} %bitcast.20, bf16[8,384,128]{2,1,0:T(8,128)(2,1)S(1)} %get-tuple-element.25.q_ref, ...), custom_call_target="tpu_custom_call" | custom-call | tf_op jit(solution)/shard_map/near_query_gradients/pallas_call | solution.py:343
  49.5 0.0 collective-permute-done.1.kv_ref
  49.5 2.5 %far_query_gradients.1 = bf16[2,128,768]{2,1,0:T(8,128)(2,1)S(1)} custom-call(s32[3]{0:T(128)S(1)} %pad_add_fusion.place_ref, s32[456]{0:T(512)S(1)} %get-tuple-element.21.table_ref, bf16[32,64,128]{2,1,0:T(8,128)(2,1)S(1)} %collective-permute-done.1.kv_ref, bf16[8,384,128]{2,1,0:T(8,128)(2,1)S(1)} %get-tuple-element.25.q_ref, ...), custom_call_target="tpu_custom_call" | custom-call | tf_op jit(solution)/shard_map/far_query_gradients/pallas_call | solution.py:353
  52.0 2.9 %collective-permute-start.3 = (bf16[128,768]{1,0:T(8,128)(2,1)S(1)}, bf16[128,768]{1,0:T(8,128)(2,1)S(1)}, u32[]{:S(2)}, u32[]{:S(2)}) collective-permute-start(bf16[128,768]{1,0:T(8,128)(2,1)S(1)} %get-tuple-element.39), channel_id=1, source_target_pairs={{0,258},{2,256},{256,2},{258,0},{1,259},{3,257},{257,3},{259,1},{4... | collective-permute-start | bytes 589832 | tf_op jit(solution)/shard_map/ppermute | solution.py:385
  54.9 3.6 %collective-permute-start.2 = (bf16[128,768]{1,0:T(8,128)(2,1)S(1)}, bf16[128,768]{1,0:T(8,128)(2,1)S(1)}, u32[]{:S(2)}, u32[]{:S(2)}) collective-permute-start(bf16[128,768]{1,0:T(8,128)(2,1)S(1)} %get-tuple-element.40), channel_id=1, source_target_pairs={{0,256},{256,0},{1,257},{257,1},{2,258},{258,2},{3,259},{259,3},{4... | collective-permute-start | bytes 589832 | tf_op jit(solution)/shard_map/ppermute | solution.py:279
  58.6 3.9 %all-to-all-done.1 = bf16[8,256,128]{2,1,0:T(8,128)(2,1)S(1)} async-done(((bf16[8,256,128]{2,1,0:T(8,128)(2,1)}), bf16[8,256,128]{2,1,0:T(8,128)(2,1)S(1)}, u32[]{:S(2)}, u32[]{:S(2)}) %all-to-all-start.1) | async-done | bytes 524320 | tf_op jit(solution)/shard_map/all_to_all | solution.py:380
  62.5 0.1 reduce_sum.12
  62.6 6.4 %all-gather.1 = bf16[512,128]{1,0:T(8,128)(2,1)S(1)} all-gather(bf16[256,128]{1,0:T(8,128)(2,1)S(1)} %reduce_sum.12), channel_id=3, replica_groups=mesh['section'=2,'tp'=8,'y'=8,'xl'=2,'core'=2] {'section'}, dimensions={0}, use_global_device_ids=true | all-gather | bytes 196608 | tf_op jit(solution)/shard_map/all_gather | solution.py:388
  69.0 0.6 constant_dynamic-slice_fusion.1
  69.6 0.0 collective-permute-done.3
  69.6 0.0 collective-permute-done.2
  69.6 0.7 %fusion = bf16[1,128,768]{2,1,0:T(8,128)(2,1)} fusion(bf16[128,768]{1,0:T(8,128)(2,1)S(1)} %collective-permute-done.3, bf16[128,768]{1,0:T(8,128)(2,1)S(1)} %collective-permute-done.2), kind=kLoop, calls=%fused_computation.3 | loop fusion | flops 393216 | bytes 589824 | tf_op jit(solution)/shard_map/broadcast_in_dim | solution.py:395
  (3 shorter events, 0.1 us)
Async XLA Ops:
  2.3 7.2 %copy-start.2 = (bf16[1,128,768]{2,1,0:T(8,128)(2,1)S(1)}, bf16[1,128,768]{2,1,0:T(8,128)(2,1)}, u32[]{:S(2)}) copy-start(bf16[1,128,768]{2,1,0:T(8,128)(2,1)} %param.9) | copy-start | bytes 589828
  2.3 7.2 %copy-start.3 = (bf16[1,128,768]{2,1,0:T(8,128)(2,1)S(1)}, bf16[1,128,768]{2,1,0:T(8,128)(2,1)}, u32[]{:S(2)}) copy-start(bf16[1,128,768]{2,1,0:T(8,128)(2,1)} %param.6) | copy-start | bytes 589828
  2.3 24.7 %all-to-all-start = ((bf16[8,2,128,128]{3,2,1,0:T(8,128)(2,1)}), bf16[8,2,128,128]{3,2,1,0:T(8,128)(2,1)S(1)}, u32[]{:S(2)}, u32[]{:S(2)}) async-start(bf16[8,2,128,128]{3,2,1,0:T(8,128)(2,1)} %broadcast_select_fusion), calls=%async_computation | async-start | bytes 1048576 | tf_op jit(solution)/shard_map/all_to_all | solution.py:371
  9.6 12.5 %collective-permute-start = (bf16[128,1536]{1,0:T(8,128)(2,1)S(1)}, bf16[128,1536]{1,0:T(8,128)(2,1)S(1)}, u32[]{:S(2)}, u32[]{:S(2)}) collective-permute-start(bf16[128,1536]{1,0:T(8,128)(2,1)S(1)} %pad_maximum_fusion), channel_id=1, source_target_pairs={{0,2},{2,0},{1,3},{3,1},{4,6},{6,4},{5,7},{7,5},{8,10},{10,8},{9,1... | collective-permute-start | bytes 1179656 | tf_op jit(solution)/shard_map/ppermute | solution.py:279
  12.4 2.5 %copy-start = (s32[1,4096]{1,0:T(1,128)S(1)}, s32[1,4096]{1,0:T(1,128)}, u32[]{:S(2)}) copy-start(s32[1,4096]{1,0:T(1,128)} %episode_ref.1) | copy-start | bytes 49156
  12.4 2.5 %copy-start.1 = (s32[64]{0:T(128)S(1)}, s32[64]{0:T(128)}, u32[]{:S(2)}) copy-start(s32[64]{0:T(128)} %order_ref.1) | copy-start | bytes 772
  40.9 21.6 %all-to-all-start.1 = ((bf16[8,256,128]{2,1,0:T(8,128)(2,1)}), bf16[8,256,128]{2,1,0:T(8,128)(2,1)S(1)}, u32[]{:S(2)}, u32[]{:S(2)}) async-start(bf16[8,256,128]{2,1,0:T(8,128)(2,1)} %bitcast.11), calls=%async_computation.1 | async-start | bytes 1048576 | tf_op jit(solution)/shard_map/all_to_all | solution.py:380
  44.4 5.1 %collective-permute-start.1 = (bf16[32,64,128]{2,1,0:T(8,128)(2,1)S(1)}, bf16[32,64,128]{2,1,0:T(8,128)(2,1)S(1)}, u32[]{:S(2)}, u32[]{:S(2)}) collective-permute-start(bf16[32,64,128]{2,1,0:T(8,128)(2,1)S(1)} %bitcast.19), channel_id=1, source_target_pairs={{0,1},{1,0},{2,3},{3,2},{4,5},{5,4},{6,7},{7,6},{8,9},{9,8},{10,11... | collective-permute-start | bytes 1572872 | tf_op jit(solution)/shard_map/ppermute | solution.py:279
  52.0 17.7 %collective-permute-start.3 = (bf16[128,768]{1,0:T(8,128)(2,1)S(1)}, bf16[128,768]{1,0:T(8,128)(2,1)S(1)}, u32[]{:S(2)}, u32[]{:S(2)}) collective-permute-start(bf16[128,768]{1,0:T(8,128)(2,1)S(1)} %get-tuple-element.39), channel_id=1, source_target_pairs={{0,258},{2,256},{256,2},{258,0},{1,259},{3,257},{257,3},{259,1},{4... | collective-permute-start | bytes 589832 | tf_op jit(solution)/shard_map/ppermute | solution.py:385
  54.9 14.7 %collective-permute-start.2 = (bf16[128,768]{1,0:T(8,128)(2,1)S(1)}, bf16[128,768]{1,0:T(8,128)(2,1)S(1)}, u32[]{:S(2)}, u32[]{:S(2)}) collective-permute-start(bf16[128,768]{1,0:T(8,128)(2,1)S(1)} %get-tuple-element.40), channel_id=1, source_target_pairs={{0,256},{256,0},{1,257},{257,1},{2,258},{258,2},{3,259},{259,3},{4... | collective-permute-start | bytes 589832 | tf_op jit(solution)/shard_map/ppermute | solution.py:279

commit v8 on v7

--- a/solution.py
+++ b/solution.py
@@ -15,6 +15,7 @@
 SLOTS = 8
 KEYS = 16
 GROUP = 4
+QUERY_UNROLLS = (4, 2, 1)
 UNROLLS = (8, 4, 2, 1)
 CHUNKS = KEYS // GROUP
 STEPS = SLOTS * CHUNKS + 2 * CHUNKS
@@ -135,9 +136,9 @@
     return slot, spans, keys, query, grad, scores, dot(values, grad, NT)
 
 
-def run_steps(table_ref, one_step):
+def run_steps(table_ref, one_step, unrolls=UNROLLS):
     at, count = jnp.int32(0), table_ref[0]
-    for steps in UNROLLS:
+    for steps in unrolls:
 
         def some(n, unused, at=at, steps=steps):
             for i in range(steps):
@@ -257,7 +258,7 @@
             parts.append((probs * (products[:, cols] - delta)).astype(jnp.bfloat16))
         acc_ref[own] += dot(jnp.concatenate(parts, axis=1), keys, NN)
 
-    run_steps(table_ref, one_step)
+    run_steps(table_ref, one_step, QUERY_UNROLLS)
 
 
 def far_kernel(

time: 71.3 us -> 70.9 us (level)
  starting transfers between devices: 22.2 us -> 24.1 us
  Pallas kernels: 16.7 us -> 15 us
    ppermute x3, starting transfers between devices: 8.5 us -> 11.4 us  [swap(): return lax.ppermute(block, axis, [(0, 1), (1, 0)])]
    ppermute x1, starting transfers between devices: 2.94 us -> 1.92 us  [per_device(): lax.ppermute(parts[1], ('section', 'xl'), [(0, 3), (1, 2), (2, 1), (3, 0)])]
    pallas_call x1, Pallas kernels: 5.45 us -> 4.56 us  [key_value_gradients(): call(key_value_kernel, 'key_value_gradients', (jax.ShapeDtypeStruct(KEYS_...]
  transfers between devices with their start and end apart: 6 -> 6, of which waited for: 3 -> 3; matrix products, arithmetic and copies ran while one was open for 1% -> 1% of each run, Pallas kernels for 12% -> 11%
where the time goes in v8:
time: 70.9 us; the launch traced here: 69.9 us
  starting transfers between devices  24.1 us (34%)
  blocking collectives  16.8 us (24%)
  Pallas kernels  15 us (21%)
  waiting for transfers between devices  9.99 us (14%)
  other arithmetic  2.58 us (4%)
  between operations  0.76 us (1%)
    ppermute x3, starting transfers between devices, swap(): return lax.ppermute(block, axis, [(0, 1), (1, 0)])  11.4 us
    all_to_all x1, starting transfers between devices, per_device(): kv_all = lax.all_to_all(kv, 'y', 0, 0, tiled=True).reshape(KEYS_VALUES)  7.23 us
    all_gather x1, blocking collectives, per_device(): both_dkv = lax.all_gather(dkv_sum, 'section', axis=0)  6.45 us
    all_gather x1, blocking collectives, per_device(): stats_all = lax.all_gather(stats, ('xl', 'core'), axis=0)  5.47 us
    pallas_call x1, Pallas kernels, key_value_gradients(): call(key_value_kernel, 'key_value_gradients', (jax.ShapeDtypeStruct(KEYS_...  4.56 us
    ppermute x3, waiting for transfers between devices, swap(): return lax.ppermute(block, axis, [(0, 1), (1, 0)])  4.15 us
    all_to_all x1, starting transfers between devices, per_device(): lax.all_to_all(dkv.reshape(ring, 2 * tokens, HEAD), 'y', 0, 0, tiled=True)  3.54 us
    all_to_all x1, waiting for transfers between devices, per_device(): lax.all_to_all(dkv.reshape(ring, 2 * tokens, HEAD), 'y', 0, 0, tiled=True)  3.22 us
  transfers between devices with their start and end apart: 6, of which 3 were waited for; matrix products, arithmetic and copies ran while one was open for 1% of the time, Pallas kernels for 11%

profile of v8, /device:TPU:6, one launch (start us, length us, event | category | flops | bytes accessed | tf_op | source)
XLA Modules:
  0.0 69.9 jit_solution(9677975851410588647)
XLA Ops:
  0.6 1.7 %broadcast_select_fusion = bf16[8,2,128,128]{3,2,1,0:T(8,128)(2,1)} fusion(pred[2]{0:T(512)(128)(4,1)S(1)} %iota_compare_fusion, bf16[128,128]{1,0:T(8,128)(2,1)} %bitcast.25, bf16[128,128]{1,0:T(8,128)(2,1)} %bitcast.26), kind=kLoop, calls=%fused_computation | loop fusion | flops 262144 | bytes 589826 | tf_op jit(solution)/shard_map/jit(_where)/select_n | solution.py:371
  2.3 0.0 copy-start.2
  2.3 0.0 copy-start.3
  2.3 7.2 %all-to-all-start = ((bf16[8,2,128,128]{3,2,1,0:T(8,128)(2,1)}), bf16[8,2,128,128]{3,2,1,0:T(8,128)(2,1)S(1)}, u32[]{:S(2)}, u32[]{:S(2)}) async-start(bf16[8,2,128,128]{3,2,1,0:T(8,128)(2,1)} %broadcast_select_fusion), calls=%async_computation | async-start | bytes 1048576 | tf_op jit(solution)/shard_map/all_to_all | solution.py:372
  9.6 0.0 copy-done.2
  9.6 0.0 copy-done.3
  9.6 2.7 %collective-permute-start = (bf16[128,1536]{1,0:T(8,128)(2,1)S(1)}, bf16[128,1536]{1,0:T(8,128)(2,1)S(1)}, u32[]{:S(2)}, u32[]{:S(2)}) collective-permute-start(bf16[128,1536]{1,0:T(8,128)(2,1)S(1)} %pad_maximum_fusion), channel_id=1, source_target_pairs={{0,2},{2,0},{1,3},{3,1},{4,6},{6,4},{5,7},{7,5},{8,10},{10,8},{9,1... | collective-permute-start | bytes 1179656 | tf_op jit(solution)/shard_map/ppermute | solution.py:280
  12.4 0.1 pad_add_fusion.place_ref
  12.4 0.0 copy-start
  12.4 0.0 copy-start.1
  12.4 2.5 %all_gather.18.own_ref = bf16[256,1536]{1,0:T(8,128)(2,1)S(1)} all-gather(bf16[128,1536]{1,0:T(8,128)(2,1)S(1)} %pad_maximum_fusion), channel_id=1, replica_groups=mesh['section'=2,'tp'=8,'y'=8,'xl'=2,'core'=2] {'core'}, dimensions={0}, use_global_device_ids=true | all-gather | bytes 1179648 | tf_op jit(solution)/shard_map/all_gather | solution.py:375
  14.9 0.0 copy-done
  14.9 0.0 copy-done.1
  14.9 3.0 %prepare.1 = (s32[456]{0:T(512)S(1)}, s32[456]{0:T(512)S(1)}, s32[456]{0:T(512)S(1)}, bf16[8,384,128]{2,1,0:T(8,128)(2,1)S(1)}, bf16[8,384,128]{2,1,0:T(8,128)(2,1)S(1)}) custom-call(s32[64]{0:T(128)S(1)} %copy-done.1, s32[3]{0:T(128)S(1)} %pad_add_fusion.place_ref, s32[1,4096]{1,0:T(1,128)S(1)} %copy-done, bf16[256,1536]{1,0:T(8,128)(2,1)S(1)} %all_gather.18.own_ref), custom_call_target="tpu_custom_call" | custom-call | tf_op jit(solution)/shard_map/prepare/pallas_call | solution.py:305
  17.9 4.1 %collective-permute-done = bf16[128,1536]{1,0:T(8,128)(2,1)S(1)} collective-permute-done((bf16[128,1536]{1,0:T(8,128)(2,1)S(1)}, bf16[128,1536]{1,0:T(8,128)(2,1)S(1)}, u32[]{:S(2)}, u32[]{:S(2)}) %collective-permute-start) | collective-permute-done | bytes 393248 | tf_op jit(solution)/shard_map/ppermute | solution.py:280
  22.1 2.4 %all_gather.19.other_ref = bf16[256,1536]{1,0:T(8,128)(2,1)S(1)} all-gather(bf16[128,1536]{1,0:T(8,128)(2,1)S(1)} %collective-permute-done), channel_id=1, replica_groups=mesh['section'=2,'tp'=8,'y'=8,'xl'=2,'core'=2] {'core'}, dimensions={0}, use_global_device_ids=true | all-gather | bytes 1179648 | tf_op jit(solution)/shard_map/all_gather | solution.py:376
  24.4 2.6 %all-to-all-done = bf16[8,2,128,128]{3,2,1,0:T(8,128)(2,1)S(1)} async-done(((bf16[8,2,128,128]{3,2,1,0:T(8,128)(2,1)}), bf16[8,2,128,128]{3,2,1,0:T(8,128)(2,1)S(1)}, u32[]{:S(2)}, u32[]{:S(2)}) %all-to-all-start) | async-done | bytes 524320 | tf_op jit(solution)/shard_map/all_to_all | solution.py:372
  27.0 2.5 %row_stats.1 = (bf16[8,384,128]{2,1,0:T(8,128)(2,1)S(1)}, bf16[8,384,128]{2,1,0:T(8,128)(2,1)S(1)}, f32[24,384]{1,0:T(8,128)S(1)}) custom-call(s32[3]{0:T(128)S(1)} %pad_add_fusion.place_ref, s32[456]{0:T(512)S(1)} %get-tuple-element.22.table_ref, bf16[32,64,128]{2,1,0:T(8,128)(2,1)S(1)} %bitcast.17, ...), custom_call_target="tpu_custom_call", output_to_operand_aliasing={{0}: (4, {}), {1}: (5, {})} | custom-call | tf_op jit(solution)/shard_map/row_stats/pallas_call | solution.py:315
  29.5 5.5 %all-gather = f32[96,384]{1,0:T(8,128)S(1)} all-gather(f32[24,384]{1,0:T(8,128)S(1)} %get-tuple-element.27), channel_id=2, replica_groups=mesh['section'=2,'tp'=8,'y'=8,'xl'=2,'core'=2] {'xl','core'}, dimensions={0}, use_global_device_ids=true | all-gather | bytes 184320 | tf_op jit(solution)/shard_map/all_gather | solution.py:379
  35.0 4.6 %key_value_gradients.1 = (bf16[32,64,128]{2,1,0:T(8,128)(2,1)}, f32[16,384]{1,0:T(8,128)S(1)}) custom-call(s32[456]{0:T(512)S(1)} %get-tuple-element.22.table_ref, bf16[32,64,128]{2,1,0:T(8,128)(2,1)S(1)} %bitcast.18, bf16[8,384,128]{2,1,0:T(8,128)(2,1)S(1)} %get-tuple-element.25.q_ref, bf16[8,384,128]{2,1,0:T(8,128)(2,1)S(1)} %get-tuple-element.26.g_ref, ...), custom_call_target="tpu_custom_call" | custom-call | tf_op jit(solution)/shard_map/key_value_gradients/pallas_call | solution.py:327
  39.5 3.5 %all-to-all-start.1 = ((bf16[8,256,128]{2,1,0:T(8,128)(2,1)}), bf16[8,256,128]{2,1,0:T(8,128)(2,1)S(1)}, u32[]{:S(2)}, u32[]{:S(2)}) async-start(bf16[8,256,128]{2,1,0:T(8,128)(2,1)} %bitcast.11), calls=%async_computation.1 | async-start | bytes 1048576 | tf_op jit(solution)/shard_map/all_to_all | solution.py:381
  43.1 3.0 %collective-permute-start.1 = (bf16[32,64,128]{2,1,0:T(8,128)(2,1)S(1)}, bf16[32,64,128]{2,1,0:T(8,128)(2,1)S(1)}, u32[]{:S(2)}, u32[]{:S(2)}) collective-permute-start(bf16[32,64,128]{2,1,0:T(8,128)(2,1)S(1)} %bitcast.19), channel_id=1, source_target_pairs={{0,1},{1,0},{2,3},{3,2},{4,5},{5,4},{6,7},{7,6},{8,9},{9,8},{10,11... | collective-permute-start | bytes 1572872 | tf_op jit(solution)/shard_map/ppermute | solution.py:280
  46.1 2.6 %near_query_gradients.1 = (f32[4,384,128]{2,1,0:T(8,128)S(1)}, f32[4,384,128]{2,1,0:T(8,128)S(1)}, f32[4,384,128]{2,1,0:T(8,128)S(1)}) custom-call(s32[3]{0:T(128)S(1)} %pad_add_fusion.place_ref, s32[456]{0:T(512)S(1)} %get-tuple-element.30.table_ref, bf16[32,64,128]{2,1,0:T(8,128)(2,1)S(1)} %bitcast.20, bf16[8,384,128]{2,1,0:T(8,128)(2,1)S(1)} %get-tuple-element.25.q_ref, ...), custom_call_target="tpu_custom_call" | custom-call | tf_op jit(solution)/shard_map/near_query_gradients/pallas_call | solution.py:344
  48.7 0.0 collective-permute-done.1.kv_ref
  48.7 2.4 %far_query_gradients.1 = bf16[2,128,768]{2,1,0:T(8,128)(2,1)S(1)} custom-call(s32[3]{0:T(128)S(1)} %pad_add_fusion.place_ref, s32[456]{0:T(512)S(1)} %get-tuple-element.21.table_ref, bf16[32,64,128]{2,1,0:T(8,128)(2,1)S(1)} %collective-permute-done.1.kv_ref, bf16[8,384,128]{2,1,0:T(8,128)(2,1)S(1)} %get-tuple-element.25.q_ref, ...), custom_call_target="tpu_custom_call" | custom-call | tf_op jit(solution)/shard_map/far_query_gradients/pallas_call | solution.py:354
  51.2 1.9 %collective-permute-start.3 = (bf16[128,768]{1,0:T(8,128)(2,1)S(1)}, bf16[128,768]{1,0:T(8,128)(2,1)S(1)}, u32[]{:S(2)}, u32[]{:S(2)}) collective-permute-start(bf16[128,768]{1,0:T(8,128)(2,1)S(1)} %get-tuple-element.39), channel_id=1, source_target_pairs={{0,258},{2,256},{256,2},{258,0},{1,259},{3,257},{257,3},{259,1},{4... | collective-permute-start | bytes 589832 | tf_op jit(solution)/shard_map/ppermute | solution.py:386
  53.1 5.7 %collective-permute-start.2 = (bf16[128,768]{1,0:T(8,128)(2,1)S(1)}, bf16[128,768]{1,0:T(8,128)(2,1)S(1)}, u32[]{:S(2)}, u32[]{:S(2)}) collective-permute-start(bf16[128,768]{1,0:T(8,128)(2,1)S(1)} %get-tuple-element.40), channel_id=1, source_target_pairs={{0,256},{256,0},{1,257},{257,1},{2,258},{258,2},{3,259},{259,3},{4... | collective-permute-start | bytes 589832 | tf_op jit(solution)/shard_map/ppermute | solution.py:280
  58.8 3.2 %all-to-all-done.1 = bf16[8,256,128]{2,1,0:T(8,128)(2,1)S(1)} async-done(((bf16[8,256,128]{2,1,0:T(8,128)(2,1)}), bf16[8,256,128]{2,1,0:T(8,128)(2,1)S(1)}, u32[]{:S(2)}, u32[]{:S(2)}) %all-to-all-start.1) | async-done | bytes 524320 | tf_op jit(solution)/shard_map/all_to_all | solution.py:381
  62.0 0.1 reduce_sum.12
  62.1 6.4 %all-gather.1 = bf16[512,128]{1,0:T(8,128)(2,1)S(1)} all-gather(bf16[256,128]{1,0:T(8,128)(2,1)S(1)} %reduce_sum.12), channel_id=3, replica_groups=mesh['section'=2,'tp'=8,'y'=8,'xl'=2,'core'=2] {'section'}, dimensions={0}, use_global_device_ids=true | all-gather | bytes 196608 | tf_op jit(solution)/shard_map/all_gather | solution.py:389
  68.6 0.6 constant_dynamic-slice_fusion.1
  69.2 0.0 collective-permute-done.3
  69.2 0.0 collective-permute-done.2
  69.2 0.7 %fusion = bf16[1,128,768]{2,1,0:T(8,128)(2,1)} fusion(bf16[128,768]{1,0:T(8,128)(2,1)S(1)} %collective-permute-done.3, bf16[128,768]{1,0:T(8,128)(2,1)S(1)} %collective-permute-done.2), kind=kLoop, calls=%fused_computation.3 | loop fusion | flops 393216 | bytes 589824 | tf_op jit(solution)/shard_map/broadcast_in_dim | solution.py:396
  (3 shorter events, 0.1 us)
Async XLA Ops:
  2.3 7.2 %copy-start.2 = (bf16[1,128,768]{2,1,0:T(8,128)(2,1)S(1)}, bf16[1,128,768]{2,1,0:T(8,128)(2,1)}, u32[]{:S(2)}) copy-start(bf16[1,128,768]{2,1,0:T(8,128)(2,1)} %param.9) | copy-start | bytes 589828
  2.3 7.2 %copy-start.3 = (bf16[1,128,768]{2,1,0:T(8,128)(2,1)S(1)}, bf16[1,128,768]{2,1,0:T(8,128)(2,1)}, u32[]{:S(2)}) copy-start(bf16[1,128,768]{2,1,0:T(8,128)(2,1)} %param.6) | copy-start | bytes 589828
  2.3 24.7 %all-to-all-start = ((bf16[8,2,128,128]{3,2,1,0:T(8,128)(2,1)}), bf16[8,2,128,128]{3,2,1,0:T(8,128)(2,1)S(1)}, u32[]{:S(2)}, u32[]{:S(2)}) async-start(bf16[8,2,128,128]{3,2,1,0:T(8,128)(2,1)} %broadcast_select_fusion), calls=%async_computation | async-start | bytes 1048576 | tf_op jit(solution)/shard_map/all_to_all | solution.py:372
  9.6 12.5 %collective-permute-start = (bf16[128,1536]{1,0:T(8,128)(2,1)S(1)}, bf16[128,1536]{1,0:T(8,128)(2,1)S(1)}, u32[]{:S(2)}, u32[]{:S(2)}) collective-permute-start(bf16[128,1536]{1,0:T(8,128)(2,1)S(1)} %pad_maximum_fusion), channel_id=1, source_target_pairs={{0,2},{2,0},{1,3},{3,1},{4,6},{6,4},{5,7},{7,5},{8,10},{10,8},{9,1... | collective-permute-start | bytes 1179656 | tf_op jit(solution)/shard_map/ppermute | solution.py:280
  12.4 2.5 %copy-start = (s32[1,4096]{1,0:T(1,128)S(1)}, s32[1,4096]{1,0:T(1,128)}, u32[]{:S(2)}) copy-start(s32[1,4096]{1,0:T(1,128)} %episode_ref.1) | copy-start | bytes 49156
  12.4 2.5 %copy-start.1 = (s32[64]{0:T(128)S(1)}, s32[64]{0:T(128)}, u32[]{:S(2)}) copy-start(s32[64]{0:T(128)} %order_ref.1) | copy-start | bytes 772
  39.5 22.5 %all-to-all-start.1 = ((bf16[8,256,128]{2,1,0:T(8,128)(2,1)}), bf16[8,256,128]{2,1,0:T(8,128)(2,1)S(1)}, u32[]{:S(2)}, u32[]{:S(2)}) async-start(bf16[8,256,128]{2,1,0:T(8,128)(2,1)} %bitcast.11), calls=%async_computation.1 | async-start | bytes 1048576 | tf_op jit(solution)/shard_map/all_to_all | solution.py:381
  43.1 5.6 %collective-permute-start.1 = (bf16[32,64,128]{2,1,0:T(8,128)(2,1)S(1)}, bf16[32,64,128]{2,1,0:T(8,128)(2,1)S(1)}, u32[]{:S(2)}, u32[]{:S(2)}) collective-permute-start(bf16[32,64,128]{2,1,0:T(8,128)(2,1)S(1)} %bitcast.19), channel_id=1, source_target_pairs={{0,1},{1,0},{2,3},{3,2},{4,5},{5,4},{6,7},{7,6},{8,9},{9,8},{10,11... | collective-permute-start | bytes 1572872 | tf_op jit(solution)/shard_map/ppermute | solution.py:280
  51.2 18.0 %collective-permute-start.3 = (bf16[128,768]{1,0:T(8,128)(2,1)S(1)}, bf16[128,768]{1,0:T(8,128)(2,1)S(1)}, u32[]{:S(2)}, u32[]{:S(2)}) collective-permute-start(bf16[128,768]{1,0:T(8,128)(2,1)S(1)} %get-tuple-element.39), channel_id=1, source_target_pairs={{0,258},{2,256},{256,2},{258,0},{1,259},{3,257},{257,3},{259,1},{4... | collective-permute-start | bytes 589832 | tf_op jit(solution)/shard_map/ppermute | solution.py:386
  53.1 16.1 %collective-permute-start.2 = (bf16[128,768]{1,0:T(8,128)(2,1)S(1)}, bf16[128,768]{1,0:T(8,128)(2,1)S(1)}, u32[]{:S(2)}, u32[]{:S(2)}) collective-permute-start(bf16[128,768]{1,0:T(8,128)(2,1)S(1)} %get-tuple-element.40), channel_id=1, source_target_pairs={{0,256},{256,0},{1,257},{257,1},{2,258},{258,2},{3,259},{259,3},{4... | collective-permute-start | bytes 589832 | tf_op jit(solution)/shard_map/ppermute | solution.py:280

commit v9 on v8

--- a/solution.py
+++ b/solution.py
@@ -367,8 +367,8 @@
     place = jnp.stack([lax.axis_index("y"), lax.axis_index("xl"), lax.axis_index("core")]).astype(
         jnp.int32
     )
-    part = lax.broadcasted_iota(jnp.int32, (ring, 2, tokens, HEAD), 1)
-    kv = jnp.where(part == 0, key_rows[None], stored_value_rows[None])
+    kv = jnp.concatenate([key_rows, stored_value_rows], axis=1)
+    kv = jnp.broadcast_to(kv, (ring, 2 * tokens, HEAD))
     kv_all = lax.all_to_all(kv, "y", 0, 0, tiled=True).reshape(KEYS_VALUES)
     both = jnp.concatenate([query_rows[0], output_grad[0]], axis=1)
     remote = swap(both, "xl")

time: 70.9 us -> 71.3 us (level)
  Pallas kernels: 15 us -> 13.2 us
  starting transfers between devices: 24.1 us -> 25.7 us
  other arithmetic: 2.58 us -> 1.68 us
  local copies, waits for them, and re-layouts: 0.67 us -> 1.53 us
  waiting for transfers between devices: 9.99 us -> 10.8 us
    ppermute x1, starting transfers between devices: 1.92 us -> 3.74 us  [per_device(): lax.ppermute(parts[1], ('section', 'xl'), [(0, 3), (1, 2), (2, 1), (3, 0)])]
    select_n x1 -> x0, other arithmetic: 1.67 us -> none  [per_device(): kv = jnp.where(part == 0, key_rows[None], stored_value_rows[None])]
    ppermute x3, starting transfers between devices: 11.4 us -> 9.78 us  [swap(): return lax.ppermute(block, axis, [(0, 1), (1, 0)])]
    all_to_all x1, starting transfers between devices: 3.54 us -> 4.91 us  [per_device(): lax.all_to_all(dkv.reshape(ring, 2 * tokens, HEAD), 'y', 0, 0, tiled=True)]
    broadcast_in_dim x0 -> x1, local copies, waits for them, and re-layouts: none -> 0.86 us  [per_device(): kv = jnp.broadcast_to(kv, (ring, 2 * tokens, HEAD))]
    broadcast_in_dim x0 -> x1, other arithmetic: none -> 0.78 us  [per_device(): kv = jnp.broadcast_to(kv, (ring, 2 * tokens, HEAD))]
    all_to_all x1, waiting for transfers between devices: 3.22 us -> 3.99 us  [per_device(): lax.all_to_all(dkv.reshape(ring, 2 * tokens, HEAD), 'y', 0, 0, tiled=True)]
  transfers between devices with their start and end apart: 6 -> 6, of which waited for: 3 -> 3; matrix products, arithmetic and copies ran while one was open for 1% -> 1% of each run, Pallas kernels for 11% -> 10%
where the time goes in v9:
time: 71.3 us; the launch traced here: 70.5 us
  starting transfers between devices  25.7 us (36%)
  blocking collectives  17 us (24%)
  Pallas kernels  13.2 us (19%)
  waiting for transfers between devices  10.8 us (15%)
  other arithmetic  1.68 us (2%)
  local copies, waits for them, and re-layouts  1.53 us (2%)
  between operations  0.75 us (1%)
    ppermute x3, starting transfers between devices, swap(): return lax.ppermute(block, axis, [(0, 1), (1, 0)])  9.78 us
    all_to_all x1, starting transfers between devices, per_device(): kv_all = lax.all_to_all(kv, 'y', 0, 0, tiled=True).reshape(KEYS_VALUES)  7.23 us
    all_gather x1, blocking collectives, per_device(): both_dkv = lax.all_gather(dkv_sum, 'section', axis=0)  6.45 us
    all_gather x1, blocking collectives, per_device(): stats_all = lax.all_gather(stats, ('xl', 'core'), axis=0)  5.67 us
    all_to_all x1, starting transfers between devices, per_device(): lax.all_to_all(dkv.reshape(ring, 2 * tokens, HEAD), 'y', 0, 0, tiled=True)  4.91 us
    ppermute x3, waiting for transfers between devices, swap(): return lax.ppermute(block, axis, [(0, 1), (1, 0)])  4.15 us
    pallas_call x1, Pallas kernels, key_value_gradients(): call(key_value_kernel, 'key_value_gradients', (jax.ShapeDtypeStruct(KEYS_...  4.09 us
    all_to_all x1, waiting for transfers between devices, per_device(): lax.all_to_all(dkv.reshape(ring, 2 * tokens, HEAD), 'y', 0, 0, tiled=True)  3.99 us
  transfers between devices with their start and end apart: 6, of which 3 were waited for; matrix products, arithmetic and copies ran while one was open for 1% of the time, Pallas kernels for 10%

profile of v9, /device:TPU:6, one launch (start us, length us, event | category | flops | bytes accessed | tf_op | source)
XLA Modules:
  0.0 70.5 jit_solution(1507196489712387643)
XLA Ops:
  0.6 0.8 %maximum_bitcast_fusion = bf16[256,128]{1,0:T(8,128)(2,1)S(1)} fusion(bf16[1,128,128]{2,1,0:T(8,128)(2,1)} %param.8, bf16[1,128,128]{2,1,0:T(8,128)(2,1)} %param.7), kind=kLoop, calls=%fused_computation.5 | loop fusion | flops 131072 | bytes 131072 | tf_op jit(solution)/shard_map/broadcast_in_dim | solution.py:371
  1.4 0.9 %broadcast_in_dim.11 = bf16[8,256,128]{2,1,0:T(8,128)(2,1)} broadcast(bf16[256,128]{1,0:T(8,128)(2,1)S(1)} %maximum_bitcast_fusion), dimensions={1,2} | broadcast | bytes 589824 | tf_op jit(solution)/shard_map/broadcast_in_dim | solution.py:371
  2.3 0.0 copy-start.2
  2.3 0.0 copy-start.3
  2.3 7.2 %all-to-all-start = ((bf16[8,256,128]{2,1,0:T(8,128)(2,1)}), bf16[8,256,128]{2,1,0:T(8,128)(2,1)S(1)}, u32[]{:S(2)}, u32[]{:S(2)}) async-start(bf16[8,256,128]{2,1,0:T(8,128)(2,1)} %broadcast_in_dim.11), calls=%async_computation | async-start | bytes 1048576 | tf_op jit(solution)/shard_map/all_to_all | solution.py:372
  9.5 0.0 copy-done.2
  9.5 0.0 copy-done.3
  9.6 2.7 %collective-permute-start = (bf16[128,1536]{1,0:T(8,128)(2,1)S(1)}, bf16[128,1536]{1,0:T(8,128)(2,1)S(1)}, u32[]{:S(2)}, u32[]{:S(2)}) collective-permute-start(bf16[128,1536]{1,0:T(8,128)(2,1)S(1)} %pad_maximum_fusion), channel_id=1, source_target_pairs={{0,2},{2,0},{1,3},{3,1},{4,6},{6,4},{5,7},{7,5},{8,10},{10,8},{9,1... | collective-permute-start | bytes 1179656 | tf_op jit(solution)/shard_map/ppermute | solution.py:280
  12.3 0.1 pad_add_fusion.place_ref
  12.4 0.0 copy-start
  12.4 0.0 copy-start.1
  12.4 2.5 %all_gather.18.own_ref = bf16[256,1536]{1,0:T(8,128)(2,1)S(1)} all-gather(bf16[128,1536]{1,0:T(8,128)(2,1)S(1)} %pad_maximum_fusion), channel_id=1, replica_groups=mesh['section'=2,'tp'=8,'y'=8,'xl'=2,'core'=2] {'core'}, dimensions={0}, use_global_device_ids=true | all-gather | bytes 1179648 | tf_op jit(solution)/shard_map/all_gather | solution.py:375
  14.9 0.0 copy-done
  14.9 0.0 copy-done.1
  14.9 3.0 %prepare.1 = (s32[456]{0:T(512)S(1)}, s32[456]{0:T(512)S(1)}, s32[456]{0:T(512)S(1)}, bf16[8,384,128]{2,1,0:T(8,128)(2,1)S(1)}, bf16[8,384,128]{2,1,0:T(8,128)(2,1)S(1)}) custom-call(s32[64]{0:T(128)S(1)} %copy-done.1, s32[3]{0:T(128)S(1)} %pad_add_fusion.place_ref, s32[1,4096]{1,0:T(1,128)S(1)} %copy-done, bf16[256,1536]{1,0:T(8,128)(2,1)S(1)} %all_gather.18.own_ref), custom_call_target="tpu_custom_call" | custom-call | tf_op jit(solution)/shard_map/prepare/pallas_call | solution.py:305
  17.9 4.1 %collective-permute-done = bf16[128,1536]{1,0:T(8,128)(2,1)S(1)} collective-permute-done((bf16[128,1536]{1,0:T(8,128)(2,1)S(1)}, bf16[128,1536]{1,0:T(8,128)(2,1)S(1)}, u32[]{:S(2)}, u32[]{:S(2)}) %collective-permute-start) | collective-permute-done | bytes 393248 | tf_op jit(solution)/shard_map/ppermute | solution.py:280
  22.0 2.4 %all_gather.19.other_ref = bf16[256,1536]{1,0:T(8,128)(2,1)S(1)} all-gather(bf16[128,1536]{1,0:T(8,128)(2,1)S(1)} %collective-permute-done), channel_id=1, replica_groups=mesh['section'=2,'tp'=8,'y'=8,'xl'=2,'core'=2] {'core'}, dimensions={0}, use_global_device_ids=true | all-gather | bytes 1179648 | tf_op jit(solution)/shard_map/all_gather | solution.py:376
  24.4 2.6 %all-to-all-done = bf16[8,256,128]{2,1,0:T(8,128)(2,1)S(1)} async-done(((bf16[8,256,128]{2,1,0:T(8,128)(2,1)}), bf16[8,256,128]{2,1,0:T(8,128)(2,1)S(1)}, u32[]{:S(2)}, u32[]{:S(2)}) %all-to-all-start) | async-done | bytes 524320 | tf_op jit(solution)/shard_map/all_to_all | solution.py:372
  27.0 2.1 %row_stats.1 = (bf16[8,384,128]{2,1,0:T(8,128)(2,1)S(1)}, bf16[8,384,128]{2,1,0:T(8,128)(2,1)S(1)}, f32[24,384]{1,0:T(8,128)S(1)}) custom-call(s32[3]{0:T(128)S(1)} %pad_add_fusion.place_ref, s32[456]{0:T(512)S(1)} %get-tuple-element.22.table_ref, bf16[32,64,128]{2,1,0:T(8,128)(2,1)S(1)} %bitcast.17, ...), custom_call_target="tpu_custom_call", output_to_operand_aliasing={{0}: (4, {}), {1}: (5, {})} | custom-call | tf_op jit(solution)/shard_map/row_stats/pallas_call | solution.py:315
  29.1 5.7 %all-gather = f32[96,384]{1,0:T(8,128)S(1)} all-gather(f32[24,384]{1,0:T(8,128)S(1)} %get-tuple-element.27), channel_id=2, replica_groups=mesh['section'=2,'tp'=8,'y'=8,'xl'=2,'core'=2] {'xl','core'}, dimensions={0}, use_global_device_ids=true | all-gather | bytes 184320 | tf_op jit(solution)/shard_map/all_gather | solution.py:379
  34.8 4.1 %key_value_gradients.1 = (bf16[32,64,128]{2,1,0:T(8,128)(2,1)}, f32[16,384]{1,0:T(8,128)S(1)}) custom-call(s32[456]{0:T(512)S(1)} %get-tuple-element.22.table_ref, bf16[32,64,128]{2,1,0:T(8,128)(2,1)S(1)} %bitcast.18, bf16[8,384,128]{2,1,0:T(8,128)(2,1)S(1)} %get-tuple-element.25.q_ref, bf16[8,384,128]{2,1,0:T(8,128)(2,1)S(1)} %get-tuple-element.26.g_ref, ...), custom_call_target="tpu_custom_call" | custom-call | tf_op jit(solution)/shard_map/key_value_gradients/pallas_call | solution.py:327
  38.9 4.9 %all-to-all-start.1 = ((bf16[8,256,128]{2,1,0:T(8,128)(2,1)}), bf16[8,256,128]{2,1,0:T(8,128)(2,1)S(1)}, u32[]{:S(2)}, u32[]{:S(2)}) async-start(bf16[8,256,128]{2,1,0:T(8,128)(2,1)} %bitcast.10), calls=%async_computation.1 | async-start | bytes 1048576 | tf_op jit(solution)/shard_map/all_to_all | solution.py:381
  43.8 2.7 %collective-permute-start.1 = (bf16[32,64,128]{2,1,0:T(8,128)(2,1)S(1)}, bf16[32,64,128]{2,1,0:T(8,128)(2,1)S(1)}, u32[]{:S(2)}, u32[]{:S(2)}) collective-permute-start(bf16[32,64,128]{2,1,0:T(8,128)(2,1)S(1)} %bitcast.19), channel_id=1, source_target_pairs={{0,1},{1,0},{2,3},{3,2},{4,5},{5,4},{6,7},{7,6},{8,9},{9,8},{10,11... | collective-permute-start | bytes 1572872 | tf_op jit(solution)/shard_map/ppermute | solution.py:280
  46.5 2.1 %near_query_gradients.1 = (f32[4,384,128]{2,1,0:T(8,128)S(1)}, f32[4,384,128]{2,1,0:T(8,128)S(1)}, f32[4,384,128]{2,1,0:T(8,128)S(1)}) custom-call(s32[3]{0:T(128)S(1)} %pad_add_fusion.place_ref, s32[456]{0:T(512)S(1)} %get-tuple-element.30.table_ref, bf16[32,64,128]{2,1,0:T(8,128)(2,1)S(1)} %bitcast.20, bf16[8,384,128]{2,1,0:T(8,128)(2,1)S(1)} %get-tuple-element.25.q_ref, ...), custom_call_target="tpu_custom_call" | custom-call | tf_op jit(solution)/shard_map/near_query_gradients/pallas_call | solution.py:344
  48.7 0.0 collective-permute-done.1.kv_ref
  48.7 1.8 %far_query_gradients.1 = bf16[2,128,768]{2,1,0:T(8,128)(2,1)S(1)} custom-call(s32[3]{0:T(128)S(1)} %pad_add_fusion.place_ref, s32[456]{0:T(512)S(1)} %get-tuple-element.21.table_ref, bf16[32,64,128]{2,1,0:T(8,128)(2,1)S(1)} %collective-permute-done.1.kv_ref, bf16[8,384,128]{2,1,0:T(8,128)(2,1)S(1)} %get-tuple-element.25.q_ref, ...), custom_call_target="tpu_custom_call" | custom-call | tf_op jit(solution)/shard_map/far_query_gradients/pallas_call | solution.py:354
  50.6 3.7 %collective-permute-start.3 = (bf16[128,768]{1,0:T(8,128)(2,1)S(1)}, bf16[128,768]{1,0:T(8,128)(2,1)S(1)}, u32[]{:S(2)}, u32[]{:S(2)}) collective-permute-start(bf16[128,768]{1,0:T(8,128)(2,1)S(1)} %get-tuple-element.39), channel_id=1, source_target_pairs={{0,258},{2,256},{256,2},{258,0},{1,259},{3,257},{257,3},{259,1},{4... | collective-permute-start | bytes 589832 | tf_op jit(solution)/shard_map/ppermute | solution.py:386
  54.3 4.3 %collective-permute-start.2 = (bf16[128,768]{1,0:T(8,128)(2,1)S(1)}, bf16[128,768]{1,0:T(8,128)(2,1)S(1)}, u32[]{:S(2)}, u32[]{:S(2)}) collective-permute-start(bf16[128,768]{1,0:T(8,128)(2,1)S(1)} %get-tuple-element.40), channel_id=1, source_target_pairs={{0,256},{256,0},{1,257},{257,1},{2,258},{258,2},{3,259},{259,3},{4... | collective-permute-start | bytes 589832 | tf_op jit(solution)/shard_map/ppermute | solution.py:280
  58.6 4.0 %all-to-all-done.1 = bf16[8,256,128]{2,1,0:T(8,128)(2,1)S(1)} async-done(((bf16[8,256,128]{2,1,0:T(8,128)(2,1)}), bf16[8,256,128]{2,1,0:T(8,128)(2,1)S(1)}, u32[]{:S(2)}, u32[]{:S(2)}) %all-to-all-start.1) | async-done | bytes 524320 | tf_op jit(solution)/shard_map/all_to_all | solution.py:381
  62.6 0.1 reduce_sum.12
  62.7 6.4 %all-gather.1 = bf16[512,128]{1,0:T(8,128)(2,1)S(1)} all-gather(bf16[256,128]{1,0:T(8,128)(2,1)S(1)} %reduce_sum.12), channel_id=3, replica_groups=mesh['section'=2,'tp'=8,'y'=8,'xl'=2,'core'=2] {'section'}, dimensions={0}, use_global_device_ids=true | all-gather | bytes 196608 | tf_op jit(solution)/shard_map/all_gather | solution.py:389
  69.1 0.6 constant_dynamic-slice_fusion.1
  69.8 0.0 collective-permute-done.3
  69.8 0.0 collective-permute-done.2
  69.8 0.7 %fusion = bf16[1,128,768]{2,1,0:T(8,128)(2,1)} fusion(bf16[128,768]{1,0:T(8,128)(2,1)S(1)} %collective-permute-done.3, bf16[128,768]{1,0:T(8,128)(2,1)S(1)} %collective-permute-done.2), kind=kLoop, calls=%fused_computation.2 | loop fusion | flops 393216 | bytes 589824 | tf_op jit(solution)/shard_map/broadcast_in_dim | solution.py:396
  (2 shorter events, 0.1 us)
Async XLA Ops:
  2.3 7.2 %copy-start.2 = (bf16[1,128,768]{2,1,0:T(8,128)(2,1)S(1)}, bf16[1,128,768]{2,1,0:T(8,128)(2,1)}, u32[]{:S(2)}) copy-start(bf16[1,128,768]{2,1,0:T(8,128)(2,1)} %param.9) | copy-start | bytes 589828
  2.3 7.2 %copy-start.3 = (bf16[1,128,768]{2,1,0:T(8,128)(2,1)S(1)}, bf16[1,128,768]{2,1,0:T(8,128)(2,1)}, u32[]{:S(2)}) copy-start(bf16[1,128,768]{2,1,0:T(8,128)(2,1)} %param.6) | copy-start | bytes 589828
  2.3 24.7 %all-to-all-start = ((bf16[8,256,128]{2,1,0:T(8,128)(2,1)}), bf16[8,256,128]{2,1,0:T(8,128)(2,1)S(1)}, u32[]{:S(2)}, u32[]{:S(2)}) async-start(bf16[8,256,128]{2,1,0:T(8,128)(2,1)} %broadcast_in_dim.11), calls=%async_computation | async-start | bytes 1048576 | tf_op jit(solution)/shard_map/all_to_all | solution.py:372
  9.6 12.5 %collective-permute-start = (bf16[128,1536]{1,0:T(8,128)(2,1)S(1)}, bf16[128,1536]{1,0:T(8,128)(2,1)S(1)}, u32[]{:S(2)}, u32[]{:S(2)}) collective-permute-start(bf16[128,1536]{1,0:T(8,128)(2,1)S(1)} %pad_maximum_fusion), channel_id=1, source_target_pairs={{0,2},{2,0},{1,3},{3,1},{4,6},{6,4},{5,7},{7,5},{8,10},{10,8},{9,1... | collective-permute-start | bytes 1179656 | tf_op jit(solution)/shard_map/ppermute | solution.py:280
  12.4 2.5 %copy-start = (s32[1,4096]{1,0:T(1,128)S(1)}, s32[1,4096]{1,0:T(1,128)}, u32[]{:S(2)}) copy-start(s32[1,4096]{1,0:T(1,128)} %episode_ref.1) | copy-start | bytes 49156
  12.4 2.5 %copy-start.1 = (s32[64]{0:T(128)S(1)}, s32[64]{0:T(128)}, u32[]{:S(2)}) copy-start(s32[64]{0:T(128)} %order_ref.1) | copy-start | bytes 772
  38.9 23.7 %all-to-all-start.1 = ((bf16[8,256,128]{2,1,0:T(8,128)(2,1)}), bf16[8,256,128]{2,1,0:T(8,128)(2,1)S(1)}, u32[]{:S(2)}, u32[]{:S(2)}) async-start(bf16[8,256,128]{2,1,0:T(8,128)(2,1)} %bitcast.10), calls=%async_computation.1 | async-start | bytes 1048576 | tf_op jit(solution)/shard_map/all_to_all | solution.py:381
  43.8 4.9 %collective-permute-start.1 = (bf16[32,64,128]{2,1,0:T(8,128)(2,1)S(1)}, bf16[32,64,128]{2,1,0:T(8,128)(2,1)S(1)}, u32[]{:S(2)}, u32[]{:S(2)}) collective-permute-start(bf16[32,64,128]{2,1,0:T(8,128)(2,1)S(1)} %bitcast.19), channel_id=1, source_target_pairs={{0,1},{1,0},{2,3},{3,2},{4,5},{5,4},{6,7},{7,6},{8,9},{9,8},{10,11... | collective-permute-start | bytes 1572872 | tf_op jit(solution)/shard_map/ppermute | solution.py:280
  50.6 19.2 %collective-permute-start.3 = (bf16[128,768]{1,0:T(8,128)(2,1)S(1)}, bf16[128,768]{1,0:T(8,128)(2,1)S(1)}, u32[]{:S(2)}, u32[]{:S(2)}) collective-permute-start(bf16[128,768]{1,0:T(8,128)(2,1)S(1)} %get-tuple-element.39), channel_id=1, source_target_pairs={{0,258},{2,256},{256,2},{258,0},{1,259},{3,257},{257,3},{259,1},{4... | collective-permute-start | bytes 589832 | tf_op jit(solution)/shard_map/ppermute | solution.py:386
  54.3 15.5 %collective-permute-start.2 = (bf16[128,768]{1,0:T(8,128)(2,1)S(1)}, bf16[128,768]{1,0:T(8,128)(2,1)S(1)}, u32[]{:S(2)}, u32[]{:S(2)}) collective-permute-start(bf16[128,768]{1,0:T(8,128)(2,1)S(1)} %get-tuple-element.40), channel_id=1, source_target_pairs={{0,256},{256,0},{1,257},{257,1},{2,258},{258,2},{3,259},{259,3},{4... | collective-permute-start | bytes 589832 | tf_op jit(solution)/shard_map/ppermute | solution.py:280
